TPU v7x, 32 devices: a whole 2x2x4 slice. The times are simulated.
32 devices in a mesh: member: 8 (over y, x, core), tile: 4 (over z).
Axes of the slice: x: 2, y: 2, z: 4, core: 2. Of those that a mesh axis runs over, the one named last changes fastest.
Arguments:
- prior_state: float32 [16, 10, 64, 1024], P('member', None, 'tile'), may hold values from -8 to 8
- velocity: float32 [16, 4, 64, 1024], P('member', None, 'tile'), may hold values from -0.3 to 0.3
- band_bins: int32 [64, 1024], P('tile'), may hold values from 0 to 3
- settle_table: float32 [4, 4], replicated, may hold values from 0.05 to 0.5
- measure_latitude: int32 [16], replicated, may hold values from 2 to 62
- measure_longitude: int32 [16], replicated, may hold values from 64 to 960
- obs_layer: int32 [16], replicated, may hold values from 0 to 1
- obs_kind: int32 [16], replicated, may hold values from 0 to 4
- obs_value: float32 [16], replicated, may hold values from 0 to 2
- obs_error: float32 [16], replicated, may hold values from 0.2 to 1
- obs_perturb: float32 [16, 16], P('member'), may hold values from -5 to 5
Outputs:
- analysis: float32 [16, 10, 64, 1024], P('member', None, 'tile')
All inputs are finite; a program needn't handle non-finite values.
Results may differ from a plain program's by a relative error of at most 0.000061.
Values sent between devices are 32-bit elements; how exact they have to be, the bound alone decides.
No kernel may reach another device: no remote copies, remote signals or barrier semaphores. Data moves between devices by JAX's collectives and lax.ppermute only.
A program may use at most 192 MiB of HBM per device.

v0:
```python
import jax
import jax.numpy as jnp
from jax import lax
from jax.sharding import PartitionSpec as P

MESH_WIDTH = 1024
NLAYER = 2
NCLASS = 4
MEASURE_COUNT = 16
WINDOW_HEIGHT = 4
WINDOW_WIDTH = 128
SUBSTEPS = 2
EVOLVED_SLOTS = 10


DIFFUSION = 0.08
DEPOSIT = 0.5


def with_halo(shard, sides, width):
    for axis, dim in sides:
        size, length = (lax.axis_size(axis), shard.shape[dim])
        up = [(i, (i + 1) % size) for i in range(size - 1)]
        down = [(j, i) for i, j in up]
        last = lax.slice_in_dim(shard, length - width, length, axis=dim)
        first = lax.slice_in_dim(shard, 0, width, axis=dim)
        before = lax.ppermute(last, axis, up)
        after = lax.ppermute(first, axis, down)
        shard = jnp.concatenate([before, shard, after], axis=dim)
    return shard


def combined_all(value, axis, join):
    pieces = jax.tree.map(lambda part: lax.all_gather(part, axis), value)
    head = jax.tree.map(lambda part: part[0], pieces)
    tail = jax.tree.map(lambda part: part[1:], pieces)
    running, _ = lax.scan(lambda running, share: (join(running, share), None), head, tail)
    return running


def transport(suspended_concentration, zonal_cfl_ratio, meridional_cfl_ratio):
    centre = suspended_concentration[..., 1:-1, :]
    upper_row = suspended_concentration[..., :-2, :]
    lower_row = suspended_concentration[..., 2:, :]
    widths = [(0, 0)] * (centre.ndim - 1) + [(1, 1)]
    widened = jnp.pad(centre, widths)
    left_cells = widened[..., :-2]
    right_cells = widened[..., 2:]
    advected = (
        jnp.maximum(zonal_cfl_ratio, 0.0) * (centre - upper_row)
        + jnp.minimum(zonal_cfl_ratio, 0.0) * (lower_row - centre)
        + jnp.maximum(meridional_cfl_ratio, 0.0) * (centre - left_cells)
        + jnp.minimum(meridional_cfl_ratio, 0.0) * (right_cells - centre)
    )
    laplace = upper_row + lower_row + left_cells + right_cells - 4.0 * centre
    return centre - advected + DIFFUSION * laplace


def deposition_advance(suspended_concentration, fall_speed):
    top_layer = suspended_concentration[..., 0, 1:, :, :]
    bottom = suspended_concentration[..., 1, 1:, :, :]
    settled = fall_speed * top_layer
    new_top = jnp.concatenate(
        [suspended_concentration[..., 0, :1, :, :], top_layer - settled], axis=-3
    )
    new_bottom = jnp.concatenate(
        [
            suspended_concentration[..., 1, :1, :, :],
            bottom + settled - DEPOSIT * fall_speed * bottom,
        ],
        axis=-3,
    )
    return jnp.stack([new_top, new_bottom], axis=-4)


def class_rates(band_bins, settle_table):
    levels = jnp.arange(settle_table.shape[0], dtype=jnp.int32)
    onehot = (band_bins[None] == levels[:, None, None]).astype(jnp.float32)
    return jnp.sum(settle_table[:, :, None, None] * onehot[:, None], axis=0)


def taper_table(patch_rows, patch_cols):
    row_pos = (jnp.arange(patch_rows, dtype=jnp.float32) + 0.5 - patch_rows / 2) / (patch_rows / 2)
    col_pos = (jnp.arange(patch_cols, dtype=jnp.float32) + 0.5 - patch_cols / 2) / (patch_cols / 2)
    return (1.0 - row_pos * row_pos)[:, None] * (1.0 - col_pos * col_pos)[None, :]


def combine_moments(earlier, later):
    count_early, mean_early, patch_early, square_early, cross_early = earlier
    count_late, mean_late, patch_late, square_late, cross_late = later
    merged_count = count_early + count_late
    delta_obs = mean_late - mean_early
    delta_patch = patch_late - patch_early
    share = count_late / merged_count
    product = count_early * count_late / merged_count
    return (
        merged_count,
        mean_early + share * delta_obs,
        patch_early + share * delta_patch,
        square_early + square_late + product * delta_obs[:, None] * delta_obs[None, :],
        cross_early + cross_late + product * delta_patch * delta_obs[:, None, None, None],
    )


def body(
    prior_state,
    velocity,
    band_bins,
    settle_table,
    measure_latitude,
    measure_longitude,
    obs_layer,
    obs_kind,
    obs_value,
    obs_error,
    obs_perturb,
):
    window_replicas = prior_state.shape[0]
    patch_row_block = prior_state.shape[2]
    total_members = window_replicas * lax.axis_size("member")
    first_row = lax.axis_index("tile") * patch_row_block
    fall_speed = class_rates(band_bins, settle_table)
    suspended_concentration = prior_state.reshape(
        window_replicas, NLAYER, NCLASS + 1, patch_row_block, MESH_WIDTH
    )
    zonal_cfl_ratio = velocity[:, 0::2, None]
    meridional_cfl_ratio = velocity[:, 1::2, None]
    for substep in range(SUBSTEPS):
        extended = with_halo(suspended_concentration, (("tile", 3),), 1)
        suspended_concentration = transport(extended, zonal_cfl_ratio, meridional_cfl_ratio)
    prior_replicas = deposition_advance(suspended_concentration, fall_speed).reshape(
        window_replicas, EVOLVED_SLOTS, patch_row_block, MESH_WIDTH
    )
    quantity_ordinal = obs_layer * (NCLASS + 1) + obs_kind
    local_index = measure_latitude - first_row
    owned = (local_index >= 0) & (local_index < patch_row_block)
    linear_position = (
        quantity_ordinal * patch_row_block + jnp.clip(local_index, 0, patch_row_block - 1)
    ) * MESH_WIDTH + measure_longitude
    selected_values = jnp.take(prior_replicas.reshape(window_replicas, -1), linear_position, axis=1)
    selected_values = jnp.where(owned[None], selected_values, 0.0)
    measured_data = lax.psum(selected_values, "tile")
    haloed_vector = jnp.pad(
        prior_replicas, ((0, 0), (0, 0), (WINDOW_HEIGHT, WINDOW_HEIGHT), (0, 0))
    )
    starts_r = jnp.clip(
        measure_latitude - WINDOW_HEIGHT // 2 - first_row + WINDOW_HEIGHT,
        0,
        patch_row_block + WINDOW_HEIGHT,
    )
    starts_c = measure_longitude - WINDOW_WIDTH // 2
    window_offset = jnp.zeros((), jnp.int32)

    def cut_patch(window_first_latitude, window_first_longitude):
        return lax.dynamic_slice(
            haloed_vector,
            (window_offset, window_offset, window_first_latitude, window_first_longitude),
            (window_replicas, EVOLVED_SLOTS, WINDOW_HEIGHT, WINDOW_WIDTH),
        )

    patches = jax.vmap(cut_patch)(starts_r, starts_c)
    patch_rows = (
        measure_latitude[:, None]
        - WINDOW_HEIGHT // 2
        + jnp.arange(WINDOW_HEIGHT, dtype=jnp.int32)[None]
    )
    inside = (patch_rows >= first_row) & (patch_rows < first_row + patch_row_block)
    patches = jnp.where(inside[:, None, None, :, None], patches, 0.0)
    mean_obs = jnp.mean(measured_data, axis=0)
    anomaly = measured_data - mean_obs
    own_moments = (
        jnp.full((), window_replicas, jnp.float32),
        mean_obs,
        jnp.mean(patches, axis=1),
        jnp.dot(anomaly.T, anomaly, precision=lax.Precision.HIGHEST),
        jnp.sum(patches * anomaly.T[:, :, None, None, None], axis=1),
    )
    merged = combined_all(own_moments, "member", combine_moments)
    cov_obs = merged[3]
    cov_cross = merged[4]
    system = cov_obs / (total_members - 1) + jnp.diag(obs_error)
    factor = jnp.linalg.cholesky(system)
    innovation = obs_value[None] + jnp.sqrt(obs_error)[None] * obs_perturb - measured_data
    weights_obs = jax.scipy.linalg.cho_solve((factor, True), innovation.T)
    gain = taper_table(WINDOW_HEIGHT, WINDOW_WIDTH) * cov_cross / (total_members - 1)

    def write_window_increment(obs_index, analysed):
        increment = gain[obs_index][None] * weights_obs[obs_index][:, None, None, None]
        corner = (window_offset, window_offset, starts_r[obs_index], starts_c[obs_index])
        current = lax.dynamic_slice(analysed, corner, increment.shape)
        return lax.dynamic_update_slice(analysed, current + increment, corner)

    analysed = lax.fori_loop(0, MEASURE_COUNT, write_window_increment, haloed_vector)
    return analysed[:, :, WINDOW_HEIGHT : WINDOW_HEIGHT + patch_row_block]


def solution(mesh):
    placed = (
        P("member", None, "tile", None),
        P("member", None, "tile", None),
        P("tile", None),
        P(),
        P(),
        P(),
        P(),
        P(),
        P(),
        P(),
        P("member", None),
    )
    return jax.shard_map(
        body, mesh=mesh, in_specs=placed, out_specs=P("member", None, "tile", None), check_vma=False
    )
```

profile of v0, /device:TPU:25, one launch (start us, length us, event | category | flops | bytes accessed | tf_op | source)
XLA Modules:
  0.0 483.5 jit_solution(9082949519994294382)
XLA Ops:
  6.5 1.5 copy.92
  8.2 1.3 collective-permute-start
  9.5 4.0 collective-permute-start.1
  15.4 1.3 fusion.26
  16.9 1.3 collective-permute-start.2
  18.2 4.0 collective-permute-start.3
  22.2 1.4 collective-permute-done.3
  23.6 1.3 fusion.12
  25.5 37.9 %copy.103 = f32[2,2,5,16,1024]{0,4,3,2,1:T(8,128)} copy(f32[2,2,5,16,1024]{4,3,2,1,0:T(8,128)S(1)} %pad_maximum_fusion.4) | data formatting | bytes 2621440 | tf_op jit(solution)/shard_map/stack | solution.py:73
  63.4 1.3 gather_fusion
  64.8 7.5 %psum.7 = f32[2,16]{1,0:T(2,128)S(1)} all-reduce(f32[2,16]{1,0:T(2,128)S(1)} %select_bitcast_fusion), channel_id=1, replica_groups=mesh['member'=8,'tile'=4] {'tile'}, use_global_device_ids=true, to_apply=%region_1.2 | all-reduce | flops 32 | bytes 256 | tf_op jit(solution)/shard_map/psum | solution.py:142
  72.6 11.2 %copy.102 = f32[2,10,16,1024]{1,0,3,2:T(2,128)} copy(f32[2,10,16,1024]{3,2,1,0:T(8,128)S(1)} %bitcast.88) | data formatting | bytes 2621440 | tf_op jit(solution)/shard_map/reshape | solution.py:131
  83.8 14.5 %pad.13 = f32[2,10,24,1024]{1,0,3,2:T(2,128)} pad(f32[2,10,16,1024]{1,0,3,2:T(2,128)} %copy.102, f32[]{:T(128)} %constant.154.clone.1), padding=0_0x0_0x4_4x0_0 | pad | bytes 3276804 | tf_op jit(solution)/shard_map/jit(_pad)/pad | solution.py:143
  98.4 18.9 %gather_fusion.1 = f32[16,2,10,4,128]{2,1,4,3,0:T(2,128)} fusion(f32[2,10,24,1024]{1,0,3,2:T(2,128)} %pad.13, s32[16]{0:T(128)S(1)} %get-tuple-element.245), kind=kCustom, calls=%fused_computation.1 | custom fusion | bytes 1310976 | tf_op jit(solution)/shard_map/vmap()/gather | solution.py:155
  117.3 29.1 %multiply_reduce_fusion = (f32[16,10,4,128]{1,3,2,0:T(8,128)}, f32[16,10,4,128]{1,3,2,0:T(8,128)}) fusion(f32[16,2,10,4,128]{2,1,4,3,0:T(2,128)} %gather_fusion.1, pred[16,4]{1,0:T(8,128)(4,1)S(1)} %fusion.44, f32[16,2]{1,0:T(8,128)S(1)} %copy.107), kind=kLoop, calls=%fused_computation.17 | loop fusion | flops 491520 | bytes 1310912 | tf_op jit(solution)/shard_map/reduce_sum | solution.py:176
  146.4 2.9 copy.105
  150.2 3.5 copy.108
  154.6 17.4 %all-reduce.5 = (f32[8]{0:T(128)}, f32[128]{0:T(128)S(1)}) all-reduce(f32[8]{0:T(128)S(1)} %dynamic-update-slice.3, f32[128]{0:T(128)S(1)} %get-tuple-element.266), channel_id=1, replica_groups=mesh['member'=8,'tile'=4] {'member'}, use_global_device_ids=true, to_apply=%add.3 | all-reduce | flops 136 | bytes 1088
  172.2 9.7 %all-gather.2 = f32[128,16]{1,0:T(8,128)S(1)} all-gather(f32[16,16]{1,0:T(8,128)S(1)} %fusion.48), channel_id=4, replica_groups=mesh['member'=8,'tile'=4] {'member'}, dimensions={0}, use_global_device_ids=true | all-gather | bytes 9216 | tf_op jit(solution)/shard_map/all_gather | solution.py:34
  181.9 21.3 %copy.110 = f32[2,10,24,1024]{3,2,1,0:T(8,128)} copy(f32[2,10,24,1024]{1,0,3,2:T(2,128)} %pad.13) | data formatting | bytes 3932160 | tf_op jit(solution)/shard_map/while | solution.py:193
  204.1 1.8 slice.165
  205.9 13.2 %all-gather.9.cloned.1.call-done = f32[128,10,4,128]{3,2,1,0:T(4,128)} async-done(((f32[16,10,4,128]{3,2,1,0:T(4,128)}), f32[128,10,4,128]{3,2,1,0:T(4,128)}) %all-gather.9.cloned.1.call-update) | async-done | bytes 2621456 | tf_op jit(solution)/shard_map/all_gather | solution.py:34
  219.2 3.3 slice.167
  222.5 36.0 %while.31 = (s32[]{:T(128)}, f32[]{:T(128)}, f32[16]{0:T(128)S(1)}, f32[16,10,4,128]{3,2,1,0:T(4,128)S(1)}, f32[16,16]{1,0:T(8,128)S(1)}, /*index=5*/f32[16,10,4...) while((s32[]{:T(128)}, f32[]{:T(128)}, f32[16]{0:T(128)S(1)}, ...), condition=%wide.region_6.7_spmd, body=%wide.region_5.6_spmd.sunk | while | flops 574278 | bytes 1970005 | solution.py:37
  225.7 1.3 fusion.73
  230.8 1.3 fusion.73
  236.0 1.3 fusion.73
  241.1 1.3 fusion.73
  246.2 1.3 fusion.73
  251.4 1.3 fusion.73
  256.5 1.3 fusion.73
  258.6 1.5 cholesky.16
  261.4 1.2 custom-call.10
  263.0 210.7 %while.32 = (s32[]{:T(128)}, f32[2,10,24,1024]{3,2,1,0:T(8,128)}, s32[16]{0:T(128)S(1)}, s32[16]{0:T(128)S(1)}, f32[16,10,4,128]{3,2,1,0:T(4,128)S(1)}, /*index=...) while((s32[]{:T(128)}, f32[2,10,24,1024]{3,2,1,0:T(8,128)}, s32[16]{0:T(128)S(1)}, ...), condition=%wide.region_10.11_spmd, body=%wide.region_9.10_spmd.sunk | while | flops 20488 | bytes 225517 | solution.py:193
  268.2 1.1 multiply_add_fusion.7
  269.2 7.6 %dynamic_update_slice.8 = f32[2,10,24,1024]{3,2,1,0:T(8,128)} dynamic-update-slice(f32[2,10,24,1024]{3,2,1,0:T(8,128)} %get-tuple-element.431, f32[2,10,4,128]{3,2,1,0:T(4,128)S(1)} %multiply_add_fusion.7, s32[]{:T(128)} %constant.153.clone.1..sunk, s32[]{:T(128)} %constant.153.clone.1..sunk, s32[]{:T(128)S(6)} %select_n.95, s32[]{:T(128)S(6)} %select_n.96) | dynamic-update-slice | bytes 81924 | tf_op jit(solution)/shard_map/while/body/eval_jaxpr/dynamic_update_slice | solution.py:191
  281.9 1.1 multiply_add_fusion.7
  283.0 7.6 %dynamic_update_slice.8 = f32[2,10,24,1024]{3,2,1,0:T(8,128)} dynamic-update-slice(f32[2,10,24,1024]{3,2,1,0:T(8,128)} %get-tuple-element.431, f32[2,10,4,128]{3,2,1,0:T(4,128)S(1)} %multiply_add_fusion.7, s32[]{:T(128)} %constant.153.clone.1..sunk, s32[]{:T(128)} %constant.153.clone.1..sunk, s32[]{:T(128)S(6)} %select_n.95, s32[]{:T(128)S(6)} %select_n.96) | dynamic-update-slice | bytes 81924 | tf_op jit(solution)/shard_map/while/body/eval_jaxpr/dynamic_update_slice | solution.py:191
  295.7 1.1 multiply_add_fusion.7
  296.8 7.6 %dynamic_update_slice.8 = f32[2,10,24,1024]{3,2,1,0:T(8,128)} dynamic-update-slice(f32[2,10,24,1024]{3,2,1,0:T(8,128)} %get-tuple-element.431, f32[2,10,4,128]{3,2,1,0:T(4,128)S(1)} %multiply_add_fusion.7, s32[]{:T(128)} %constant.153.clone.1..sunk, s32[]{:T(128)} %constant.153.clone.1..sunk, s32[]{:T(128)S(6)} %select_n.95, s32[]{:T(128)S(6)} %select_n.96) | dynamic-update-slice | bytes 81924 | tf_op jit(solution)/shard_map/while/body/eval_jaxpr/dynamic_update_slice | solution.py:191
  310.5 7.0 %dynamic_update_slice.8 = f32[2,10,24,1024]{3,2,1,0:T(8,128)} dynamic-update-slice(f32[2,10,24,1024]{3,2,1,0:T(8,128)} %get-tuple-element.431, f32[2,10,4,128]{3,2,1,0:T(4,128)S(1)} %multiply_add_fusion.7, s32[]{:T(128)} %constant.153.clone.1..sunk, s32[]{:T(128)} %constant.153.clone.1..sunk, s32[]{:T(128)S(6)} %select_n.95, s32[]{:T(128)S(6)} %select_n.96) | dynamic-update-slice | bytes 81924 | tf_op jit(solution)/shard_map/while/body/eval_jaxpr/dynamic_update_slice | solution.py:191
  322.6 1.1 multiply_add_fusion.7
  323.7 7.6 %dynamic_update_slice.8 = f32[2,10,24,1024]{3,2,1,0:T(8,128)} dynamic-update-slice(f32[2,10,24,1024]{3,2,1,0:T(8,128)} %get-tuple-element.431, f32[2,10,4,128]{3,2,1,0:T(4,128)S(1)} %multiply_add_fusion.7, s32[]{:T(128)} %constant.153.clone.1..sunk, s32[]{:T(128)} %constant.153.clone.1..sunk, s32[]{:T(128)S(6)} %select_n.95, s32[]{:T(128)S(6)} %select_n.96) | dynamic-update-slice | bytes 81924 | tf_op jit(solution)/shard_map/while/body/eval_jaxpr/dynamic_update_slice | solution.py:191
  336.4 1.1 multiply_add_fusion.7
  337.5 7.6 %dynamic_update_slice.8 = f32[2,10,24,1024]{3,2,1,0:T(8,128)} dynamic-update-slice(f32[2,10,24,1024]{3,2,1,0:T(8,128)} %get-tuple-element.431, f32[2,10,4,128]{3,2,1,0:T(4,128)S(1)} %multiply_add_fusion.7, s32[]{:T(128)} %constant.153.clone.1..sunk, s32[]{:T(128)} %constant.153.clone.1..sunk, s32[]{:T(128)S(6)} %select_n.95, s32[]{:T(128)S(6)} %select_n.96) | dynamic-update-slice | bytes 81924 | tf_op jit(solution)/shard_map/while/body/eval_jaxpr/dynamic_update_slice | solution.py:191
  350.2 1.1 multiply_add_fusion.7
  351.3 7.6 %dynamic_update_slice.8 = f32[2,10,24,1024]{3,2,1,0:T(8,128)} dynamic-update-slice(f32[2,10,24,1024]{3,2,1,0:T(8,128)} %get-tuple-element.431, f32[2,10,4,128]{3,2,1,0:T(4,128)S(1)} %multiply_add_fusion.7, s32[]{:T(128)} %constant.153.clone.1..sunk, s32[]{:T(128)} %constant.153.clone.1..sunk, s32[]{:T(128)S(6)} %select_n.95, s32[]{:T(128)S(6)} %select_n.96) | dynamic-update-slice | bytes 81924 | tf_op jit(solution)/shard_map/while/body/eval_jaxpr/dynamic_update_slice | solution.py:191
  363.9 1.1 multiply_add_fusion.7
  365.0 3.4 dynamic_update_slice.8
  374.5 2.8 dynamic_update_slice.8
  382.4 1.1 multiply_add_fusion.7
  383.5 7.6 %dynamic_update_slice.8 = f32[2,10,24,1024]{3,2,1,0:T(8,128)} dynamic-update-slice(f32[2,10,24,1024]{3,2,1,0:T(8,128)} %get-tuple-element.431, f32[2,10,4,128]{3,2,1,0:T(4,128)S(1)} %multiply_add_fusion.7, s32[]{:T(128)} %constant.153.clone.1..sunk, s32[]{:T(128)} %constant.153.clone.1..sunk, s32[]{:T(128)S(6)} %select_n.95, s32[]{:T(128)S(6)} %select_n.96) | dynamic-update-slice | bytes 81924 | tf_op jit(solution)/shard_map/while/body/eval_jaxpr/dynamic_update_slice | solution.py:191
  396.2 1.1 multiply_add_fusion.7
  397.3 7.6 %dynamic_update_slice.8 = f32[2,10,24,1024]{3,2,1,0:T(8,128)} dynamic-update-slice(f32[2,10,24,1024]{3,2,1,0:T(8,128)} %get-tuple-element.431, f32[2,10,4,128]{3,2,1,0:T(4,128)S(1)} %multiply_add_fusion.7, s32[]{:T(128)} %constant.153.clone.1..sunk, s32[]{:T(128)} %constant.153.clone.1..sunk, s32[]{:T(128)S(6)} %select_n.95, s32[]{:T(128)S(6)} %select_n.96) | dynamic-update-slice | bytes 81924 | tf_op jit(solution)/shard_map/while/body/eval_jaxpr/dynamic_update_slice | solution.py:191
  409.9 1.1 multiply_add_fusion.7
  411.0 7.6 %dynamic_update_slice.8 = f32[2,10,24,1024]{3,2,1,0:T(8,128)} dynamic-update-slice(f32[2,10,24,1024]{3,2,1,0:T(8,128)} %get-tuple-element.431, f32[2,10,4,128]{3,2,1,0:T(4,128)S(1)} %multiply_add_fusion.7, s32[]{:T(128)} %constant.153.clone.1..sunk, s32[]{:T(128)} %constant.153.clone.1..sunk, s32[]{:T(128)S(6)} %select_n.95, s32[]{:T(128)S(6)} %select_n.96) | dynamic-update-slice | bytes 81924 | tf_op jit(solution)/shard_map/while/body/eval_jaxpr/dynamic_update_slice | solution.py:191
  423.7 1.1 multiply_add_fusion.7
  424.8 7.6 %dynamic_update_slice.8 = f32[2,10,24,1024]{3,2,1,0:T(8,128)} dynamic-update-slice(f32[2,10,24,1024]{3,2,1,0:T(8,128)} %get-tuple-element.431, f32[2,10,4,128]{3,2,1,0:T(4,128)S(1)} %multiply_add_fusion.7, s32[]{:T(128)} %constant.153.clone.1..sunk, s32[]{:T(128)} %constant.153.clone.1..sunk, s32[]{:T(128)S(6)} %select_n.95, s32[]{:T(128)S(6)} %select_n.96) | dynamic-update-slice | bytes 81924 | tf_op jit(solution)/shard_map/while/body/eval_jaxpr/dynamic_update_slice | solution.py:191
  438.6 7.6 %dynamic_update_slice.8 = f32[2,10,24,1024]{3,2,1,0:T(8,128)} dynamic-update-slice(f32[2,10,24,1024]{3,2,1,0:T(8,128)} %get-tuple-element.431, f32[2,10,4,128]{3,2,1,0:T(4,128)S(1)} %multiply_add_fusion.7, s32[]{:T(128)} %constant.153.clone.1..sunk, s32[]{:T(128)} %constant.153.clone.1..sunk, s32[]{:T(128)S(6)} %select_n.95, s32[]{:T(128)S(6)} %select_n.96) | dynamic-update-slice | bytes 81924 | tf_op jit(solution)/shard_map/while/body/eval_jaxpr/dynamic_update_slice | solution.py:191
  451.3 1.1 multiply_add_fusion.7
  452.4 7.6 %dynamic_update_slice.8 = f32[2,10,24,1024]{3,2,1,0:T(8,128)} dynamic-update-slice(f32[2,10,24,1024]{3,2,1,0:T(8,128)} %get-tuple-element.431, f32[2,10,4,128]{3,2,1,0:T(4,128)S(1)} %multiply_add_fusion.7, s32[]{:T(128)} %constant.153.clone.1..sunk, s32[]{:T(128)} %constant.153.clone.1..sunk, s32[]{:T(128)S(6)} %select_n.95, s32[]{:T(128)S(6)} %select_n.96) | dynamic-update-slice | bytes 81924 | tf_op jit(solution)/shard_map/while/body/eval_jaxpr/dynamic_update_slice | solution.py:191
  465.1 1.1 multiply_add_fusion.7
  466.2 7.6 %dynamic_update_slice.8 = f32[2,10,24,1024]{3,2,1,0:T(8,128)} dynamic-update-slice(f32[2,10,24,1024]{3,2,1,0:T(8,128)} %get-tuple-element.431, f32[2,10,4,128]{3,2,1,0:T(4,128)S(1)} %multiply_add_fusion.7, s32[]{:T(128)} %constant.153.clone.1..sunk, s32[]{:T(128)} %constant.153.clone.1..sunk, s32[]{:T(128)S(6)} %select_n.95, s32[]{:T(128)S(6)} %select_n.96) | dynamic-update-slice | bytes 81924 | tf_op jit(solution)/shard_map/while/body/eval_jaxpr/dynamic_update_slice | solution.py:191
  473.8 2.8 slice.137
  (178 shorter events, 34.3 us)
Async XLA Ops:
  6.5 6.9 %copy-start = (f32[2,4,16,1024]{3,2,1,0:T(8,128)S(1)}, f32[2,4,16,1024]{3,2,1,0:T(8,128)}, u32[]{:S(2)}) copy-start(f32[2,4,16,1024]{3,2,1,0:T(8,128)} %param.16) | copy-start | bytes 1572868
  6.5 197.6 %all-gather.7.cloned.1.call-start = ((), (), s32[]{:S(2)}) async-start(), calls=%async_computation | async-start | bytes 2949120 | tf_op jit(solution)/shard_map/all_gather | solution.py:34
  8.0 5.7 %copy-start.2 = (s32[16,1024]{1,0:T(8,128)S(1)}, s32[16,1024]{1,0:T(8,128)}, u32[]{:S(2)}) copy-start(s32[16,1024]{1,0:T(8,128)} %param.17) | copy-start | bytes 196612
  8.0 5.7 %copy-start.3 = (f32[4,4]{1,0:T(4,128)S(1)}, f32[4,4]{1,0:T(4,128)}, u32[]{:S(2)}) copy-start(f32[4,4]{1,0:T(4,128)} %param.18) | copy-start | bytes 196
  8.2 7.3 %collective-permute-start = (f32[2,2,5,1,1024]{4,3,0,2,1:T(1,128)S(1)}, f32[2,2,5,1,1024]{4,3,0,2,1:T(1,128)S(1)}, u32[]{:S(2)}, u32[]{:S(2)}) collective-permute-start(f32[2,2,5,1,1024]{4,3,0,2,1:T(1,128)S(1)} %get-tuple-element.257), channel_id=1, source_target_pairs={{0,1},{1,2},{2,3},{4,5},{5,6},{6,7},{8,9},{9,10},{10,11},{12,13},{... | collective-permute-start | bytes 245768 | tf_op jit(solution)/shard_map/ppermute | solution.py:27
  9.5 6.0 %collective-permute-start.1 = (f32[2,2,5,1,1024]{4,3,0,2,1:T(1,128)S(1)}, f32[2,2,5,1,1024]{4,3,0,2,1:T(1,128)S(1)}, u32[]{:S(2)}, u32[]{:S(2)}) collective-permute-start(f32[2,2,5,1,1024]{4,3,0,2,1:T(1,128)S(1)} %get-tuple-element.258), channel_id=1, source_target_pairs={{1,0},{2,1},{3,2},{5,4},{6,5},{7,6},{9,8},{10,9},{11,10},{13,12},{... | collective-permute-start | bytes 245768 | tf_op jit(solution)/shard_map/ppermute | solution.py:28
  13.5 0.7 copy-start.5
  13.5 0.7 copy-start.6
  13.5 0.7 copy-start.9
  13.5 0.7 copy-start.10
  13.5 0.8 copy-start.11
  16.9 5.3 %collective-permute-start.2 = (f32[2,2,5,1,1024]{4,3,0,2,1:T(1,128)S(1)}, f32[2,2,5,1,1024]{4,3,0,2,1:T(1,128)S(1)}, u32[]{:S(2)}, u32[]{:S(2)}) collective-permute-start(f32[2,2,5,1,1024]{4,3,0,2,1:T(1,128)S(1)} %get-tuple-element.255), channel_id=1, source_target_pairs={{0,1},{1,2},{2,3},{4,5},{5,6},{6,7},{8,9},{9,10},{10,11},{12,13},{... | collective-permute-start | bytes 245768 | tf_op jit(solution)/shard_map/ppermute | solution.py:27
  18.2 5.5 %collective-permute-start.3 = (f32[2,2,5,1,1024]{4,3,0,2,1:T(1,128)S(1)}, f32[2,2,5,1,1024]{4,3,0,2,1:T(1,128)S(1)}, u32[]{:S(2)}, u32[]{:S(2)}) collective-permute-start(f32[2,2,5,1,1024]{4,3,0,2,1:T(1,128)S(1)} %get-tuple-element.256), channel_id=1, source_target_pairs={{1,0},{2,1},{3,2},{5,4},{6,5},{7,6},{9,8},{10,9},{11,10},{13,12},{... | collective-permute-start | bytes 245768 | tf_op jit(solution)/shard_map/ppermute | solution.py:28
  150.2 69.0 %all-gather.9.cloned.1.call-start = ((), (), s32[]{:S(2)}) async-start(), calls=%async_computation.1 | async-start | bytes 2949120 | tf_op jit(solution)/shard_map/all_gather | solution.py:34
  150.2 3.5 copy-start.4
  181.9 21.4 %copy-start.1 = (f32[128,16]{1,0:T(8,128)}, f32[128,16]{1,0:T(8,128)S(1)}, u32[]{:S(2)}) copy-start(f32[128,16]{1,0:T(8,128)S(1)} %all-gather.2) | copy-start | bytes 24580
  205.9 16.5 %slice-start.1 = ((f32[128,10,4,128]{3,2,1,0:T(4,128)}), f32[16,10,4,128]{3,2,1,0:T(4,128)S(1)}, s32[]{:S(2)}) async-start(f32[128,10,4,128]{3,2,1,0:T(4,128)} %all-gather.7.cloned.1.call-done), calls=%async_computation.3 | async-start | bytes 655360 | tf_op jit(solution)/shard_map/slice | solution.py:35
  205.9 16.5 %slice-start.2 = ((f32[128,16]{1,0:T(8,128)}), f32[16,16]{1,0:T(8,128)S(1)}, s32[]{:S(2)}) async-start(f32[128,16]{1,0:T(8,128)} %copy-done.1), calls=%async_computation.4 | async-start | bytes 16384 | tf_op jit(solution)/shard_map/slice | solution.py:35
  219.2 3.3 slice-start
  222.4 40.2 %copy-start.7 = (f32[2,16]{1,0:T(2,128)S(1)}, f32[2,16]{1,0:T(2,128)}, u32[]{:S(2)}) copy-start(f32[2,16]{1,0:T(2,128)} %param.25) | copy-start | bytes 388
  222.4 40.2 %copy-start.8 = (f32[16]{0:T(128)S(1)}, f32[16]{0:T(128)}, u32[]{:S(2)}) copy-start(f32[16]{0:T(128)} %param.23) | copy-start | bytes 196
Sparse Core Ops, SparseCore 0:
  150.3 36.7 all-gather.6
  189.0 30.1 all-gather.8
where the time goes:
time: 487 us; the launch traced here: 483 us
  local copies, waits for them, and re-layouts  260 us (53%)
  loops' own time  84.9 us (17%)
  other arithmetic  64.1 us (13%)
  blocking collectives  34.6 us (7%)
  waiting for transfers between devices  14.7 us (3%)
  between operations  14.4 us (3%)
  starting transfers between devices  10.6 us (2%)
    dynamic_update_slice x16, local copies, waits for them, and re-layouts, write_window_increment(): return lax.dynamic_update_slice(analysed, current + increment, corner)  112 us
    another operation x1, loops' own time, body(): lax.fori_loop(0, MEASURE_COUNT, write_window_increment, haloed_vector)  62.6 us
    another operation x1, local copies, waits for them, and re-layouts, deposition_advance(): return jnp.stack([new_top, new_bottom], axis=-4)  37.9 us
    reduce_sum x1, other arithmetic, body(): jnp.sum(patches * anomaly.T[:, :, None, None, None], axis=1)  29.1 us
    another operation x1, loops' own time, combined_all(): lax.scan(lambda running, share: (join(running, share), None), head, tail)  22.2 us
    while x1, local copies, waits for them, and re-layouts, body(): lax.fori_loop(0, MEASURE_COUNT, write_window_increment, haloed_vector)  21.3 us
    gather x1, local copies, waits for them, and re-layouts, cut_patch(): lax.dynamic_slice(haloed_vector, (window_offset, window_offset, window_fi...  18.9 us
    unnamed x1, blocking collectives  17.4 us
  transfers between devices with their start and end apart: 6, of which 2 were waited for; matrix products, arithmetic and copies ran while one was open for 6% of the time, Pallas kernels for 0%

commit v1 on v0

v1 whole, which is shorter than its diff:
```python
import functools

import jax
import jax.numpy as jnp
from jax import lax
from jax.experimental import pallas as pl
from jax.experimental.pallas import tpu as pltpu
from jax.sharding import PartitionSpec as P

NLAYER = 2
NCLASS = 4
KINDS = NCLASS + 1
FIELDS = NLAYER * KINDS
WINDOW_HEIGHT = 4
WINDOW_WIDTH = 128
DIFFUSION = 0.08
DEPOSIT = 0.5

LANES = 128
PAD = 8
GROUP = 8
NEAR_BLOCKS = 12
EXACT = lax.Precision.HIGHEST
MIB = 1024 * 1024

SMEM = pl.BlockSpec(memory_space=pltpu.SMEM)
VMEM = pl.BlockSpec(memory_space=pltpu.VMEM)


def call(kernel, name, in_specs, outs, scratch=(), flops=1000000):
    return pl.pallas_call(
        kernel,
        name=name,
        in_specs=in_specs,
        out_specs=[VMEM] * len(outs),
        out_shape=[jax.ShapeDtypeStruct(shape, jnp.float32) for shape in outs],
        scratch_shapes=list(scratch),
        compiler_params=pltpu.CompilerParams(vmem_limit_bytes=40 * MIB),
        cost_estimate=pl.CostEstimate(flops=flops, bytes_accessed=1000000, transcendentals=0),
    )


def lane_index(rows=8):
    return lax.broadcasted_iota(jnp.int32, (rows, LANES), 1)


def row_index(rows=8):
    return lax.broadcasted_iota(jnp.int32, (rows, LANES), 0)


def spread(ref, group, rows=8):
    index = lane_index(rows) // group
    total = jnp.zeros((rows, LANES), ref.dtype)
    for j in range(ref.shape[0]):
        total = jnp.where(index == j, ref[j], total)
    return total


def find_slots(lat, slots, first, rows, cap):
    for s in range(cap + 1):
        slots[s] = 0
    count = jnp.int32(0)
    for j in range(lat.shape[0]):
        start = lat[j] - WINDOW_HEIGHT // 2 - first
        slots[jnp.minimum(count, cap)] = j
        count = count + ((start < rows) & (start + WINDOW_HEIGHT > 0)).astype(jnp.int32)
    return jnp.minimum(count, cap)


def window(lat, lon, j, first, rows, tiles):
    row = jnp.clip(lat[j] - WINDOW_HEIGHT // 2 - first, -WINDOW_HEIGHT, rows) + PAD
    left = lon[j] - WINDOW_WIDTH // 2
    block = left // LANES
    return row, block, jnp.minimum(block + 1, tiles - 1), left % LANES


def coefficients(u, w):
    return (
        (1.0 - 4.0 * DIFFUSION) - (jnp.abs(u) + jnp.abs(w)),
        jnp.maximum(u, 0.0) + DIFFUSION,
        DIFFUSION - jnp.minimum(u, 0.0),
        jnp.maximum(w, 0.0) + DIFFUSION,
        DIFFUSION - jnp.minimum(w, 0.0),
    )


def stencil(coef, centre, up, down, left, right):
    return (coef[0] * centre + coef[1] * up) + (coef[2] * down + coef[3] * left) + coef[4] * right


def pack_kernel(lat, lon, kind, state, vel, band, out_a, out_b, near):
    members, _, rows, width = state.shape
    tiles = width // LANES
    tile = lax.axis_index("tile")
    even = tile % 2 == 0
    per = members * (2 * FIELDS + 2 * NLAYER)

    def edge(out, row, vrow):
        for i in range(tiles):
            lanes = slice(i * LANES, (i + 1) * LANES)
            for m in range(members):
                for f in range(FIELDS):
                    to = i * per + (m * FIELDS + f) * 2
                    out[to : to + 2, :] = state[m, f, row : row + 2, lanes]
                for c in range(2 * NLAYER):
                    to = i * per + members * FIELDS * 2 + m * 2 * NLAYER + c
                    out[to : to + 1, :] = vel[m, c, vrow : vrow + 1, lanes]

    @pl.when(even)
    def _():
        edge(out_a, rows - 2, rows - 1)
        edge(out_b, 0, 0)

    @pl.when(jnp.logical_not(even))
    def _():
        edge(out_a, 0, 0)
        edge(out_b, rows - 2, rows - 1)

    first = tile * rows
    latv = spread(lat, GROUP, rows)
    kindv = spread(kind, GROUP, rows)
    lonv = spread(lon, GROUP, 8)[:1]
    column = lonv - 2 + (lane_index(8)[:1] % GROUP)
    pick = (lax.broadcasted_iota(jnp.int32, (width, LANES), 0) == column).astype(jnp.float32)

    def chosen(array, lead):
        flat = array.reshape(lead * rows, width)
        out = jnp.dot(flat, pick, precision=EXACT, preferred_element_type=jnp.float32)
        return [out[n * rows : (n + 1) * rows] for n in range(lead)]

    qs = chosen(state[...], members * FIELDS)
    vs = chosen(vel[...], members * 2 * NLAYER)
    bs = chosen(band[...].astype(jnp.float32), 1)
    near[...] = jnp.zeros(near.shape, jnp.float32)
    at = row_index(rows) + first - latv

    def put(block, s, offset, values):
        row = jnp.sum(jnp.where(at == offset, values, 0.0), axis=0, keepdims=True)
        near[block * 8 + s : block * 8 + s + 1, :] = row

    for m in range(members):
        for l in range(NLAYER):
            s = m * NLAYER + l
            q = jnp.zeros((rows, LANES), jnp.float32)
            for k in range(KINDS):
                q = jnp.where(kindv == k, qs[m * FIELDS + l * KINDS + k], q)
            for i in range(5):
                put(i, s, i - 2, q)
            for c in range(2):
                for i in range(3):
                    put(5 + 3 * c + i, s, i - 1, vs[m * 2 * NLAYER + 2 * l + c])
    put(11, 0, 0, bs[0])
    base = tiles * per
    out_a[base : base + NEAR_BLOCKS * 8, :] = near[...]


def forecast_kernel(cap, others, lat, lon, layer, kind, table, state, vel, band, from_a, from_b, *rest):
    nears, rest = rest[: 1 + others], rest[1 + others :]
    out, own, send, obs_out, sel, s0, s1, vs, padded, slots = rest
    members, _, rows, width = state.shape
    tiles = width // LANES
    tile = lax.axis_index("tile")
    count_tiles = lax.axis_size("tile")
    core = lax.axis_index("member") % 2
    first = tile * rows
    even = tile % 2 == 0
    per = members * (2 * FIELDS + 2 * NLAYER)
    total_rows = rows + 2 * PAD
    zero = jnp.zeros((total_rows, LANES), jnp.float32)
    inside = slice(PAD, PAD + rows)

    for mf in range(members * FIELDS):
        for i in range(tiles):
            s0[mf, i + 1, inside, :] = state[mf // FIELDS, mf % FIELDS, :, i * LANES : (i + 1) * LANES]
        for buffer in (s0, s1):
            buffer[mf, 0, :, :] = zero
            buffer[mf, tiles + 1, :, :] = zero
    for mc in range(members * 2 * NLAYER):
        for i in range(tiles):
            vs[mc, i, inside, :] = vel[mc // (2 * NLAYER), mc % (2 * NLAYER), :, i * LANES : (i + 1) * LANES]

    def edge(source, row, vrow):
        for i in range(tiles):
            for mf in range(members * FIELDS):
                at = i * per + mf * 2
                s0[mf, i + 1, row : row + 2, :] = source[at : at + 2, :]
            for mc in range(members * 2 * NLAYER):
                at = i * per + members * FIELDS * 2 + mc
                vs[mc, i, vrow : vrow + 1, :] = source[at : at + 1, :]

    @pl.when(even)
    def _():
        edge(from_a, PAD + rows, PAD + rows)
        edge(from_b, PAD - 2, PAD - 1)

    @pl.when(jnp.logical_not(even))
    def _():
        edge(from_a, PAD - 2, PAD - 1)
        edge(from_b, PAD + rows, PAD + rows)

    lane = lane_index()
    at_left = lane == 0
    at_right = lane == LANES - 1

    def advance(source, f, i, r, coef):
        centre = source[f, i + 1, r : r + 8, :]
        up = source[f, i + 1, r - 1 : r + 7, :]
        down = source[f, i + 1, r + 1 : r + 9, :]
        before = source[f, i, r : r + 8, :]
        after = source[f, i + 2, r : r + 8, :]
        left = pltpu.roll(jnp.where(at_right, before, centre), 1, 1)
        right = pltpu.roll(jnp.where(at_left, after, centre), LANES - 1, 1)
        return stencil(coef, centre, up, down, left, right)

    def first_step(t, carry):
        ml, i = t // tiles, t % tiles
        for r in range(PAD - 1, PAD + rows + 1, 8):
            coef = coefficients(vs[2 * ml, i, r : r + 8, :], vs[2 * ml + 1, i, r : r + 8, :])
            for k in range(KINDS):
                s1[ml * KINDS + k, i + 1, r : r + 8, :] = advance(s0, ml * KINDS + k, i, r, coef)
        return carry

    lax.fori_loop(0, members * NLAYER * tiles, first_step, 0)

    @pl.when(tile == 0)
    def _():
        s1[:, :, PAD - 1 : PAD, :] = jnp.zeros((members * FIELDS, tiles + 2, 1, LANES), jnp.float32)

    @pl.when(tile == count_tiles - 1)
    def _():
        s1[:, :, PAD + rows : PAD + rows + 1, :] = jnp.zeros(
            (members * FIELDS, tiles + 2, 1, LANES), jnp.float32
        )

    def second_step(t, carry):
        m, i = t // tiles, t % tiles
        lanes = pl.ds(pl.multiple_of(i * LANES, LANES), LANES)
        for r in range(PAD, PAD + rows, 8):
            coefs = []
            for l in range(NLAYER):
                mc = (m * NLAYER + l) * 2
                coefs.append(coefficients(vs[mc, i, r : r + 8, :], vs[mc + 1, i, r : r + 8, :]))
            bins = band[r - PAD : r - PAD + 8, lanes]
            for k in range(KINDS):
                upper = m * FIELDS + k
                lower = upper + KINDS
                a = advance(s1, upper, i, r, coefs[0])
                b = advance(s1, lower, i, r, coefs[1])
                if k > 0:
                    rate = jnp.full((8, LANES), table[0, k - 1], jnp.float32)
                    for level in range(1, table.shape[0]):
                        rate = jnp.where(bins == level, table[level, k - 1], rate)
                    settled = rate * a
                    a, b = a - settled, b + settled - DEPOSIT * rate * b
                for f, value in ((k, a), (k + KINDS, b)):
                    padded[m * FIELDS + f, i, r : r + 8, :] = value
                    out[m, f, r - PAD : r - PAD + 8, lanes] = value
        return carry

    lax.fori_loop(0, members * tiles, second_step, 0)

    for mf in range(members * FIELDS):
        for i in range(tiles):
            padded[mf, i, :PAD, :] = zero[:PAD]
            padded[mf, i, PAD + rows :, :] = zero[:PAD]

    base = tiles * per
    blocks = []
    for n in range(NEAR_BLOCKS):
        block = from_a[base + 8 * n : base + 8 * n + 8, :]
        for near in nears:
            block = block + near[8 * n : 8 * n + 8, :]
        blocks.append(block)

    def step(up, centre, down, coef):
        return stencil(
            coef, centre, up, down, pltpu.roll(centre, 1, 1), pltpu.roll(centre, LANES - 1, 1)
        )

    coefs = [coefficients(blocks[5 + i], blocks[8 + i]) for i in range(3)]
    once = [step(blocks[i], blocks[i + 1], blocks[i + 2], coefs[i]) for i in range(3)]
    value = step(once[0], once[1], once[2], coefs[1])
    bins = jnp.broadcast_to(blocks[11][:1], (8, LANES))
    kinds = spread(kind, GROUP)
    rate = jnp.zeros((8, LANES), jnp.float32)
    for level in range(table.shape[0]):
        here = jnp.abs(bins - level) < 0.5
        for k in range(NCLASS):
            rate = jnp.where(here & (kinds == k + 1), table[level, k], rate)
    bottom = row_index() % 2 == 1
    above = pltpu.roll(value, 1, 0)
    settled = jnp.where(
        bottom, value + rate * above - DEPOSIT * rate * value, value - rate * value
    )
    settled = jnp.where(spread(layer, GROUP) == 0, settled, pltpu.roll(settled, 7, 0))
    squeeze = (
        lax.broadcasted_iota(jnp.int32, (LANES, LANES), 0)
        == lax.broadcasted_iota(jnp.int32, (LANES, LANES), 1) * GROUP + 2
    ).astype(jnp.float32)
    seen = jnp.dot(settled, squeeze, precision=EXACT, preferred_element_type=jnp.float32)
    obs_out[...] = jnp.zeros((8, LANES), jnp.float32)
    for m in range(members):
        obs_out[m : m + 1, :] = seen[2 * m : 2 * m + 1]

    size = cap * WINDOW_HEIGHT
    count = find_slots(lat, slots, first, rows, cap)
    for s in range(cap):
        sel[s * 4 : s * 4 + 4, :] = (lane[:4] == slots[s]).astype(jnp.float32)
    send[members * KINDS * size :, :] = obs_out[...]

    def cut(layer_of_own):
        def one(s, carry):
            row, block, after, shift = window(lat, lon, slots[s], first, rows, tiles)
            here = lane >= shift
            for l, target in ((layer_of_own, own), (1 - layer_of_own, send)):
                for m in range(members):
                    for k in range(KINDS):
                        f = m * FIELDS + l * KINDS + k
                        both = jnp.where(
                            here, padded[f, block, pl.ds(row, 8), :], padded[f, after, pl.ds(row, 8), :]
                        )
                        patch = pltpu.roll(both, (LANES - shift) % LANES, 1)
                        target[pl.ds((m * KINDS + k) * size + s * 4, 4), :] = patch[:4]
            return carry

        lax.fori_loop(0, count, one, 0)

    for c in range(2):
        pl.when(core == c)(functools.partial(cut, c))


def pair_kernel(cap, members, own, got, obs, sel, msg):
    size = cap * WINDOW_HEIGHT
    part = KINDS * size
    seen = obs[:members, :]
    theirs = got[members * part : members * part + members, :]
    mean = (jnp.sum(seen, axis=0, keepdims=True) + jnp.sum(theirs, axis=0, keepdims=True)) / (2 * members)
    sources = [(own, m, seen[m : m + 1]) for m in range(members)]
    sources += [(got, m, theirs[m : m + 1]) for m in range(members)]
    weight = [jnp.sum(sel[...] * (o - mean), axis=1, keepdims=True) for _, _, o in sources]
    for k in range(KINDS):
        cross = jnp.zeros((size, LANES), jnp.float32)
        total = jnp.zeros((size, LANES), jnp.float32)
        for (ref, m, _), o in zip(sources, weight):
            patch = ref[m * part + k * size : m * part + (k + 1) * size, :]
            cross = cross + patch * o
            total = total + patch
        msg[k * size : (k + 1) * size, :] = cross
        msg[part + k * size : part + (k + 1) * size, :] = total
    msg[2 * part :, :] = jnp.zeros((8, LANES), jnp.float32)
    msg[2 * part : 2 * part + members, :] = seen
    msg[2 * part + members : 2 * part + 2 * members, :] = theirs


def merge_kernel(cap, members, chips, value, error, perturb, obs, sel, *rest):
    msgs, (gain, weights, everyone) = rest[:chips], rest[chips:]
    size = cap * WINDOW_HEIGHT
    part = KINDS * size
    both = 2 * members
    number = chips * both
    observations = value.shape[0]
    means = []
    for c, msg in enumerate(msgs):
        seen = msg[2 * part : 2 * part + both, :]
        everyone[c * both : (c + 1) * both, :] = seen
        means.append(jnp.sum(seen, axis=0, keepdims=True) / both)
    mean = functools.reduce(jnp.add, means) / chips
    shifts = [jnp.sum(sel[...] * (own - mean), axis=1, keepdims=True) for own in means]
    row = (row_index(size) % WINDOW_HEIGHT).astype(jnp.float32)
    column = lane_index(size).astype(jnp.float32)
    row = (row + 0.5 - WINDOW_HEIGHT / 2) / (WINDOW_HEIGHT / 2)
    column = (column + 0.5 - WINDOW_WIDTH / 2) / (WINDOW_WIDTH / 2)
    taper = (1.0 - row * row) * (1.0 - column * column) / (number - 1)
    for k in range(KINDS):
        cross = jnp.zeros((size, LANES), jnp.float32)
        for msg, shift in zip(msgs, shifts):
            cross = cross + msg[k * size : (k + 1) * size, :]
            cross = cross + shift * msg[part + k * size : part + (k + 1) * size, :]
        gain[k * size : (k + 1) * size, :] = taper * cross
    gain[part:, :] = jnp.zeros((8, LANES), jnp.float32)

    anomaly = everyone[...] - mean
    over = (((0,), (0,)), ((), ()))
    cov = lax.dot_general(anomaly, anomaly, over, precision=EXACT, preferred_element_type=jnp.float32)
    row16 = row_index(observations)
    lane16 = lane_index(observations)
    errors = spread(error, 1)
    innovation = spread(value, 1)[:members] - obs[:members, :]
    noise = jnp.concatenate(
        [perturb[...], jnp.zeros((members, LANES - observations), jnp.float32)], axis=1
    )
    innovation = innovation + jnp.sqrt(errors[:members]) * noise
    place = (lane_index(members) == row_index(members) + observations).astype(jnp.float32)
    sides = lax.dot_general(innovation, place, over, precision=EXACT, preferred_element_type=jnp.float32)
    system = jnp.where(lane16 < observations, cov[:observations] / (number - 1), sides[:observations])
    system = system + jnp.where(lane16 == row16, jnp.broadcast_to(errors[:1], row16.shape), 0.0)
    for k in range(observations):
        pivot = system[k : k + 1, :] / system[k : k + 1, k : k + 1]
        system = jnp.where(row16 == k, pivot, system - system[:, k : k + 1] * pivot)
    for m in range(members):
        weights[m, :, :] = jnp.broadcast_to(
            system[:, observations + m : observations + m + 1], (observations, LANES)
        )


def apply_kernel(cap, lat, lon, field, mine, theirs, weights, out, work, slots):
    members, _, rows, width = field.shape
    tiles = width // LANES
    size = cap * WINDOW_HEIGHT
    first = lax.axis_index("tile") * rows
    core = lax.axis_index("member") % 2
    for mf in range(members * FIELDS):
        for i in range(tiles):
            work[mf, i, PAD : PAD + rows, :] = field[
                mf // FIELDS, mf % FIELDS, :, i * LANES : (i + 1) * LANES
            ]
    count = find_slots(lat, slots, first, rows, cap)
    lane = lane_index()
    patch_row = row_index() < WINDOW_HEIGHT

    def add(layer_of_own):
        def one(s, carry):
            j = slots[s]
            row, block, after, shift = window(lat, lon, j, first, rows, tiles)
            here = patch_row & (lane >= shift)
            there = patch_row & (lane < shift)
            w = [weights[m, pl.ds(j, 1), :] for m in range(members)]
            for l, source in ((layer_of_own, mine), (1 - layer_of_own, theirs)):
                for k in range(KINDS):
                    gain = pltpu.roll(source[pl.ds(k * size + s * 4, 8), :], shift, 1)
                    near = jnp.where(here, gain, 0.0)
                    far = jnp.where(there, gain, 0.0)
                    for m in range(members):
                        f = m * FIELDS + l * KINDS + k
                        work[f, block, pl.ds(row, 8), :] += near * w[m]
                        work[f, after, pl.ds(row, 8), :] += far * w[m]
            return carry

        lax.fori_loop(0, count, one, 0)

    for c in range(2):
        pl.when(core == c)(functools.partial(add, c))
    for mf in range(members * FIELDS):
        for i in range(tiles):
            out[mf // FIELDS, mf % FIELDS, :, i * LANES : (i + 1) * LANES] = work[
                mf, i, PAD : PAD + rows, :
            ]


def partner(size, k):
    if size & (size - 1) == 0:
        return [(i, i ^ k) for i in range(size)]
    return [(i, (i + k) % size) for i in range(size)]


def body(state, vel, band, table, lat, lon, layer, kind, value, error, perturb):
    members, _, rows, width = state.shape
    tiles = width // LANES
    row_tiles = lax.axis_size("tile")
    devices = lax.axis_size("member")
    chips = devices // 2
    observations = lat.shape[0]
    per = members * (2 * FIELDS + 2 * NLAYER)
    edge = tiles * per
    near_rows = NEAR_BLOCKS * 8
    out_a, out_b, near = call(
        pack_kernel,
        "pack_edges",
        [SMEM] * 3 + [VMEM] * 3,
        [(edge + near_rows, LANES), (edge, LANES), (near_rows, LANES)],
    )(lat, lon, kind, state, vel, band)
    pairs_a = [(i, i + 1) for i in range(0, row_tiles - 1, 2)]
    pairs_b = [(i, i + 1) for i in range(1, row_tiles - 1, 2)]
    from_a = lax.ppermute(out_a, "tile", pairs_a + [(j, i) for i, j in pairs_a])
    from_b = lax.ppermute(out_b, "tile", pairs_b + [(j, i) for i, j in pairs_b])
    nears = [near] + [lax.ppermute(near, "tile", partner(row_tiles, k)) for k in range(2, row_tiles)]

    cap = observations
    size = cap * WINDOW_HEIGHT
    part = KINDS * size
    padded_rows = rows + 2 * PAD
    field, own, send, obs, sel = call(
        functools.partial(forecast_kernel, cap, len(nears) - 1),
        "forecast",
        [SMEM] * 5 + [VMEM] * (5 + len(nears)),
        [
            state.shape,
            (members * part, LANES),
            (members * part + 8, LANES),
            (8, LANES),
            (size, LANES),
        ],
        [
            pltpu.VMEM((members * FIELDS, tiles + 2, padded_rows, LANES), jnp.float32),
            pltpu.VMEM((members * FIELDS, tiles + 2, padded_rows, LANES), jnp.float32),
            pltpu.VMEM((members * 2 * NLAYER, tiles, padded_rows, LANES), jnp.float32),
            pltpu.VMEM((members * FIELDS, tiles, padded_rows, LANES), jnp.float32),
            pltpu.SMEM((cap + 1,), jnp.int32),
        ],
    )(lat, lon, layer, kind, table, state, vel, band, from_a, from_b, *nears)
    got = lax.ppermute(send, "member", [(i, i ^ 1) for i in range(devices)])
    (msg,) = call(
        functools.partial(pair_kernel, cap, members),
        "pair_moments",
        [VMEM] * 4,
        [(2 * part + 8, LANES)],
    )(own, got, obs, sel)
    msgs = [msg] + [lax.ppermute(msg, "member", partner(devices, 2 * k)) for k in range(1, chips)]
    mine, weights = call(
        functools.partial(merge_kernel, cap, members, chips),
        "merge_moments",
        [SMEM] * 2 + [VMEM] * (3 + chips),
        [(part + 8, LANES), (members, observations, LANES)],
        [pltpu.VMEM((chips * 2 * members, LANES), jnp.float32)],
    )(value, error, perturb, obs, sel, *msgs)
    theirs = lax.ppermute(mine, "member", [(i, i ^ 1) for i in range(devices)])
    (analysed,) = call(
        functools.partial(apply_kernel, cap),
        "apply_increments",
        [SMEM] * 2 + [VMEM] * 4,
        [state.shape],
        [
            pltpu.VMEM((members * FIELDS, tiles, padded_rows, LANES), jnp.float32),
            pltpu.SMEM((cap + 1,), jnp.int32),
        ],
    )(lat, lon, field, mine, theirs, weights)
    return analysed


def solution(mesh):
    placed = (
        P("member", None, "tile", None),
        P("member", None, "tile", None),
        P("tile", None),
        P(),
        P(),
        P(),
        P(),
        P(),
        P(),
        P(),
        P("member", None),
    )
    return jax.shard_map(
        body, mesh=mesh, in_specs=placed, out_specs=P("member", None, "tile", None), check_vma=False
    )
```

time: 487 us -> 57.9 us (0.12)
  the two profiles are of different devices: /device:TPU:25 before, /device:TPU:1 now
where the time goes in v1:
time: 57.9 us
  waiting for transfers between devices  24 us (41%)
  Pallas kernels  15.4 us (27%)
  starting transfers between devices  13.2 us (23%)
  local copies, waits for them, and re-layouts  5.19 us (9%)
    ppermute x3, waiting for transfers between devices, body(): lax.ppermute(msg, 'member', partner(devices, 2 * k))  15.1 us
    pallas_call x1, Pallas kernels, body(): call(functools.partial(forecast_kernel, cap, len(nears) - 1), 'forecast',...  7.5 us
    ppermute x2, waiting for transfers between devices, body(): lax.ppermute(near, 'tile', partner(row_tiles, k))  6.64 us
    unnamed x22, local copies, waits for them, and re-layouts  5.19 us
    ppermute x2, starting transfers between devices, body(): lax.ppermute(near, 'tile', partner(row_tiles, k))  5.07 us
    pallas_call x1, Pallas kernels, body(): call(functools.partial(apply_kernel, cap), 'apply_increments', [SMEM] * 2...  2.93 us
    ppermute x3, starting transfers between devices, body(): lax.ppermute(msg, 'member', partner(devices, 2 * k))  2.71 us
    pallas_call x1, Pallas kernels, body(): call(pack_kernel, 'pack_edges', [SMEM] * 3 + [VMEM] * 3, [(edge + near_ro...  2.63 us
  transfers between devices with their start and end apart: 9, of which 6 were waited for; matrix products, arithmetic and copies ran while one was open for 0% of the time, Pallas kernels for 0%

profile of v1, /device:TPU:1, one launch (start us, length us, event | category | flops | bytes accessed | tf_op | source)
XLA Modules:
  0.0 57.9 jit_solution(4175186878689266946)
XLA Ops:
  0.0 0.0 copy-start
  0.0 1.3 %copy-done = f32[2,10,16,1024]{3,2,1,0:T(8,128)S(1)} copy-done((f32[2,10,16,1024]{3,2,1,0:T(8,128)S(1)}, f32[2,10,16,1024]{3,2,1,0:T(8,128)}, u32[]{:S(2)}) %copy-start) | copy-done | bytes 1310744
  1.3 0.0 copy-start.1
  1.3 1.0 %copy-done.1 = f32[2,4,16,1024]{3,2,1,0:T(8,128)S(1)} copy-done((f32[2,4,16,1024]{3,2,1,0:T(8,128)S(1)}, f32[2,4,16,1024]{3,2,1,0:T(8,128)}, u32[]{:S(2)}) %copy-start.1) | copy-done | bytes 524312
  2.4 0.0 copy-start.2
  2.4 0.8 %copy-done.2 = s32[16,1024]{1,0:T(8,128)S(1)} copy-done((s32[16,1024]{1,0:T(8,128)S(1)}, s32[16,1024]{1,0:T(8,128)}, u32[]{:S(2)}) %copy-start.2) | copy-done | bytes 65560
  3.2 0.0 copy-start.3
  3.2 0.7 %copy-done.3 = s32[16]{0:T(128)S(1)} copy-done((s32[16]{0:T(128)S(1)}, s32[16]{0:T(128)}, u32[]{:S(2)}) %copy-start.3) | copy-done | bytes 88
  3.9 0.0 copy-start.4
  3.9 0.7 %copy-done.4 = s32[16]{0:T(128)S(1)} copy-done((s32[16]{0:T(128)S(1)}, s32[16]{0:T(128)}, u32[]{:S(2)}) %copy-start.4) | copy-done | bytes 88
  4.5 0.0 copy-start.6
  4.5 0.7 %copy-done.6 = s32[16]{0:T(128)S(1)} copy-done((s32[16]{0:T(128)S(1)}, s32[16]{0:T(128)}, u32[]{:S(2)}) %copy-start.6) | copy-done | bytes 88
  5.2 0.0 copy-start.5
  5.2 0.0 copy-start.8
  5.2 2.6 %pack_edges.1 = (f32[480,128]{1,0:T(8,128)S(1)}, f32[384,128]{1,0:T(8,128)S(1)}, f32[96,128]{1,0:T(8,128)S(1)}) custom-call(s32[16]{0:T(128)S(1)} %copy-done.3, s32[16]{0:T(128)S(1)} %copy-done.4, s32[16]{0:T(128)S(1)} %copy-done.6, f32[2,10,16,1024]{3,2,1,0:T(8,128)S(1)} %copy-done, f32[2,4,16,1024]{3,2,1,0:T(8,128)S(1)} %copy-done.1, s32[16,1024]{1,0:T(8,128)S(1)} %copy-done.2), custom_call_target="tpu_custom_call" | custom-call | flops 1000000 | bytes 1000000 | tf_op jit(solution)/shard_map/pack_edges/pallas_call | solution.py:466
  7.8 2.2 %collective-permute-start = (f32[480,128]{1,0:T(8,128)S(1)}, f32[480,128]{1,0:T(8,128)S(1)}, u32[]{:S(2)}, u32[]{:S(2)}) collective-permute-start(f32[480,128]{1,0:T(8,128)S(1)} %get-tuple-element.15), channel_id=1, source_target_pairs={{0,1},{2,3},{1,0},{3,2},{4,5},{6,7},{5,4},{7,6},{8,9},{10,11},{9,8... | collective-permute-start | bytes 737288 | tf_op jit(solution)/shard_map/ppermute | solution.py:474
  10.0 0.7 %collective-permute-start.1 = (f32[384,128]{1,0:T(8,128)S(1)}, f32[384,128]{1,0:T(8,128)S(1)}, u32[]{:S(2)}, u32[]{:S(2)}) collective-permute-start(f32[384,128]{1,0:T(8,128)S(1)} %get-tuple-element.16), channel_id=1, source_target_pairs={{1,2},{2,1},{5,6},{6,5},{9,10},{10,9},{13,14},{14,13},{17,18},{18,... | collective-permute-start | bytes 589832 | tf_op jit(solution)/shard_map/ppermute | solution.py:475
  10.7 0.0 copy-start.7
  10.7 0.0 copy-start.9
  10.7 0.0 copy-start.10
  10.7 2.3 %collective-permute-start.3 = (f32[96,128]{1,0:T(8,128)S(1)}, f32[96,128]{1,0:T(8,128)S(1)}, u32[]{:S(2)}, u32[]{:S(2)}) collective-permute-start(f32[96,128]{1,0:T(8,128)S(1)} %get-tuple-element.17.rest_0_), channel_id=1, source_target_pairs={{0,3},{1,2},{2,1},{3,0},{4,7},{5,6},{6,5},{7,4},{8,11},{9,10},{10,... | collective-permute-start | bytes 147464 | tf_op jit(solution)/shard_map/ppermute | solution.py:476
  13.0 2.8 %collective-permute-start.2 = (f32[96,128]{1,0:T(8,128)S(1)}, f32[96,128]{1,0:T(8,128)S(1)}, u32[]{:S(2)}, u32[]{:S(2)}) collective-permute-start(f32[96,128]{1,0:T(8,128)S(1)} %get-tuple-element.17.rest_0_), channel_id=1, source_target_pairs={{0,2},{1,3},{2,0},{3,1},{4,6},{5,7},{6,4},{7,5},{8,10},{9,11},{10,... | collective-permute-start | bytes 147464 | tf_op jit(solution)/shard_map/ppermute | solution.py:476
  15.8 2.5 %collective-permute-done.3.rest_2_ = f32[96,128]{1,0:T(8,128)S(1)} collective-permute-done((f32[96,128]{1,0:T(8,128)S(1)}, f32[96,128]{1,0:T(8,128)S(1)}, u32[]{:S(2)}, u32[]{:S(2)}) %collective-permute-start.3) | collective-permute-done | bytes 49184 | tf_op jit(solution)/shard_map/ppermute | solution.py:476
  18.3 4.1 %collective-permute-done.2.rest_1_ = f32[96,128]{1,0:T(8,128)S(1)} collective-permute-done((f32[96,128]{1,0:T(8,128)S(1)}, f32[96,128]{1,0:T(8,128)S(1)}, u32[]{:S(2)}, u32[]{:S(2)}) %collective-permute-start.2) | collective-permute-done | bytes 49184 | tf_op jit(solution)/shard_map/ppermute | solution.py:476
  22.4 0.0 collective-permute-done.1.from_b
  22.4 0.0 collective-permute-done.from_a
  22.4 0.0 copy-done.5
  22.4 0.0 copy-done.8
  22.4 7.5 %forecast.1 = (f32[2,10,16,1024]{3,2,1,0:T(8,128)S(1)}, f32[640,128]{1,0:T(8,128)S(1)}, f32[648,128]{1,0:T(8,128)S(1)}, f32[8,128]{1,0:T(8,128)S(1)}, f32[64,128]{1,0:T(8,128)S(1)}) custom-call(s32[16]{0:T(128)S(1)} %copy-done.3, s32[16]{0:T(128)S(1)} %copy-done.4, s32[16]{0:T(128)S(1)} %copy-done.8, s32[16]{0:T(128)S(1)} %copy-done.6, ...), custom_call_target="tpu_custom_call" | custom-call | flops 1000000 | bytes 1000000 | tf_op jit(solution)/shard_map/forecast/pallas_call | solution.py:482
  29.9 1.9 %collective-permute-start.4 = (f32[648,128]{1,0:T(8,128)S(1)}, f32[648,128]{1,0:T(8,128)S(1)}, u32[]{:S(2)}, u32[]{:S(2)}) collective-permute-start(f32[648,128]{1,0:T(8,128)S(1)} %get-tuple-element.22), channel_id=1, source_target_pairs={{0,4},{4,0},{8,12},{12,8},{16,20},{20,16},{24,28},{28,24},{1,5},{5... | collective-permute-start | bytes 995336 | tf_op jit(solution)/shard_map/ppermute | solution.py:501
  31.9 1.3 %collective-permute-done.4.got = f32[648,128]{1,0:T(8,128)S(1)} collective-permute-done((f32[648,128]{1,0:T(8,128)S(1)}, f32[648,128]{1,0:T(8,128)S(1)}, u32[]{:S(2)}, u32[]{:S(2)}) %collective-permute-start.4) | collective-permute-done | bytes 331808 | tf_op jit(solution)/shard_map/ppermute | solution.py:501
  33.1 0.1 pair_moments.1.rest_0_
  33.3 2.2 %collective-permute-start.7 = (f32[648,128]{1,0:T(8,128)S(1)}, f32[648,128]{1,0:T(8,128)S(1)}, u32[]{:S(2)}, u32[]{:S(2)}) collective-permute-start(f32[648,128]{1,0:T(8,128)S(1)} %pair_moments.1.rest_0_), channel_id=1, source_target_pairs={{0,24},{4,28},{8,16},{12,20},{16,8},{20,12},{24,0},{28,4},{1,25},{... | collective-permute-start | bytes 995336 | tf_op jit(solution)/shard_map/ppermute | solution.py:508
  35.5 0.2 collective-permute-start.6
  35.7 0.3 collective-permute-start.5
  36.0 7.3 %collective-permute-done.7.rest_3_ = f32[648,128]{1,0:T(8,128)S(1)} collective-permute-done((f32[648,128]{1,0:T(8,128)S(1)}, f32[648,128]{1,0:T(8,128)S(1)}, u32[]{:S(2)}, u32[]{:S(2)}) %collective-permute-start.7) | collective-permute-done | bytes 331808 | tf_op jit(solution)/shard_map/ppermute | solution.py:508
  43.3 7.8 %collective-permute-done.6.rest_2_ = f32[648,128]{1,0:T(8,128)S(1)} collective-permute-done((f32[648,128]{1,0:T(8,128)S(1)}, f32[648,128]{1,0:T(8,128)S(1)}, u32[]{:S(2)}, u32[]{:S(2)}) %collective-permute-start.6) | collective-permute-done | bytes 331808 | tf_op jit(solution)/shard_map/ppermute | solution.py:508
  51.0 0.0 collective-permute-done.5.rest_1_
  51.1 0.0 copy-done.7
  51.1 0.0 copy-done.9
  51.1 0.0 copy-done.10
  51.1 2.2 %merge_moments.1 = (f32[328,128]{1,0:T(8,128)S(1)}, f32[2,16,128]{2,1,0:T(8,128)S(1)}) custom-call(f32[16]{0:T(128)S(1)} %copy-done.9, f32[16]{0:T(128)S(1)} %copy-done.10, f32[2,16]{1,0:T(2,128)S(1)} %copy-done.7, f32[8,128]{1,0:T(8,128)S(1)} %get-tuple-element.19.obs, f32[64,128]{1,0:T(8,128)S(1)} %get-tuple-element.20.sel, ...), custom_call_target="tpu_custom_call" | custom-call | flops 1000000 | bytes 1000000 | tf_op jit(solution)/shard_map/merge_moments/pallas_call | solution.py:509
  53.3 0.6 %collective-permute-start.8 = (f32[328,128]{1,0:T(8,128)S(1)}, f32[328,128]{1,0:T(8,128)S(1)}, u32[]{:S(2)}, u32[]{:S(2)}) collective-permute-start(f32[328,128]{1,0:T(8,128)S(1)} %get-tuple-element.23.mine), channel_id=1, source_target_pairs={{0,4},{4,0},{8,12},{12,8},{16,20},{20,16},{24,28},{28,24},{1,5},{5... | collective-permute-start | bytes 503816 | tf_op jit(solution)/shard_map/ppermute | solution.py:516
  53.9 1.0 %collective-permute-done.8.theirs = f32[328,128]{1,0:T(8,128)S(1)} collective-permute-done((f32[328,128]{1,0:T(8,128)S(1)}, f32[328,128]{1,0:T(8,128)S(1)}, u32[]{:S(2)}, u32[]{:S(2)}) %collective-permute-start.8) | collective-permute-done | bytes 167968 | tf_op jit(solution)/shard_map/ppermute | solution.py:516
  54.9 2.9 %apply_increments.1 = f32[2,10,16,1024]{3,2,1,0:T(8,128)} custom-call(s32[16]{0:T(128)S(1)} %copy-done.3, s32[16]{0:T(128)S(1)} %copy-done.4, f32[2,10,16,1024]{3,2,1,0:T(8,128)S(1)} %get-tuple-element.18.field, f32[328,128]{1,0:T(8,128)S(1)} %get-tuple-element.23.mine, f32[328,128]{1,0:T(8,128)S(1)} %collective-permute-done.8.theirs, ...), custom_call_target="tpu_custom_call" | custom-call | flops 1000000 | bytes 1000000 | tf_op jit(solution)/shard_map/apply_increments/pallas_call | solution.py:517
Async XLA Ops:
  0.0 1.3 %copy-start = (f32[2,10,16,1024]{3,2,1,0:T(8,128)S(1)}, f32[2,10,16,1024]{3,2,1,0:T(8,128)}, u32[]{:S(2)}) copy-start(f32[2,10,16,1024]{3,2,1,0:T(8,128)} %state.3) | copy-start | bytes 3932164
  1.3 1.0 %copy-start.1 = (f32[2,4,16,1024]{3,2,1,0:T(8,128)S(1)}, f32[2,4,16,1024]{3,2,1,0:T(8,128)}, u32[]{:S(2)}) copy-start(f32[2,4,16,1024]{3,2,1,0:T(8,128)} %vel.3) | copy-start | bytes 1572868
  2.4 0.8 %copy-start.2 = (s32[16,1024]{1,0:T(8,128)S(1)}, s32[16,1024]{1,0:T(8,128)}, u32[]{:S(2)}) copy-start(s32[16,1024]{1,0:T(8,128)} %band.3) | copy-start | bytes 196612
  3.2 0.7 %copy-start.3 = (s32[16]{0:T(128)S(1)}, s32[16]{0:T(128)}, u32[]{:S(2)}) copy-start(s32[16]{0:T(128)} %lat.5) | copy-start | bytes 196
  3.9 0.7 %copy-start.4 = (s32[16]{0:T(128)S(1)}, s32[16]{0:T(128)}, u32[]{:S(2)}) copy-start(s32[16]{0:T(128)} %lon.5) | copy-start | bytes 196
  4.5 0.7 %copy-start.6 = (s32[16]{0:T(128)S(1)}, s32[16]{0:T(128)}, u32[]{:S(2)}) copy-start(s32[16]{0:T(128)} %kind.3) | copy-start | bytes 196
  5.2 17.3 %copy-start.5 = (f32[4,4]{1,0:T(4,128)S(1)}, f32[4,4]{1,0:T(4,128)}, u32[]{:S(2)}) copy-start(f32[4,4]{1,0:T(4,128)} %table.1) | copy-start | bytes 196
  5.2 17.3 %copy-start.8 = (s32[16]{0:T(128)S(1)}, s32[16]{0:T(128)}, u32[]{:S(2)}) copy-start(s32[16]{0:T(128)} %layer.1) | copy-start | bytes 196
  7.8 14.6 %collective-permute-start = (f32[480,128]{1,0:T(8,128)S(1)}, f32[480,128]{1,0:T(8,128)S(1)}, u32[]{:S(2)}, u32[]{:S(2)}) collective-permute-start(f32[480,128]{1,0:T(8,128)S(1)} %get-tuple-element.15), channel_id=1, source_target_pairs={{0,1},{2,3},{1,0},{3,2},{4,5},{6,7},{5,4},{7,6},{8,9},{10,11},{9,8... | collective-permute-start | bytes 737288 | tf_op jit(solution)/shard_map/ppermute | solution.py:474
  10.0 12.4 %collective-permute-start.1 = (f32[384,128]{1,0:T(8,128)S(1)}, f32[384,128]{1,0:T(8,128)S(1)}, u32[]{:S(2)}, u32[]{:S(2)}) collective-permute-start(f32[384,128]{1,0:T(8,128)S(1)} %get-tuple-element.16), channel_id=1, source_target_pairs={{1,2},{2,1},{5,6},{6,5},{9,10},{10,9},{13,14},{14,13},{17,18},{18,... | collective-permute-start | bytes 589832 | tf_op jit(solution)/shard_map/ppermute | solution.py:475
  10.7 40.4 %copy-start.7 = (f32[2,16]{1,0:T(2,128)S(1)}, f32[2,16]{1,0:T(2,128)}, u32[]{:S(2)}) copy-start(f32[2,16]{1,0:T(2,128)} %perturb.1) | copy-start | bytes 388
  10.7 40.4 %copy-start.9 = (f32[16]{0:T(128)S(1)}, f32[16]{0:T(128)}, u32[]{:S(2)}) copy-start(f32[16]{0:T(128)} %value.1) | copy-start | bytes 196
  10.7 40.4 %copy-start.10 = (f32[16]{0:T(128)S(1)}, f32[16]{0:T(128)}, u32[]{:S(2)}) copy-start(f32[16]{0:T(128)} %error.1) | copy-start | bytes 196
  10.7 7.6 %collective-permute-start.3 = (f32[96,128]{1,0:T(8,128)S(1)}, f32[96,128]{1,0:T(8,128)S(1)}, u32[]{:S(2)}, u32[]{:S(2)}) collective-permute-start(f32[96,128]{1,0:T(8,128)S(1)} %get-tuple-element.17.rest_0_), channel_id=1, source_target_pairs={{0,3},{1,2},{2,1},{3,0},{4,7},{5,6},{6,5},{7,4},{8,11},{9,10},{10,... | collective-permute-start | bytes 147464 | tf_op jit(solution)/shard_map/ppermute | solution.py:476
  13.0 9.5 %collective-permute-start.2 = (f32[96,128]{1,0:T(8,128)S(1)}, f32[96,128]{1,0:T(8,128)S(1)}, u32[]{:S(2)}, u32[]{:S(2)}) collective-permute-start(f32[96,128]{1,0:T(8,128)S(1)} %get-tuple-element.17.rest_0_), channel_id=1, source_target_pairs={{0,2},{1,3},{2,0},{3,1},{4,6},{5,7},{6,4},{7,5},{8,10},{9,11},{10,... | collective-permute-start | bytes 147464 | tf_op jit(solution)/shard_map/ppermute | solution.py:476
  29.9 3.2 %collective-permute-start.4 = (f32[648,128]{1,0:T(8,128)S(1)}, f32[648,128]{1,0:T(8,128)S(1)}, u32[]{:S(2)}, u32[]{:S(2)}) collective-permute-start(f32[648,128]{1,0:T(8,128)S(1)} %get-tuple-element.22), channel_id=1, source_target_pairs={{0,4},{4,0},{8,12},{12,8},{16,20},{20,16},{24,28},{28,24},{1,5},{5... | collective-permute-start | bytes 995336 | tf_op jit(solution)/shard_map/ppermute | solution.py:501
  33.3 10.0 %collective-permute-start.7 = (f32[648,128]{1,0:T(8,128)S(1)}, f32[648,128]{1,0:T(8,128)S(1)}, u32[]{:S(2)}, u32[]{:S(2)}) collective-permute-start(f32[648,128]{1,0:T(8,128)S(1)} %pair_moments.1.rest_0_), channel_id=1, source_target_pairs={{0,24},{4,28},{8,16},{12,20},{16,8},{20,12},{24,0},{28,4},{1,25},{... | collective-permute-start | bytes 995336 | tf_op jit(solution)/shard_map/ppermute | solution.py:508
  35.5 15.6 %collective-permute-start.6 = (f32[648,128]{1,0:T(8,128)S(1)}, f32[648,128]{1,0:T(8,128)S(1)}, u32[]{:S(2)}, u32[]{:S(2)}) collective-permute-start(f32[648,128]{1,0:T(8,128)S(1)} %pair_moments.1.rest_0_), channel_id=1, source_target_pairs={{0,16},{4,20},{8,24},{12,28},{16,0},{20,4},{24,8},{28,12},{1,17},{... | collective-permute-start | bytes 995336 | tf_op jit(solution)/shard_map/ppermute | solution.py:508
  35.7 15.3 %collective-permute-start.5 = (f32[648,128]{1,0:T(8,128)S(1)}, f32[648,128]{1,0:T(8,128)S(1)}, u32[]{:S(2)}, u32[]{:S(2)}) collective-permute-start(f32[648,128]{1,0:T(8,128)S(1)} %pair_moments.1.rest_0_), channel_id=1, source_target_pairs={{0,8},{4,12},{8,0},{12,4},{16,24},{20,28},{24,16},{28,20},{1,9},{5... | collective-permute-start | bytes 995336 | tf_op jit(solution)/shard_map/ppermute | solution.py:508
  53.3 1.7 %collective-permute-start.8 = (f32[328,128]{1,0:T(8,128)S(1)}, f32[328,128]{1,0:T(8,128)S(1)}, u32[]{:S(2)}, u32[]{:S(2)}) collective-permute-start(f32[328,128]{1,0:T(8,128)S(1)} %get-tuple-element.23.mine), channel_id=1, source_target_pairs={{0,4},{4,0},{8,12},{12,8},{16,20},{20,16},{24,28},{28,24},{1,5},{5... | collective-permute-start | bytes 503816 | tf_op jit(solution)/shard_map/ppermute | solution.py:516

commit v2 on v1

v2 whole, which is shorter than its diff:
```python
import functools

import jax
import jax.numpy as jnp
from jax import lax
from jax.experimental import pallas as pl
from jax.experimental.pallas import tpu as pltpu
from jax.sharding import PartitionSpec as P

NLAYER = 2
NCLASS = 4
KINDS = NCLASS + 1
FIELDS = NLAYER * KINDS
WINDOW_HEIGHT = 4
WINDOW_WIDTH = 128
DIFFUSION = 0.08
DEPOSIT = 0.5
CAP = 16

LANES = 128
PAD = 8
GROUP = 8
NEAR_ROWS = 48
EXACT = lax.Precision.HIGHEST
MIB = 1024 * 1024

SMEM = pl.BlockSpec(memory_space=pltpu.SMEM)
VMEM = pl.BlockSpec(memory_space=pltpu.VMEM)
HBM = pl.BlockSpec(memory_space=pltpu.HBM)


def call(kernel, name, in_specs, outs, scratch=(), flops=1000, aliases=None, limit=40):
    return pl.pallas_call(
        kernel,
        name=name,
        in_specs=in_specs,
        out_specs=[VMEM] * len(outs),
        out_shape=[jax.ShapeDtypeStruct(shape, jnp.float32) for shape in outs],
        scratch_shapes=list(scratch),
        input_output_aliases=aliases or {},
        compiler_params=pltpu.CompilerParams(vmem_limit_bytes=limit * MIB),
        cost_estimate=pl.CostEstimate(flops=flops, bytes_accessed=1000, transcendentals=0),
    )


def held(*arrays):
    return [pltpu.with_memory_space_constraint(array, pltpu.HBM) for array in arrays]


def lane_index(rows=8):
    return lax.broadcasted_iota(jnp.int32, (rows, LANES), 1)


def row_index(rows=8):
    return lax.broadcasted_iota(jnp.int32, (rows, LANES), 0)


def spread(ref, group, rows=8):
    index = lane_index(rows) // group
    total = jnp.zeros((rows, LANES), ref.dtype)
    for j in range(ref.shape[0]):
        total = jnp.where(index == j, ref[j], total)
    return total


def find_slots(lat, slots, first, rows, cap):
    for s in range(cap + 1):
        slots[s] = 0
    count = jnp.int32(0)
    for j in range(lat.shape[0]):
        start = lat[j] - WINDOW_HEIGHT // 2 - first
        slots[jnp.minimum(count, cap)] = j
        count = count + ((start < rows) & (start + WINDOW_HEIGHT > 0)).astype(jnp.int32)
    return jnp.minimum(count, cap)


def window(lat, lon, j, first, rows, tiles):
    row = jnp.clip(lat[j] - WINDOW_HEIGHT // 2 - first, -WINDOW_HEIGHT, rows) + PAD
    left = lon[j] - WINDOW_WIDTH // 2
    block = left // LANES
    return row, block, jnp.minimum(block + 1, tiles - 1), left % LANES


def coefficients(u, w):
    return (
        (1.0 - 4.0 * DIFFUSION) - (jnp.abs(u) + jnp.abs(w)),
        jnp.maximum(u, 0.0) + DIFFUSION,
        DIFFUSION - jnp.minimum(u, 0.0),
        jnp.maximum(w, 0.0) + DIFFUSION,
        DIFFUSION - jnp.minimum(w, 0.0),
    )


def stencil(coef, centre, up, down, left, right):
    return (coef[0] * centre + coef[1] * up) + (coef[2] * down + coef[3] * left) + coef[4] * right


def choose(values, pick):
    total = jnp.zeros((values.shape[0], LANES), jnp.float32)
    for _ in range(3):
        part = values.astype(jnp.bfloat16)
        total = total + jnp.dot(part, pick, preferred_element_type=jnp.float32)
        values = values - part.astype(jnp.float32)
    return total


def lane_tiles(source, target, members, tiles, each, rows, shift):
    return [
        (
            source.at[m, :, :, pl.ds(i * LANES, LANES)],
            target.at[pl.ds(m * each, each), i + shift, pl.ds(PAD, rows), :],
        )
        for m in range(members)
        for i in range(tiles)
    ]


def start_copies(moves, sems):
    copies = [pltpu.make_async_copy(src, dst, sems.at[n]) for n, (src, dst) in enumerate(moves)]
    for copy in copies:
        copy.start()
    return copies


def pack_kernel(lat_hbm, lon_hbm, kind_hbm, state_hbm, vel_hbm, band_hbm, out_a, out_b, near, s0, vs, bs, lat, lon, kind, sems):
    members, _, rows, width = state_hbm.shape
    tiles = width // LANES
    fields, parts = members * FIELDS, members * 2 * NLAYER
    moves = lane_tiles(state_hbm, s0, members, tiles, FIELDS, rows, 0)
    moves += lane_tiles(vel_hbm, vs, members, tiles, 2 * NLAYER, rows, 0)
    moves += [(band_hbm.at[:, pl.ds(i * LANES, LANES)], bs.at[i, pl.ds(PAD, rows), :]) for i in range(tiles)]
    moves += [(lat_hbm, lat), (lon_hbm, lon), (kind_hbm, kind)]
    copies = start_copies(moves, sems)
    tile = lax.axis_index("tile")
    even = tile % 2 == 0
    first = tile * rows
    zero = jnp.zeros((PAD, LANES), jnp.float32)
    for ref in (s0, vs, bs):
        for n in range(ref.shape[0]) if ref is not bs else (None,):
            for i in range(tiles):
                lead = (i,) if n is None else (n, i)
                ref[lead + (slice(0, PAD),)] = zero.astype(ref.dtype)
                ref[lead + (slice(PAD + rows, None),)] = zero.astype(ref.dtype)
    for copy in copies:
        copy.wait()

    def edge(out, q_first, v_at):
        for i in range(tiles):
            for c in range(parts):
                to = NEAR_ROWS + i * parts + c
                out[to : to + 1, :] = vs[c, i, v_at : v_at + 1, :]
            for f in range(fields):
                to = NEAR_ROWS + tiles * parts + (i * fields + f) * 2
                out[to : to + 2, :] = s0[f, i, q_first : q_first + 2, :]

    top, bottom = PAD, PAD + rows

    @pl.when(even)
    def _():
        edge(out_a, bottom - 2, bottom - 1)
        edge(out_b, top, top)

    @pl.when(jnp.logical_not(even))
    def _():
        edge(out_a, top, top)
        edge(out_b, bottom - 2, bottom - 1)

    lane = lane_index()
    row = row_index()
    blank = jnp.zeros((8, LANES), jnp.float32)
    pairs = members * NLAYER
    qs, us, ws, bins = [blank] * pairs, [blank] * pairs, [blank] * pairs, blank
    for j in range(lat.shape[0]):
        start = jnp.clip(lat[j] - 2 - first, -PAD, rows) + PAD
        left = lon[j] - 2
        block, shift = left // LANES, left % LANES
        after = jnp.minimum(block + 1, tiles - 1)
        turn = (GROUP * j - shift + LANES) % LANES
        here = lane >= shift
        mine = (lane // GROUP) == j

        def fetch(ref, old, *lead):
            both = jnp.where(
                here, ref[lead + (block, pl.ds(start, 8))], ref[lead + (after, pl.ds(start, 8))]
            )
            return jnp.where(mine, pltpu.roll(both.astype(jnp.float32), turn, 1), old)

        for m in range(members):
            for l in range(NLAYER):
                s = m * NLAYER + l
                qs[s] = fetch(s0, qs[s], m * FIELDS + l * KINDS + kind[j])
                us[s] = fetch(vs, us[s], 2 * s)
                ws[s] = fetch(vs, ws[s], 2 * s + 1)
        bins = fetch(bs, bins)

    blocks = [jnp.where(row < 5, q, pltpu.roll(u, 4, 0)) for q, u in zip(qs, us)]
    for m in range(members):
        w = jnp.where(row < 4, ws[2 * m], pltpu.roll(ws[2 * m + 1], 4, 0))
        blocks.append(jnp.where(row == 0, pltpu.roll(bins, 6, 0), w))
    for n, block in enumerate(blocks):
        for out in (near, out_a, out_b):
            out[8 * n : 8 * n + 8, :] = block


def combine_kernel(near, from_a, _, out):
    out[...] = near[...] + from_a[:NEAR_ROWS, :]


def advance(source, f, i, r, coef, lane):
    centre = source[f, i + 1, r : r + 8, :]
    up = source[f, i + 1, r - 1 : r + 7, :]
    down = source[f, i + 1, r + 1 : r + 9, :]
    left, right = sides_of(source[f, i, r : r + 8, :], centre, source[f, i + 2, r : r + 8, :], lane)
    return stencil(coef, centre, up, down, left, right)


def sides_of(before, centre, after, lane):
    left = pltpu.roll(jnp.where(lane == LANES - 1, before, centre), 1, 1)
    right = pltpu.roll(jnp.where(lane == 0, after, centre), LANES - 1, 1)
    return left, right


def settle(a, b, bins, table, k):
    if k == 0:
        return a, b
    rate = jnp.full(a.shape, table[0, k - 1], jnp.float32)
    for level in range(1, table.shape[0]):
        rate = jnp.where(bins == level, table[level, k - 1], rate)
    settled = rate * a
    return a - settled, b + settled - DEPOSIT * rate * b


def interior_kernel(table_hbm, state, vel, band_hbm, padded, own_edge, once_edge, vel_edge, bin_edge, s0, s1, vs, band, table, sems):
    members, _, rows, width = state.shape
    tiles = width // LANES
    fields, parts = members * FIELDS, members * 2 * NLAYER
    moves = lane_tiles(vel, vs, members, tiles, 2 * NLAYER, rows, 0)
    moves += lane_tiles(state, s0, members, tiles, FIELDS, rows, 1)
    moves += [(band_hbm, band), (table_hbm, table)]
    copies = start_copies(moves, sems)
    zero = jnp.zeros((rows + 2 * PAD, LANES), jnp.float32)
    lane = lane_index()
    for f in range(fields):
        for buffer in (s0, s1):
            buffer[f, 0, :, :] = zero
            buffer[f, tiles + 1, :, :] = zero
    for copy in copies:
        copy.wait()

    def first_step(t, carry):
        ml, i = t // tiles, t % tiles
        for r in range(PAD, PAD + rows, 8):
            coef = coefficients(vs[2 * ml, i, r : r + 8, :], vs[2 * ml + 1, i, r : r + 8, :])
            for k in range(KINDS):
                s1[ml * KINDS + k, i + 1, r : r + 8, :] = advance(s0, ml * KINDS + k, i, r, coef, lane)
        return carry

    for t in range(members * NLAYER * tiles):
        first_step(t, 0)

    def second_step(t, carry):
        m, i = t // tiles, t % tiles
        lanes = pl.ds(i * LANES, LANES)
        for r in range(PAD, PAD + rows, 8):
            coefs = []
            for l in range(NLAYER):
                mc = (m * NLAYER + l) * 2
                coefs.append(coefficients(vs[mc, i, r : r + 8, :], vs[mc + 1, i, r : r + 8, :]))
            bins = band[r - PAD : r - PAD + 8, lanes]
            for k in range(KINDS):
                upper = m * FIELDS + k
                lower = upper + KINDS
                a = advance(s1, upper, i, r, coefs[0], lane)
                b = advance(s1, lower, i, r, coefs[1], lane)
                a, b = settle(a, b, bins, table, k)
                padded[upper, i, r : r + 8, :] = a
                padded[lower, i, r : r + 8, :] = b
        return carry

    for t in range(members * tiles):
        second_step(t, 0)

    top, bottom = PAD, PAD + rows
    half = row_index() < 4

    def halves(ref, lead, low, high):
        return jnp.where(half, ref[lead + (slice(low, low + 8), slice(None))], ref[lead + (slice(high - 4, high + 4), slice(None))])

    for i in range(tiles):
        for f in range(fields):
            padded[f, i, :PAD, :] = zero[:PAD]
            padded[f, i, PAD + rows :, :] = zero[:PAD]
            own_edge[f, i, :, :] = halves(s0, (f, i + 1), top - 2, bottom - 2)
            once_edge[f, i, :, :] = halves(s1, (f, i + 1), top - 1, bottom - 3)
        for c in range(parts):
            vel_edge[0, c, i, :, :] = halves(vs, (c, i), top - 2, bottom - 2)
            vel_edge[1, c, i, :, :] = halves(vs, (c, i), top - 1, bottom - 3)
        upper = band[0:8, i * LANES : (i + 1) * LANES].astype(jnp.float32)
        lower = band[rows - 8 : rows, i * LANES : (i + 1) * LANES].astype(jnp.float32)
        bin_edge[i, :, :] = jnp.where(half, pltpu.roll(upper, 1, 0), pltpu.roll(lower, 7, 0))


def observe_kernel(members, layer, kind, table, *rest):
    parts, out = rest[:-1], rest[-1]
    pairs = members * NLAYER
    blocks = []
    for n in range(pairs + members):
        block = parts[0][8 * n : 8 * n + 8, :]
        for more in parts[1:]:
            block = block + more[8 * n : 8 * n + 8, :]
        blocks.append(block)
    bins = jnp.broadcast_to(blocks[pairs][:1], (8, LANES))
    kinds = spread(kind, GROUP)
    layers = spread(layer, GROUP)
    rate = jnp.zeros((8, LANES), jnp.float32)
    for level in range(table.shape[0]):
        here = jnp.abs(bins - level) < 0.5
        for k in range(NCLASS):
            rate = jnp.where(here & (kinds == k + 1), table[level, k], rate)
    row = row_index()

    def step(q, coef):
        return stencil(
            coef,
            q,
            pltpu.roll(q, 1, 0),
            pltpu.roll(q, 7, 0),
            pltpu.roll(q, 1, 1),
            pltpu.roll(q, LANES - 1, 1),
        )

    seen = jnp.zeros((8, LANES), jnp.float32)
    for m in range(members):
        values = []
        for l in range(NLAYER):
            q = blocks[m * NLAYER + l]
            u = pltpu.roll(q, 4, 0)
            w = blocks[pairs + m]
            coef = coefficients(u, w if l == 0 else pltpu.roll(w, 4, 0))
            values.append(step(step(q, coef), coef))
        a, b = values
        settled = rate * a
        value = jnp.where(layers == 0, a - settled, b + settled - DEPOSIT * rate * b)
        seen = jnp.where(row == m, pltpu.roll(value, (m - 2) % 8, 0), seen)
    squeeze = (
        lax.broadcasted_iota(jnp.int32, (LANES, LANES), 0)
        == lax.broadcasted_iota(jnp.int32, (LANES, LANES), 1) * GROUP + 2
    ).astype(jnp.bfloat16)
    out[...] = choose(seen, squeeze)


def join_kernel(members, obs, got, out):
    out[...] = jnp.where(row_index() < members, obs[...], pltpu.roll(got[...], members, 0))


def edge_kernel(table, own_edge, once_edge, vel_edge, bin_edge, from_a, from_b, inner, near, padded, e0, e1, up, down):
    fields, tiles, padded_rows, _ = padded.shape
    rows = padded_rows - 2 * PAD
    members = fields // FIELDS
    parts = members * 2 * NLAYER
    tile = lax.axis_index("tile")
    count_tiles = lax.axis_size("tile")
    even = tile % 2 == 0
    sent = from_a.shape[0]

    @pl.when(even)
    def _():
        down[:sent, :] = from_a[...]
        up[:sent, :] = from_b[...]

    @pl.when(jnp.logical_not(even))
    def _():
        up[:sent, :] = from_a[...]
        down[:sent, :] = from_b[...]

    lane = lane_index()
    row = row_index()
    zero = jnp.zeros((8, LANES), jnp.float32)
    v_base = NEAR_ROWS
    q_base = NEAR_ROWS + tiles * parts
    for f in range(fields):
        for buffer in (e0, e1):
            buffer[f, 0, :, :] = zero
            buffer[f, tiles + 1, :, :] = zero

    def gather(i, carry):
        for f in range(fields):
            at = q_base + (i * fields + f) * 2
            q = jnp.where(row < 2, up[pl.ds(at, 8), :], own_edge[f, i, :, :])
            e0[f, i + 1, :, :] = jnp.where(row > 5, down[pl.ds(at - 6, 8), :], q)
        return carry

    for i in range(tiles):
        gather(i, 0)
    outside = ((row == 0) & (tile == 0)) | ((row == 7) & (tile == count_tiles - 1))

    def first_step(t, carry):
        ml, i = t // tiles, t % tiles
        flow = []
        for c in range(2):
            at = v_base + i * parts + 2 * ml + c
            v = jnp.where(row == 1, up[pl.ds(at - 1, 8), :], vel_edge[0, 2 * ml + c, i, :, :])
            flow.append(jnp.where(row == 6, down[pl.ds(at - 6, 8), :], v))
        coef = coefficients(*flow)
        for k in range(KINDS):
            f = ml * KINDS + k
            centre = e0[f, i + 1, :, :]
            left, right = sides_of(e0[f, i, :, :], centre, e0[f, i + 2, :, :], lane)
            q = stencil(coef, centre, pltpu.roll(centre, 1, 0), pltpu.roll(centre, 7, 0), left, right)
            q = jnp.where(row < 2, pltpu.roll(q, 7, 0), jnp.where(row > 5, pltpu.roll(q, 1, 0), once_edge[f, i, :, :]))
            e1[f, i + 1, :, :] = jnp.where(outside, 0.0, q)
        return carry

    for t in range(members * NLAYER * tiles):
        first_step(t, 0)

    def second_step(t, carry):
        m, i = t // tiles, t % tiles
        bins = bin_edge[i, :, :].astype(jnp.int32)
        values = []
        for l in range(NLAYER):
            mc = (m * NLAYER + l) * 2
            coef = coefficients(vel_edge[1, mc, i, :, :], vel_edge[1, mc + 1, i, :, :])
            for k in range(KINDS):
                f = m * FIELDS + l * KINDS + k
                centre = e1[f, i + 1, :, :]
                left, right = sides_of(e1[f, i, :, :], centre, e1[f, i + 2, :, :], lane)
                values.append(
                    stencil(coef, centre, pltpu.roll(centre, 1, 0), pltpu.roll(centre, 7, 0), left, right)
                )
        for k in range(KINDS):
            for l, q in enumerate(settle(values[k], values[KINDS + k], bins, table, k)):
                f = m * FIELDS + l * KINDS + k
                padded[f, i, PAD : PAD + 2, :] = q[1:3]
                padded[f, i, PAD + rows - 2 : PAD + rows, :] = q[5:7]
        return carry

    for t in range(members * tiles):
        second_step(t, 0)


def cut_kernel(cap, lat, lon, padded, _, own, send, sel, slots):
    fields, tiles, padded_rows, _ = padded.shape
    rows = padded_rows - 2 * PAD
    members = fields // FIELDS
    core = lax.axis_index("member") % 2
    first = lax.axis_index("tile") * rows
    lane = lane_index()
    size = cap * WINDOW_HEIGHT
    count = find_slots(lat, slots, first, rows, cap)
    for s in range(cap):
        sel[s * 4 : s * 4 + 4, :] = (lane[:4] == slots[s]).astype(jnp.float32)

    def cut(layer_of_own):
        def one(s, carry):
            row, block, after, shift = window(lat, lon, slots[s], first, rows, tiles)
            here = lane >= shift
            for l, target in ((layer_of_own, own), (1 - layer_of_own, send)):
                for m in range(members):
                    for k in range(KINDS):
                        f = m * FIELDS + l * KINDS + k
                        both = jnp.where(
                            here, padded[f, block, pl.ds(row, 8), :], padded[f, after, pl.ds(row, 8), :]
                        )
                        patch = pltpu.roll(both, (LANES - shift) % LANES, 1)
                        target[pl.ds((m * KINDS + k) * size + s * 4, 4), :] = patch[:4]
            return carry

        lax.fori_loop(0, count, one, 0)

    for c in range(2):
        pl.when(core == c)(functools.partial(cut, c))


def moment_kernel(cap, members, chips, own, got, sel, *rest):
    seens, (cross, everyone) = rest[:chips], rest[chips:]
    size = cap * WINDOW_HEIGHT
    part = KINDS * size
    both = 2 * members
    for c, seen in enumerate(seens):
        everyone[c * both : (c + 1) * both, :] = seen[:both, :]
    mean = jnp.sum(everyone[...], axis=0, keepdims=True) / (chips * both)
    sources = [(own, m, m) for m in range(members)] + [(got, m, members + m) for m in range(members)]
    weight = [
        jnp.sum(sel[...] * (everyone[o : o + 1, :] - mean), axis=1, keepdims=True) for _, _, o in sources
    ]
    for k in range(KINDS):
        total = jnp.zeros((size, LANES), jnp.float32)
        for (ref, m, _), o in zip(sources, weight):
            total = total + ref[m * part + k * size : m * part + (k + 1) * size, :] * o
        cross[k * size : (k + 1) * size, :] = total


def weight_kernel(value, error, perturb, everyone_ref, weights):
    members, observations = perturb.shape
    everyone = everyone_ref[...]
    number = everyone.shape[0]
    anomaly = everyone - jnp.sum(everyone, axis=0, keepdims=True) / number
    over = (((0,), (0,)), ((), ()))
    cov = lax.dot_general(anomaly, anomaly, over, precision=EXACT, preferred_element_type=jnp.float32)
    row16 = row_index(observations)
    lane16 = lane_index(observations)
    errors = spread(error, 1)
    innovation = spread(value, 1)[:members] - everyone[:members]
    noise = jnp.concatenate(
        [perturb[...], jnp.zeros((members, LANES - observations), jnp.float32)], axis=1
    )
    innovation = innovation + jnp.sqrt(errors[:members]) * noise
    place = (lane_index(members) == row_index(members) + observations).astype(jnp.float32)
    sides = lax.dot_general(innovation, place, over, precision=EXACT, preferred_element_type=jnp.float32)
    system = jnp.where(lane16 < observations, cov[:observations] / (number - 1), sides[:observations])
    system = system + jnp.where(lane16 == row16, jnp.broadcast_to(errors[:1], row16.shape), 0.0)
    for k in range(observations):
        pivot = system[k : k + 1, :] / system[k : k + 1, k : k + 1]
        system = jnp.where(row16 == k, pivot, system - system[:, k : k + 1] * pivot)
    for m in range(members):
        weights[m, :, :] = jnp.broadcast_to(
            system[:, observations + m : observations + m + 1], (observations, LANES)
        )


def merge_kernel(cap, number, _, *rest):
    parts, gain = rest[:-1], rest[-1]
    size = cap * WINDOW_HEIGHT
    row = (row_index(size) % WINDOW_HEIGHT).astype(jnp.float32)
    column = lane_index(size).astype(jnp.float32)
    row = (row + 0.5 - WINDOW_HEIGHT / 2) / (WINDOW_HEIGHT / 2)
    column = (column + 0.5 - WINDOW_WIDTH / 2) / (WINDOW_WIDTH / 2)
    taper = (1.0 - row * row) * (1.0 - column * column) / (number - 1)
    for k in range(KINDS):
        total = parts[0][k * size : (k + 1) * size, :]
        for more in parts[1:]:
            total = total + more[k * size : (k + 1) * size, :]
        gain[k * size : (k + 1) * size, :] = taper * total
    gain[KINDS * size :, :] = jnp.zeros((8, LANES), jnp.float32)


def apply_kernel(cap, lat, lon, field, mine, theirs, weights, out, work, slots):
    members, _, rows, width = out.shape
    tiles = width // LANES
    size = cap * WINDOW_HEIGHT
    first = lax.axis_index("tile") * rows
    core = lax.axis_index("member") % 2
    count = find_slots(lat, slots, first, rows, cap)
    lane = lane_index()
    patch_row = row_index() < WINDOW_HEIGHT

    def add(layer_of_own):
        def one(s, carry):
            j = slots[s]
            row, block, after, shift = window(lat, lon, j, first, rows, tiles)
            here = patch_row & (lane >= shift)
            there = patch_row & (lane < shift)
            w = [weights[m, pl.ds(j, 1), :] for m in range(members)]
            for l, source in ((layer_of_own, mine), (1 - layer_of_own, theirs)):
                for k in range(KINDS):
                    gain = pltpu.roll(source[pl.ds(k * size + s * 4, 8), :], shift, 1)
                    near = jnp.where(here, gain, 0.0)
                    far = jnp.where(there, gain, 0.0)
                    for m in range(members):
                        f = m * FIELDS + l * KINDS + k
                        work[f, block, pl.ds(row, 8), :] += near * w[m]
                        work[f, after, pl.ds(row, 8), :] += far * w[m]
            return carry

        lax.fori_loop(0, count, one, 0)

    for c in range(2):
        pl.when(core == c)(functools.partial(add, c))
    for f in range(members * FIELDS):
        for i in range(tiles):
            out[f // FIELDS, f % FIELDS, :, i * LANES : (i + 1) * LANES] = work[f, i, PAD : PAD + rows, :]


def partner(size, k):
    if size & (size - 1) == 0:
        return [(i, i ^ k) for i in range(size)]
    return [(i, (i + k) % size) for i in range(size)]


def analyse(cap, shape, field, near, lat, lon, layer, kind, table, value, error, perturb):
    members, _, rows, width = shape
    row_tiles = lax.axis_size("tile")
    devices = lax.axis_size("member")
    chips = devices // 2
    both = 2 * members
    observations = lat.shape[0]
    size = cap * WINDOW_HEIGHT
    part = KINDS * size
    other_core = [(i, i ^ 1) for i in range(devices)]
    slots = pltpu.SMEM((cap + 1,), jnp.int32)
    (obs,) = call(
        functools.partial(observe_kernel, members),
        "observe",
        [SMEM] * 3 + [VMEM] * len(near),
        [(8, LANES)],
    )(layer, kind, table, *near)
    got_obs = lax.ppermute(obs, "member", other_core)
    own, send, sel = call(
        functools.partial(cut_kernel, cap),
        "cut_patches",
        [SMEM] * 2 + [VMEM] * 2,
        [(members * part, LANES), (members * part, LANES), (size, LANES)],
        [slots],
    )(lat, lon, field, obs)
    got = lax.ppermute(send, "member", other_core)
    (seen,) = call(functools.partial(join_kernel, members), "join_observed", [VMEM] * 2, [(8, LANES)])(obs, got_obs)
    seens = [seen] + [lax.ppermute(seen, "member", partner(devices, 2 * k)) for k in range(1, chips)]
    cross, everyone = call(
        functools.partial(moment_kernel, cap, members, chips),
        "moments",
        [VMEM] * (3 + chips),
        [(part, LANES), (chips * both, LANES)],
    )(own, got, sel, *seens)
    crosses = [cross] + [lax.ppermute(cross, "member", partner(devices, 2 * k)) for k in range(1, chips)]
    (weights,) = call(
        weight_kernel,
        "solve_weights",
        [SMEM] * 2 + [VMEM] * 2,
        [(members, observations, LANES)],
    )(value, error, perturb, everyone)
    (mine,) = call(
        functools.partial(merge_kernel, cap, chips * both),
        "merge_moments",
        [VMEM] * (1 + chips),
        [(part + 8, LANES)],
    )(weights, *crosses)
    theirs = lax.ppermute(mine, "member", other_core)
    analysed, _ = call(
        functools.partial(apply_kernel, cap),
        "apply_increments",
        [SMEM] * 2 + [VMEM] * 4,
        [shape, field.shape],
        [slots],
        aliases={2: 1},
    )(lat, lon, field, mine, theirs, weights)
    return analysed


def body(state, vel, band, table, lat, lon, layer, kind, value, error, perturb):
    members, _, rows, width = state.shape
    tiles = width // LANES
    row_tiles = lax.axis_size("tile")
    fields, parts = members * FIELDS, members * 2 * NLAYER
    padded_rows = rows + 2 * PAD
    message = (NEAR_ROWS + tiles * (parts + 2 * fields), LANES)
    out_a, out_b, near = call(
        pack_kernel,
        "pack_edges",
        [HBM] * 6,
        [message, message, (NEAR_ROWS, LANES)],
        [
            pltpu.VMEM((fields, tiles, padded_rows, LANES), jnp.float32),
            pltpu.VMEM((parts, tiles, padded_rows, LANES), jnp.float32),
            pltpu.VMEM((tiles, padded_rows, LANES), jnp.int32),
            pltpu.SMEM(lat.shape, jnp.int32),
            pltpu.SMEM(lon.shape, jnp.int32),
            pltpu.SMEM(kind.shape, jnp.int32),
            pltpu.SemaphoreType.DMA((4 * members * tiles + tiles + 3,)),
        ],
    )(*held(lat, lon, kind, state, vel, band))
    pairs_a = [(i, i + 1) for i in range(0, row_tiles - 1, 2)]
    pairs_b = [(i, i + 1) for i in range(1, row_tiles - 1, 2)]
    from_a = lax.ppermute(out_a, "tile", pairs_a + [(j, i) for i, j in pairs_a])
    from_b = lax.ppermute(out_b, "tile", pairs_b + [(j, i) for i, j in pairs_b])
    wide = pltpu.VMEM((fields, tiles + 2, padded_rows, LANES), jnp.float32)
    inner, own_edge, once_edge, vel_edge, bin_edge = call(
        interior_kernel,
        "interior_rows",
        [HBM] * 4,
        [
            (fields, tiles, padded_rows, LANES),
            (fields, tiles, 8, LANES),
            (fields, tiles, 8, LANES),
            (2, parts, tiles, 8, LANES),
            (tiles, 8, LANES),
        ],
        [
            wide,
            wide,
            pltpu.VMEM((parts, tiles, padded_rows, LANES), jnp.float32),
            pltpu.VMEM(band.shape, jnp.int32),
            pltpu.SMEM(table.shape, jnp.float32),
            pltpu.SemaphoreType.DMA((2 * members * tiles + 2,)),
        ],
        flops=20000000,
    )(*held(table, state, vel, band))
    if row_tiles & (row_tiles - 1) == 0:
        (near,) = call(combine_kernel, "combine_near", [VMEM] * 3, [(NEAR_ROWS, LANES)])(near, from_a, bin_edge)
        step = 2
        while step < row_tiles // 2:
            near = near + lax.ppermute(near, "tile", partner(row_tiles, step))
            step *= 2
        nears = [near] + ([lax.ppermute(near, "tile", partner(row_tiles, step))] if step < row_tiles else [])
    else:
        nears = [lax.psum(near, "tile")]
    narrow = pltpu.VMEM((fields, tiles + 2, 8, LANES), jnp.float32)
    halo = pltpu.VMEM((message[0] + 8, LANES), jnp.float32)
    (field,) = call(
        edge_kernel,
        "edge_rows",
        [SMEM] + [VMEM] * 8,
        [(fields, tiles, padded_rows, LANES)],
        [narrow, narrow, halo, halo],
        aliases={7: 0},
    )(table, own_edge, once_edge, vel_edge, bin_edge, from_a, from_b, inner, near)
    return analyse(CAP, state.shape, field, nears, lat, lon, layer, kind, table, value, error, perturb)


def solution(mesh):
    placed = (
        P("member", None, "tile", None),
        P("member", None, "tile", None),
        P("tile", None),
        P(),
        P(),
        P(),
        P(),
        P(),
        P(),
        P(),
        P("member", None),
    )
    return jax.shard_map(
        body, mesh=mesh, in_specs=placed, out_specs=P("member", None, "tile", None), check_vma=False
    )
```

time: 57.9 us -> 41 us (0.71)
  the two profiles are of different devices: /device:TPU:1 before, /device:TPU:9 now
where the time goes in v2:
time: 41 us; the launch traced here: 40.9 us
  Pallas kernels  15.3 us (37%)
  starting transfers between devices  14.4 us (35%)
  waiting for transfers between devices  11.1 us (27%)
    ppermute x3, waiting for transfers between devices, analyse(): lax.ppermute(cross, 'member', partner(devices, 2 * k))  4.71 us
    ppermute x1, starting transfers between devices, body(): from_b = lax.ppermute(out_b, 'tile', pairs_b + [(j, i) for i, j in pairs_b])  4.48 us
    pallas_call x1, Pallas kernels, body(): call(interior_kernel, 'interior_rows', [HBM] * 4, [(fields, tiles, padded...  4.17 us
    pallas_call x1, Pallas kernels, body(): call(pack_kernel, 'pack_edges', [HBM] * 6, [message, message, (NEAR_ROWS,...  2.72 us
    ppermute x3, starting transfers between devices, analyse(): lax.ppermute(cross, 'member', partner(devices, 2 * k))  2.71 us
    ppermute x3, starting transfers between devices, analyse(): lax.ppermute(seen, 'member', partner(devices, 2 * k))  2.65 us
    pallas_call x1, Pallas kernels, analyse(): call(functools.partial(apply_kernel, cap), 'apply_increments', [SMEM] * 2...  2.57 us
    ppermute x1, starting transfers between devices, analyse(): got = lax.ppermute(send, 'member', other_core)  2.45 us
  transfers between devices with their start and end apart: 12, of which 9 were waited for; matrix products, arithmetic and copies ran while one was open for 0% of the time, Pallas kernels for 19%

profile of v2, /device:TPU:9, one launch (start us, length us, event | category | flops | bytes accessed | tf_op | source)
XLA Modules:
  0.0 40.9 jit_solution(11113755494635704646)
XLA Ops:
  0.0 0.0 copy-start
  0.0 2.7 %pack_edges.1 = (f32[432,128]{1,0:T(8,128)S(1)}, f32[432,128]{1,0:T(8,128)S(1)}, f32[48,128]{1,0:T(8,128)S(1)}) custom-call(s32[16]{0:T(128)} %lat.3, s32[16]{0:T(128)} %lon.3, s32[16]{0:T(128)} %kind.1, f32[2,10,16,1024]{3,2,1,0:T(8,128)} %state_hbm.1, f32[2,4,16,1024]{3,2,1,0:T(8,128)} %vel_hbm.1, s32[16,1024]{1,0:T(8,128)} %band_hbm.3), custom_call_target="tpu_custom_call" | custom-call | flops 1000 | bytes 1000 | tf_op jit(solution)/shard_map/pack_edges/pallas_call | solution.py:647
  2.7 0.1 collective-permute-start
  2.8 4.5 %collective-permute-start.1 = (f32[432,128]{1,0:T(8,128)S(1)}, f32[432,128]{1,0:T(8,128)S(1)}, u32[]{:S(2)}, u32[]{:S(2)}) collective-permute-start(f32[432,128]{1,0:T(8,128)S(1)} %get-tuple-element.24), channel_id=1, source_target_pairs={{1,2},{2,1},{5,6},{6,5},{9,10},{10,9},{13,14},{14,13},{17,18},{18,... | collective-permute-start | bytes 663560 | tf_op jit(solution)/shard_map/ppermute | solution.py:665
  7.3 4.2 %interior_rows.1 = (f32[20,8,32,128]{3,2,1,0:T(8,128)S(1)}, f32[20,8,8,128]{3,2,1,0:T(8,128)S(1)}, f32[20,8,8,128]{3,2,1,0:T(8,128)S(1)}, f32[2,8,8,8,128]{4,3,2,1,0:T(8,128)S(1)}, f32[8,8,128]{2,1,0:T(8,128)S(1)}) custom-call(f32[4,4]{1,0:T(4,128)} %table.3, f32[2,10,16,1024]{3,2,1,0:T(8,128)} %state_hbm.1, f32[2,4,16,1024]{3,2,1,0:T(8,128)} %vel_hbm.1, ...), custom_call_target="tpu_custom_call" | custom-call | flops 20000000 | bytes 1000 | tf_op jit(solution)/shard_map/interior_rows/pallas_call | solution.py:667
  11.5 0.0 collective-permute-done.from_a
  11.5 0.1 collective-permute-start.2
  11.6 0.5 %collective-permute-done.1.from_b = f32[432,128]{1,0:T(8,128)S(1)} collective-permute-done((f32[432,128]{1,0:T(8,128)S(1)}, f32[432,128]{1,0:T(8,128)S(1)}, u32[]{:S(2)}, u32[]{:S(2)}) %collective-permute-start.1) | collective-permute-done | bytes 221216 | tf_op jit(solution)/shard_map/ppermute | solution.py:665
  12.1 0.0 copy-done
  12.1 0.0 copy-start.3
  12.1 0.0 copy-start.5
  12.1 0.0 copy-start.1
  12.1 0.0 copy-start.2
  12.1 1.6 %edge_rows.1.padded.field = f32[20,8,32,128]{3,2,1,0:T(8,128)S(1)} custom-call(f32[4,4]{1,0:T(4,128)S(1)} %copy-done, f32[20,8,8,128]{3,2,1,0:T(8,128)S(1)} %get-tuple-element.19.own_edge, f32[20,8,8,128]{3,2,1,0:T(8,128)S(1)} %get-tuple-element.20.once_edge, f32[2,8,8,8,128]{4,3,2,1,0:T(8,128)S(1)} %get-tuple-element.21.vel_edge, ...), custom_call_target="tpu_custom_call", output_to_operand_aliasing={{}: (7, {})} | custom-call | flops 1000 | bytes 1000 | tf_op jit(solution)/shard_map/edge_rows/pallas_call | solution.py:699
  13.7 0.0 copy-start.4
  13.7 0.0 copy-start.6
  13.7 0.0 copy-start.7
  13.8 1.4 %collective-permute-done.2.rest_1_ = f32[48,128]{1,0:T(8,128)S(1)} collective-permute-done((f32[48,128]{1,0:T(8,128)S(1)}, f32[48,128]{1,0:T(8,128)S(1)}, u32[]{:S(2)}, u32[]{:S(2)}) %collective-permute-start.2) | collective-permute-done | bytes 24608 | tf_op jit(solution)/shard_map/ppermute | solution.py:694
  15.1 0.0 copy-done.3
  15.1 0.0 copy-done.5
  15.1 0.8 %observe.1._.obs = f32[8,128]{1,0:T(8,128)S(1)} custom-call(s32[16]{0:T(128)S(1)} %copy-done.5, s32[16]{0:T(128)S(1)} %copy-done.3, f32[4,4]{1,0:T(4,128)S(1)} %copy-done, f32[48,128]{1,0:T(8,128)S(1)} %combine_near.1.near.rest_0_, f32[48,128]{1,0:T(8,128)S(1)} %collective-permute-done.2.rest_1_), custom_call_target="tpu_custom_call" | custom-call | flops 1000 | bytes 1000 | tf_op jit(solution)/shard_map/observe/pallas_call | solution.py:592
  16.0 0.0 copy-done.1
  16.0 0.0 copy-done.2
  16.0 1.1 %cut_patches.1 = (f32[640,128]{1,0:T(8,128)S(1)}, f32[640,128]{1,0:T(8,128)S(1)}, f32[64,128]{1,0:T(8,128)S(1)}) custom-call(s32[16]{0:T(128)S(1)} %copy-done.1, s32[16]{0:T(128)S(1)} %copy-done.2, f32[20,8,32,128]{3,2,1,0:T(8,128)S(1)} %edge_rows.1.padded.field, f32[8,128]{1,0:T(8,128)S(1)} %observe.1._.obs), custom_call_target="tpu_custom_call" | custom-call | flops 1000 | bytes 1000 | tf_op jit(solution)/shard_map/cut_patches/pallas_call | solution.py:599
  17.1 2.5 %collective-permute-start.3 = (f32[640,128]{1,0:T(8,128)S(1)}, f32[640,128]{1,0:T(8,128)S(1)}, u32[]{:S(2)}, u32[]{:S(2)}) collective-permute-start(f32[640,128]{1,0:T(8,128)S(1)} %get-tuple-element.28), channel_id=1, source_target_pairs={{0,4},{4,0},{8,12},{12,8},{16,20},{20,16},{24,28},{28,24},{1,5},{5... | collective-permute-start | bytes 983048 | tf_op jit(solution)/shard_map/ppermute | solution.py:606
  19.6 0.1 collective-permute-start.4
  19.7 1.2 %collective-permute-done.4.got = f32[8,128]{1,0:T(8,128)S(1)} collective-permute-done((f32[8,128]{1,0:T(8,128)S(1)}, f32[8,128]{1,0:T(8,128)S(1)}, u32[]{:S(2)}, u32[]{:S(2)}) %collective-permute-start.4) | collective-permute-done | bytes 4128 | tf_op jit(solution)/shard_map/ppermute | solution.py:598
  20.8 2.2 %collective-permute-start.7 = (f32[8,128]{1,0:T(8,128)S(1)}, f32[8,128]{1,0:T(8,128)S(1)}, u32[]{:S(2)}, u32[]{:S(2)}) collective-permute-start(f32[8,128]{1,0:T(8,128)S(1)} %join_observed.1.rest_0_), channel_id=1, source_target_pairs={{0,24},{4,28},{8,16},{12,20},{16,8},{20,12},{24,0},{28,4},{1,25},{... | collective-permute-start | bytes 12296 | tf_op jit(solution)/shard_map/ppermute | solution.py:608
  23.0 0.2 collective-permute-start.6
  23.2 0.3 collective-permute-start.5
  23.5 0.7 %collective-permute-done.7.rest_3_ = f32[8,128]{1,0:T(8,128)S(1)} collective-permute-done((f32[8,128]{1,0:T(8,128)S(1)}, f32[8,128]{1,0:T(8,128)S(1)}, u32[]{:S(2)}, u32[]{:S(2)}) %collective-permute-start.7) | collective-permute-done | bytes 4128 | tf_op jit(solution)/shard_map/ppermute | solution.py:608
  24.2 1.3 %collective-permute-done.6.rest_2_ = f32[8,128]{1,0:T(8,128)S(1)} collective-permute-done((f32[8,128]{1,0:T(8,128)S(1)}, f32[8,128]{1,0:T(8,128)S(1)}, u32[]{:S(2)}, u32[]{:S(2)}) %collective-permute-start.6) | collective-permute-done | bytes 4128 | tf_op jit(solution)/shard_map/ppermute | solution.py:608
  25.5 0.2 collective-permute-done.5.rest_1_
  25.7 0.0 collective-permute-done.3.got
  25.7 0.1 moments.1
  25.8 1.6 %collective-permute-start.10 = (f32[320,128]{1,0:T(8,128)S(1)}, f32[320,128]{1,0:T(8,128)S(1)}, u32[]{:S(2)}, u32[]{:S(2)}) collective-permute-start(f32[320,128]{1,0:T(8,128)S(1)} %get-tuple-element.31.rest_0_), channel_id=1, source_target_pairs={{0,24},{4,28},{8,16},{12,20},{16,8},{20,12},{24,0},{28,4},{1,25},{... | collective-permute-start | bytes 491528 | tf_op jit(solution)/shard_map/ppermute | solution.py:615
  27.4 0.2 collective-permute-start.9
  27.6 0.9 %collective-permute-start.8 = (f32[320,128]{1,0:T(8,128)S(1)}, f32[320,128]{1,0:T(8,128)S(1)}, u32[]{:S(2)}, u32[]{:S(2)}) collective-permute-start(f32[320,128]{1,0:T(8,128)S(1)} %get-tuple-element.31.rest_0_), channel_id=1, source_target_pairs={{0,8},{4,12},{8,0},{12,4},{16,24},{20,28},{24,16},{28,20},{1,9},{5... | collective-permute-start | bytes 491528 | tf_op jit(solution)/shard_map/ppermute | solution.py:615
  28.6 0.0 copy-done.4
  28.6 0.0 copy-done.6
  28.6 0.0 copy-done.7
  28.6 2.1 %solve_weights.1._.weights = f32[2,16,128]{2,1,0:T(8,128)S(1)} custom-call(f32[16]{0:T(128)S(1)} %copy-done.6, f32[16]{0:T(128)S(1)} %copy-done.7, f32[2,16]{1,0:T(2,128)S(1)} %copy-done.4, f32[16,128]{1,0:T(8,128)S(1)} %get-tuple-element.30.everyone_ref), custom_call_target="tpu_custom_call" | custom-call | flops 1000 | bytes 1000 | tf_op jit(solution)/shard_map/solve_weights/pallas_call | solution.py:616
  30.7 0.4 collective-permute-done.10.rest_3_
  31.1 4.3 %collective-permute-done.9.rest_2_ = f32[320,128]{1,0:T(8,128)S(1)} collective-permute-done((f32[320,128]{1,0:T(8,128)S(1)}, f32[320,128]{1,0:T(8,128)S(1)}, u32[]{:S(2)}, u32[]{:S(2)}) %collective-permute-start.9) | collective-permute-done | bytes 163872 | tf_op jit(solution)/shard_map/ppermute | solution.py:615
  35.4 0.0 collective-permute-done.8.rest_1_
  35.4 0.1 merge_moments.1.mine
  35.5 1.9 %collective-permute-start.11 = (f32[328,128]{1,0:T(8,128)S(1)}, f32[328,128]{1,0:T(8,128)S(1)}, u32[]{:S(2)}, u32[]{:S(2)}) collective-permute-start(f32[328,128]{1,0:T(8,128)S(1)} %merge_moments.1.mine), channel_id=1, source_target_pairs={{0,4},{4,0},{8,12},{12,8},{16,20},{20,16},{24,28},{28,24},{1,5},{5... | collective-permute-start | bytes 503816 | tf_op jit(solution)/shard_map/ppermute | solution.py:628
  37.3 1.0 %collective-permute-done.11.theirs = f32[328,128]{1,0:T(8,128)S(1)} collective-permute-done((f32[328,128]{1,0:T(8,128)S(1)}, f32[328,128]{1,0:T(8,128)S(1)}, u32[]{:S(2)}, u32[]{:S(2)}) %collective-permute-start.11) | collective-permute-done | bytes 167968 | tf_op jit(solution)/shard_map/ppermute | solution.py:628
  38.4 2.6 %apply_increments.1 = (f32[2,10,16,1024]{3,2,1,0:T(8,128)}, f32[20,8,32,128]{3,2,1,0:T(8,128)S(1)}) custom-call(s32[16]{0:T(128)S(1)} %copy-done.1, s32[16]{0:T(128)S(1)} %copy-done.2, f32[20,8,32,128]{3,2,1,0:T(8,128)S(1)} %edge_rows.1.padded.field, f32[328,128]{1,0:T(8,128)S(1)} %merge_moments.1.mine, ...), custom_call_target="tpu_custom_call", output_to_operand_aliasing={{1}: (2, {})} | custom-call | flops 1000 | bytes 1000 | tf_op jit(solution)/shard_map/apply_increments/pallas_call | solution.py:629
  (2 shorter events, 0.0 us)
Async XLA Ops:
  0.0 12.1 %copy-start = (f32[4,4]{1,0:T(4,128)S(1)}, f32[4,4]{1,0:T(4,128)}, u32[]{:S(2)}) copy-start(f32[4,4]{1,0:T(4,128)} %table.3) | copy-start | bytes 196
  2.7 8.7 %collective-permute-start = (f32[432,128]{1,0:T(8,128)S(1)}, f32[432,128]{1,0:T(8,128)S(1)}, u32[]{:S(2)}, u32[]{:S(2)}) collective-permute-start(f32[432,128]{1,0:T(8,128)S(1)} %get-tuple-element.23), channel_id=1, source_target_pairs={{0,1},{2,3},{1,0},{3,2},{4,5},{6,7},{5,4},{7,6},{8,9},{10,11},{9,8... | collective-permute-start | bytes 663560 | tf_op jit(solution)/shard_map/ppermute | solution.py:664
  2.8 9.3 %collective-permute-start.1 = (f32[432,128]{1,0:T(8,128)S(1)}, f32[432,128]{1,0:T(8,128)S(1)}, u32[]{:S(2)}, u32[]{:S(2)}) collective-permute-start(f32[432,128]{1,0:T(8,128)S(1)} %get-tuple-element.24), channel_id=1, source_target_pairs={{1,2},{2,1},{5,6},{6,5},{9,10},{10,9},{13,14},{14,13},{17,18},{18,... | collective-permute-start | bytes 663560 | tf_op jit(solution)/shard_map/ppermute | solution.py:665
  11.5 3.6 %collective-permute-start.2 = (f32[48,128]{1,0:T(8,128)S(1)}, f32[48,128]{1,0:T(8,128)S(1)}, u32[]{:S(2)}, u32[]{:S(2)}) collective-permute-start(f32[48,128]{1,0:T(8,128)S(1)} %combine_near.1.near.rest_0_), channel_id=1, source_target_pairs={{0,2},{1,3},{2,0},{3,1},{4,6},{5,7},{6,4},{7,5},{8,10},{9,11},{10,... | collective-permute-start | bytes 73736 | tf_op jit(solution)/shard_map/ppermute | solution.py:694
  12.1 3.0 %copy-start.3 = (s32[16]{0:T(128)S(1)}, s32[16]{0:T(128)}, u32[]{:S(2)}) copy-start(s32[16]{0:T(128)} %kind.1) | copy-start | bytes 196
  12.1 3.0 %copy-start.5 = (s32[16]{0:T(128)S(1)}, s32[16]{0:T(128)}, u32[]{:S(2)}) copy-start(s32[16]{0:T(128)} %layer.1) | copy-start | bytes 196
  12.1 3.9 %copy-start.1 = (s32[16]{0:T(128)S(1)}, s32[16]{0:T(128)}, u32[]{:S(2)}) copy-start(s32[16]{0:T(128)} %lat.3) | copy-start | bytes 196
  12.1 3.9 %copy-start.2 = (s32[16]{0:T(128)S(1)}, s32[16]{0:T(128)}, u32[]{:S(2)}) copy-start(s32[16]{0:T(128)} %lon.3) | copy-start | bytes 196
  13.7 14.8 %copy-start.4 = (f32[2,16]{1,0:T(2,128)S(1)}, f32[2,16]{1,0:T(2,128)}, u32[]{:S(2)}) copy-start(f32[2,16]{1,0:T(2,128)} %perturb.1) | copy-start | bytes 388
  13.7 14.8 %copy-start.6 = (f32[16]{0:T(128)S(1)}, f32[16]{0:T(128)}, u32[]{:S(2)}) copy-start(f32[16]{0:T(128)} %value.1) | copy-start | bytes 196
  13.7 14.8 %copy-start.7 = (f32[16]{0:T(128)S(1)}, f32[16]{0:T(128)}, u32[]{:S(2)}) copy-start(f32[16]{0:T(128)} %error.1) | copy-start | bytes 196
  17.1 8.6 %collective-permute-start.3 = (f32[640,128]{1,0:T(8,128)S(1)}, f32[640,128]{1,0:T(8,128)S(1)}, u32[]{:S(2)}, u32[]{:S(2)}) collective-permute-start(f32[640,128]{1,0:T(8,128)S(1)} %get-tuple-element.28), channel_id=1, source_target_pairs={{0,4},{4,0},{8,12},{12,8},{16,20},{20,16},{24,28},{28,24},{1,5},{5... | collective-permute-start | bytes 983048 | tf_op jit(solution)/shard_map/ppermute | solution.py:606
  19.6 1.3 %collective-permute-start.4 = (f32[8,128]{1,0:T(8,128)S(1)}, f32[8,128]{1,0:T(8,128)S(1)}, u32[]{:S(2)}, u32[]{:S(2)}) collective-permute-start(f32[8,128]{1,0:T(8,128)S(1)} %observe.1._.obs), channel_id=1, source_target_pairs={{0,4},{4,0},{8,12},{12,8},{16,20},{20,16},{24,28},{28,24},{1,5},{5... | collective-permute-start | bytes 12296 | tf_op jit(solution)/shard_map/ppermute | solution.py:598
  20.8 3.4 %collective-permute-start.7 = (f32[8,128]{1,0:T(8,128)S(1)}, f32[8,128]{1,0:T(8,128)S(1)}, u32[]{:S(2)}, u32[]{:S(2)}) collective-permute-start(f32[8,128]{1,0:T(8,128)S(1)} %join_observed.1.rest_0_), channel_id=1, source_target_pairs={{0,24},{4,28},{8,16},{12,20},{16,8},{20,12},{24,0},{28,4},{1,25},{... | collective-permute-start | bytes 12296 | tf_op jit(solution)/shard_map/ppermute | solution.py:608
  23.0 2.5 %collective-permute-start.6 = (f32[8,128]{1,0:T(8,128)S(1)}, f32[8,128]{1,0:T(8,128)S(1)}, u32[]{:S(2)}, u32[]{:S(2)}) collective-permute-start(f32[8,128]{1,0:T(8,128)S(1)} %join_observed.1.rest_0_), channel_id=1, source_target_pairs={{0,16},{4,20},{8,24},{12,28},{16,0},{20,4},{24,8},{28,12},{1,17},{... | collective-permute-start | bytes 12296 | tf_op jit(solution)/shard_map/ppermute | solution.py:608
  23.2 2.5 %collective-permute-start.5 = (f32[8,128]{1,0:T(8,128)S(1)}, f32[8,128]{1,0:T(8,128)S(1)}, u32[]{:S(2)}, u32[]{:S(2)}) collective-permute-start(f32[8,128]{1,0:T(8,128)S(1)} %join_observed.1.rest_0_), channel_id=1, source_target_pairs={{0,8},{4,12},{8,0},{12,4},{16,24},{20,28},{24,16},{28,20},{1,9},{5... | collective-permute-start | bytes 12296 | tf_op jit(solution)/shard_map/ppermute | solution.py:608
  25.8 5.2 %collective-permute-start.10 = (f32[320,128]{1,0:T(8,128)S(1)}, f32[320,128]{1,0:T(8,128)S(1)}, u32[]{:S(2)}, u32[]{:S(2)}) collective-permute-start(f32[320,128]{1,0:T(8,128)S(1)} %get-tuple-element.31.rest_0_), channel_id=1, source_target_pairs={{0,24},{4,28},{8,16},{12,20},{16,8},{20,12},{24,0},{28,4},{1,25},{... | collective-permute-start | bytes 491528 | tf_op jit(solution)/shard_map/ppermute | solution.py:615
  27.4 8.0 %collective-permute-start.9 = (f32[320,128]{1,0:T(8,128)S(1)}, f32[320,128]{1,0:T(8,128)S(1)}, u32[]{:S(2)}, u32[]{:S(2)}) collective-permute-start(f32[320,128]{1,0:T(8,128)S(1)} %get-tuple-element.31.rest_0_), channel_id=1, source_target_pairs={{0,16},{4,20},{8,24},{12,28},{16,0},{20,4},{24,8},{28,12},{1,17},{... | collective-permute-start | bytes 491528 | tf_op jit(solution)/shard_map/ppermute | solution.py:615
  27.6 7.8 %collective-permute-start.8 = (f32[320,128]{1,0:T(8,128)S(1)}, f32[320,128]{1,0:T(8,128)S(1)}, u32[]{:S(2)}, u32[]{:S(2)}) collective-permute-start(f32[320,128]{1,0:T(8,128)S(1)} %get-tuple-element.31.rest_0_), channel_id=1, source_target_pairs={{0,8},{4,12},{8,0},{12,4},{16,24},{20,28},{24,16},{28,20},{1,9},{5... | collective-permute-start | bytes 491528 | tf_op jit(solution)/shard_map/ppermute | solution.py:615
  35.5 2.9 %collective-permute-start.11 = (f32[328,128]{1,0:T(8,128)S(1)}, f32[328,128]{1,0:T(8,128)S(1)}, u32[]{:S(2)}, u32[]{:S(2)}) collective-permute-start(f32[328,128]{1,0:T(8,128)S(1)} %merge_moments.1.mine), channel_id=1, source_target_pairs={{0,4},{4,0},{8,12},{12,8},{16,20},{20,16},{24,28},{28,24},{1,5},{5... | collective-permute-start | bytes 503816 | tf_op jit(solution)/shard_map/ppermute | solution.py:628

commit v3 on v2

--- a/solution.py
+++ b/solution.py
@@ -15,7 +15,7 @@
 WINDOW_WIDTH = 128
 DIFFUSION = 0.08
 DEPOSIT = 0.5
-CAP = 16
+CAPS = (6, 7, 8, 10)
 
 LANES = 128
 PAD = 8
@@ -29,13 +29,18 @@
 HBM = pl.BlockSpec(memory_space=pltpu.HBM)
 
 
-def call(kernel, name, in_specs, outs, scratch=(), flops=1000, aliases=None, limit=40):
+def call(kernel, name, in_specs, outs, scratch=(), flops=1000, aliases=None, limit=40, out_space=VMEM):
     return pl.pallas_call(
         kernel,
         name=name,
         in_specs=in_specs,
-        out_specs=[VMEM] * len(outs),
-        out_shape=[jax.ShapeDtypeStruct(shape, jnp.float32) for shape in outs],
+        out_specs=[SMEM if shape == (1,) else out_space for shape in outs],
+        out_shape=[
+            shape
+            if isinstance(shape, jax.ShapeDtypeStruct)
+            else jax.ShapeDtypeStruct(shape, jnp.int32 if shape == (1,) else jnp.float32)
+            for shape in outs
+        ],
         scratch_shapes=list(scratch),
         input_output_aliases=aliases or {},
         compiler_params=pltpu.CompilerParams(vmem_limit_bytes=limit * MIB),
@@ -122,36 +127,42 @@
     return copies
 
 
-def pack_kernel(lat_hbm, lon_hbm, kind_hbm, state_hbm, vel_hbm, band_hbm, out_a, out_b, near, s0, vs, bs, lat, lon, kind, sems):
+def load_kernel(lat_hbm, lon_hbm, kind_hbm, state_hbm, vel_hbm, band_hbm, out_a, out_b, near, s0, vs, bs, lat, lon, kind, sems):
     members, _, rows, width = state_hbm.shape
     tiles = width // LANES
     fields, parts = members * FIELDS, members * 2 * NLAYER
-    moves = lane_tiles(state_hbm, s0, members, tiles, FIELDS, rows, 0)
+    moves = lane_tiles(state_hbm, s0, members, tiles, FIELDS, rows, 1)
     moves += lane_tiles(vel_hbm, vs, members, tiles, 2 * NLAYER, rows, 0)
     moves += [(band_hbm.at[:, pl.ds(i * LANES, LANES)], bs.at[i, pl.ds(PAD, rows), :]) for i in range(tiles)]
     moves += [(lat_hbm, lat), (lon_hbm, lon), (kind_hbm, kind)]
     copies = start_copies(moves, sems)
     tile = lax.axis_index("tile")
+    first = tile * rows
     even = tile % 2 == 0
-    first = tile * rows
     zero = jnp.zeros((PAD, LANES), jnp.float32)
-    for ref in (s0, vs, bs):
-        for n in range(ref.shape[0]) if ref is not bs else (None,):
-            for i in range(tiles):
-                lead = (i,) if n is None else (n, i)
-                ref[lead + (slice(0, PAD),)] = zero.astype(ref.dtype)
-                ref[lead + (slice(PAD + rows, None),)] = zero.astype(ref.dtype)
+    bands = jnp.zeros((PAD, LANES), jnp.int32)
+    for i in range(tiles):
+        for part in (slice(0, PAD), slice(PAD + rows, None)):
+            for f in range(fields):
+                s0[f, i + 1, part, :] = zero
+            for c in range(parts):
+                vs[c, i, part, :] = zero
+            bs[i, part, :] = bands
+    for f in range(fields):
+        for r in range(0, rows + 2 * PAD, PAD):
+            s0[f, 0, r : r + PAD, :] = zero
+            s0[f, tiles + 1, r : r + PAD, :] = zero
     for copy in copies:
         copy.wait()
 
     def edge(out, q_first, v_at):
         for i in range(tiles):
             for c in range(parts):
-                to = NEAR_ROWS + i * parts + c
+                to = i * parts + c
                 out[to : to + 1, :] = vs[c, i, v_at : v_at + 1, :]
             for f in range(fields):
-                to = NEAR_ROWS + tiles * parts + (i * fields + f) * 2
-                out[to : to + 2, :] = s0[f, i, q_first : q_first + 2, :]
+                to = tiles * parts + (i * fields + f) * 2
+                out[to : to + 2, :] = s0[f, i + 1, q_first : q_first + 2, :]
 
     top, bottom = PAD, PAD + rows
 
@@ -179,16 +190,16 @@
         here = lane >= shift
         mine = (lane // GROUP) == j
 
-        def fetch(ref, old, *lead):
+        def fetch(ref, old, *lead, by=0):
             both = jnp.where(
-                here, ref[lead + (block, pl.ds(start, 8))], ref[lead + (after, pl.ds(start, 8))]
+                here, ref[lead + (block + by, pl.ds(start, 8))], ref[lead + (after + by, pl.ds(start, 8))]
             )
             return jnp.where(mine, pltpu.roll(both.astype(jnp.float32), turn, 1), old)
 
         for m in range(members):
             for l in range(NLAYER):
                 s = m * NLAYER + l
-                qs[s] = fetch(s0, qs[s], m * FIELDS + l * KINDS + kind[j])
+                qs[s] = fetch(s0, qs[s], m * FIELDS + l * KINDS + kind[j], by=1)
                 us[s] = fetch(vs, us[s], 2 * s)
                 ws[s] = fetch(vs, ws[s], 2 * s + 1)
         bins = fetch(bs, bins)
@@ -198,12 +209,13 @@
         w = jnp.where(row < 4, ws[2 * m], pltpu.roll(ws[2 * m + 1], 4, 0))
         blocks.append(jnp.where(row == 0, pltpu.roll(bins, 6, 0), w))
     for n, block in enumerate(blocks):
-        for out in (near, out_a, out_b):
-            out[8 * n : 8 * n + 8, :] = block
+        near[8 * n : 8 * n + 8, :] = block
+        base = tiles * (parts + 2 * fields) + 8 * n
+        out_a[base : base + 8, :] = block
 
 
 def combine_kernel(near, from_a, _, out):
-    out[...] = near[...] + from_a[:NEAR_ROWS, :]
+    out[...] = near[...] + from_a[from_a.shape[0] - NEAR_ROWS :, :]
 
 
 def advance(source, f, i, r, coef, lane):
@@ -230,22 +242,16 @@
     return a - settled, b + settled - DEPOSIT * rate * b
 
 
-def interior_kernel(table_hbm, state, vel, band_hbm, padded, own_edge, once_edge, vel_edge, bin_edge, s0, s1, vs, band, table, sems):
-    members, _, rows, width = state.shape
-    tiles = width // LANES
-    fields, parts = members * FIELDS, members * 2 * NLAYER
-    moves = lane_tiles(vel, vs, members, tiles, 2 * NLAYER, rows, 0)
-    moves += lane_tiles(state, s0, members, tiles, FIELDS, rows, 1)
-    moves += [(band_hbm, band), (table_hbm, table)]
-    copies = start_copies(moves, sems)
+def interior_kernel(row_tiles, rows, caps, lat_hbm, table_hbm, s0, vs, band, padded, own_edge, once_edge, vel_edge, bin_edge, step_of, s1, lat, table, sems):
+    fields, tiles, _, _ = padded.shape
+    members = fields // FIELDS
+    parts = members * 2 * NLAYER
+    copies = start_copies([(lat_hbm, lat), (table_hbm, table)], sems)
     zero = jnp.zeros((rows + 2 * PAD, LANES), jnp.float32)
     lane = lane_index()
     for f in range(fields):
-        for buffer in (s0, s1):
-            buffer[f, 0, :, :] = zero
-            buffer[f, tiles + 1, :, :] = zero
-    for copy in copies:
-        copy.wait()
+        s1[f, 0, :, :] = zero
+        s1[f, tiles + 1, :, :] = zero
 
     def first_step(t, carry):
         ml, i = t // tiles, t % tiles
@@ -257,16 +263,26 @@
 
     for t in range(members * NLAYER * tiles):
         first_step(t, 0)
+    for copy in copies:
+        copy.wait()
+
+    most = jnp.int32(0)
+    for n in range(row_tiles):
+        count = jnp.int32(0)
+        for j in range(lat.shape[0]):
+            start = lat[j] - WINDOW_HEIGHT // 2 - n * rows
+            count = count + ((start < rows) & (start + WINDOW_HEIGHT > 0)).astype(jnp.int32)
+        most = jnp.maximum(most, count)
+    step_of[0] = sum((most > cap).astype(jnp.int32) for cap in caps)
 
     def second_step(t, carry):
         m, i = t // tiles, t % tiles
-        lanes = pl.ds(i * LANES, LANES)
         for r in range(PAD, PAD + rows, 8):
             coefs = []
             for l in range(NLAYER):
                 mc = (m * NLAYER + l) * 2
                 coefs.append(coefficients(vs[mc, i, r : r + 8, :], vs[mc + 1, i, r : r + 8, :]))
-            bins = band[r - PAD : r - PAD + 8, lanes]
+            bins = band[i, r : r + 8, :]
             for k in range(KINDS):
                 upper = m * FIELDS + k
                 lower = upper + KINDS
@@ -295,9 +311,7 @@
         for c in range(parts):
             vel_edge[0, c, i, :, :] = halves(vs, (c, i), top - 2, bottom - 2)
             vel_edge[1, c, i, :, :] = halves(vs, (c, i), top - 1, bottom - 3)
-        upper = band[0:8, i * LANES : (i + 1) * LANES].astype(jnp.float32)
-        lower = band[rows - 8 : rows, i * LANES : (i + 1) * LANES].astype(jnp.float32)
-        bin_edge[i, :, :] = jnp.where(half, pltpu.roll(upper, 1, 0), pltpu.roll(lower, 7, 0))
+        bin_edge[i, :, :] = halves(band, (i,), top - 1, bottom - 3).astype(jnp.float32)
 
 
 def observe_kernel(members, layer, kind, table, *rest):
@@ -349,10 +363,6 @@
     out[...] = choose(seen, squeeze)
 
 
-def join_kernel(members, obs, got, out):
-    out[...] = jnp.where(row_index() < members, obs[...], pltpu.roll(got[...], members, 0))
-
-
 def edge_kernel(table, own_edge, once_edge, vel_edge, bin_edge, from_a, from_b, inner, near, padded, e0, e1, up, down):
     fields, tiles, padded_rows, _ = padded.shape
     rows = padded_rows - 2 * PAD
@@ -361,23 +371,29 @@
     tile = lax.axis_index("tile")
     count_tiles = lax.axis_size("tile")
     even = tile % 2 == 0
-    sent = from_a.shape[0]
+    sent = from_b.shape[0]
 
     @pl.when(even)
     def _():
-        down[:sent, :] = from_a[...]
-        up[:sent, :] = from_b[...]
+        down[PAD : PAD + sent, :] = from_a[:sent, :]
+        up[PAD : PAD + sent, :] = from_b[...]
 
     @pl.when(jnp.logical_not(even))
     def _():
-        up[:sent, :] = from_a[...]
-        down[:sent, :] = from_b[...]
+        up[PAD : PAD + sent, :] = from_a[:sent, :]
+        down[PAD : PAD + sent, :] = from_b[...]
+
+    for edge_tile, ref in ((0, up), (count_tiles - 1, down)):
+
+        @pl.when(tile == edge_tile)
+        def _():
+            ref[...] = jnp.zeros(ref.shape, jnp.float32)
 
     lane = lane_index()
     row = row_index()
     zero = jnp.zeros((8, LANES), jnp.float32)
-    v_base = NEAR_ROWS
-    q_base = NEAR_ROWS + tiles * parts
+    v_base = PAD
+    q_base = PAD + tiles * parts
     for f in range(fields):
         for buffer in (e0, e1):
             buffer[f, 0, :, :] = zero
@@ -439,7 +455,7 @@
         second_step(t, 0)
 
 
-def cut_kernel(cap, lat, lon, padded, _, own, send, sel, slots):
+def cut_kernel(cap, lat, lon, padded, obs, own, send, sel, slots):
     fields, tiles, padded_rows, _ = padded.shape
     rows = padded_rows - 2 * PAD
     members = fields // FIELDS
@@ -450,6 +466,7 @@
     count = find_slots(lat, slots, first, rows, cap)
     for s in range(cap):
         sel[s * 4 : s * 4 + 4, :] = (lane[:4] == slots[s]).astype(jnp.float32)
+    send[members * KINDS * size :, :] = obs[...]
 
     def cut(layer_of_own):
         def one(s, carry):
@@ -472,23 +489,26 @@
         pl.when(core == c)(functools.partial(cut, c))
 
 
-def moment_kernel(cap, members, chips, own, got, sel, *rest):
-    seens, (cross, everyone) = rest[:chips], rest[chips:]
+def pair_kernel(cap, members, own, got, obs, sel, msg):
     size = cap * WINDOW_HEIGHT
     part = KINDS * size
-    both = 2 * members
-    for c, seen in enumerate(seens):
-        everyone[c * both : (c + 1) * both, :] = seen[:both, :]
-    mean = jnp.sum(everyone[...], axis=0, keepdims=True) / (chips * both)
-    sources = [(own, m, m) for m in range(members)] + [(got, m, members + m) for m in range(members)]
-    weight = [
-        jnp.sum(sel[...] * (everyone[o : o + 1, :] - mean), axis=1, keepdims=True) for _, _, o in sources
-    ]
+    seen, theirs = obs[:members, :], got[members * part : members * part + members, :]
+    mean = (jnp.sum(seen, axis=0, keepdims=True) + jnp.sum(theirs, axis=0, keepdims=True)) / (2 * members)
+    sources = [(own, m, seen[m : m + 1]) for m in range(members)]
+    sources += [(got, m, theirs[m : m + 1]) for m in range(members)]
+    weight = [jnp.sum(sel[...] * (o - mean), axis=1, keepdims=True) for _, _, o in sources]
     for k in range(KINDS):
+        cross = jnp.zeros((size, LANES), jnp.float32)
         total = jnp.zeros((size, LANES), jnp.float32)
         for (ref, m, _), o in zip(sources, weight):
-            total = total + ref[m * part + k * size : m * part + (k + 1) * size, :] * o
-        cross[k * size : (k + 1) * size, :] = total
+            patch = ref[m * part + k * size : m * part + (k + 1) * size, :]
+            cross = cross + patch * o
+            total = total + patch
+        msg[k * size : (k + 1) * size, :] = cross
+        msg[part + k * size : part + (k + 1) * size, :] = total
+    msg[2 * part :, :] = jnp.zeros((8, LANES), jnp.float32)
+    msg[2 * part : 2 * part + members, :] = seen
+    msg[2 * part + members : 2 * part + 2 * members, :] = theirs
 
 
 def weight_kernel(value, error, perturb, everyone_ref, weights):
@@ -519,20 +539,31 @@
         )
 
 
-def merge_kernel(cap, number, _, *rest):
-    parts, gain = rest[:-1], rest[-1]
+def merge_kernel(cap, members, chips, sel, *rest):
+    msgs, (gain, everyone) = rest[:chips], rest[chips:]
     size = cap * WINDOW_HEIGHT
+    part = KINDS * size
+    both = 2 * members
+    number = chips * both
+    means = []
+    for c, msg in enumerate(msgs):
+        seen = msg[2 * part : 2 * part + both, :]
+        everyone[c * both : (c + 1) * both, :] = seen
+        means.append(jnp.sum(seen, axis=0, keepdims=True) / both)
+    mean = functools.reduce(jnp.add, means) / chips
+    shifts = [jnp.sum(sel[...] * (own - mean), axis=1, keepdims=True) for own in means]
     row = (row_index(size) % WINDOW_HEIGHT).astype(jnp.float32)
     column = lane_index(size).astype(jnp.float32)
     row = (row + 0.5 - WINDOW_HEIGHT / 2) / (WINDOW_HEIGHT / 2)
     column = (column + 0.5 - WINDOW_WIDTH / 2) / (WINDOW_WIDTH / 2)
     taper = (1.0 - row * row) * (1.0 - column * column) / (number - 1)
     for k in range(KINDS):
-        total = parts[0][k * size : (k + 1) * size, :]
-        for more in parts[1:]:
-            total = total + more[k * size : (k + 1) * size, :]
-        gain[k * size : (k + 1) * size, :] = taper * total
-    gain[KINDS * size :, :] = jnp.zeros((8, LANES), jnp.float32)
+        cross = jnp.zeros((size, LANES), jnp.float32)
+        for msg, shift in zip(msgs, shifts):
+            cross = cross + msg[k * size : (k + 1) * size, :]
+            cross = cross + shift * msg[part + k * size : part + (k + 1) * size, :]
+        gain[k * size : (k + 1) * size, :] = taper * cross
+    gain[part:, :] = jnp.zeros((8, LANES), jnp.float32)
 
 
 def apply_kernel(cap, lat, lon, field, mine, theirs, weights, out, work, slots):
@@ -572,6 +603,16 @@
             out[f // FIELDS, f % FIELDS, :, i * LANES : (i + 1) * LANES] = work[f, i, PAD : PAD + rows, :]
 
 
+def swaps(devices, row_tiles, start):
+    routes = []
+    for i in range(devices):
+        for t in range(row_tiles):
+            pair = t + 1 if (t - start) % 2 == 0 else t - 1
+            to = (i, pair) if t >= start and pair < row_tiles else (i ^ 1, t)
+            routes.append((i * row_tiles + t, to[0] * row_tiles + to[1]))
+    return routes
+
+
 def partner(size, k):
     if size & (size - 1) == 0:
         return [(i, i ^ k) for i in range(size)]
@@ -595,37 +636,34 @@
         [SMEM] * 3 + [VMEM] * len(near),
         [(8, LANES)],
     )(layer, kind, table, *near)
-    got_obs = lax.ppermute(obs, "member", other_core)
     own, send, sel = call(
         functools.partial(cut_kernel, cap),
         "cut_patches",
         [SMEM] * 2 + [VMEM] * 2,
-        [(members * part, LANES), (members * part, LANES), (size, LANES)],
+        [(members * part, LANES), (members * part + 8, LANES), (size, LANES)],
         [slots],
     )(lat, lon, field, obs)
     got = lax.ppermute(send, "member", other_core)
-    (seen,) = call(functools.partial(join_kernel, members), "join_observed", [VMEM] * 2, [(8, LANES)])(obs, got_obs)
-    seens = [seen] + [lax.ppermute(seen, "member", partner(devices, 2 * k)) for k in range(1, chips)]
-    cross, everyone = call(
-        functools.partial(moment_kernel, cap, members, chips),
-        "moments",
-        [VMEM] * (3 + chips),
-        [(part, LANES), (chips * both, LANES)],
-    )(own, got, sel, *seens)
-    crosses = [cross] + [lax.ppermute(cross, "member", partner(devices, 2 * k)) for k in range(1, chips)]
+    (msg,) = call(
+        functools.partial(pair_kernel, cap, members),
+        "pair_moments",
+        [VMEM] * 4,
+        [(2 * part + 8, LANES)],
+    )(own, got, obs, sel)
+    msgs = [msg] + [lax.ppermute(msg, "member", partner(devices, 2 * k)) for k in range(1, chips)]
+    mine, everyone = call(
+        functools.partial(merge_kernel, cap, members, chips),
+        "merge_moments",
+        [VMEM] * (1 + chips),
+        [(part + 8, LANES), (chips * both, LANES)],
+    )(sel, *msgs)
+    theirs = lax.ppermute(mine, "member", other_core)
     (weights,) = call(
         weight_kernel,
         "solve_weights",
         [SMEM] * 2 + [VMEM] * 2,
         [(members, observations, LANES)],
     )(value, error, perturb, everyone)
-    (mine,) = call(
-        functools.partial(merge_kernel, cap, chips * both),
-        "merge_moments",
-        [VMEM] * (1 + chips),
-        [(part + 8, LANES)],
-    )(weights, *crosses)
-    theirs = lax.ppermute(mine, "member", other_core)
     analysed, _ = call(
         functools.partial(apply_kernel, cap),
         "apply_increments",
@@ -643,59 +681,65 @@
     row_tiles = lax.axis_size("tile")
     fields, parts = members * FIELDS, members * 2 * NLAYER
     padded_rows = rows + 2 * PAD
-    message = (NEAR_ROWS + tiles * (parts + 2 * fields), LANES)
-    out_a, out_b, near = call(
-        pack_kernel,
-        "pack_edges",
+    caps = [cap for cap in CAPS if cap < lat.shape[0]] + [lat.shape[0]]
+    message = (tiles * (parts + 2 * fields), LANES)
+    out_a, out_b, near, s0, vs, bins = call(
+        load_kernel,
+        "load_arguments",
         [HBM] * 6,
-        [message, message, (NEAR_ROWS, LANES)],
         [
-            pltpu.VMEM((fields, tiles, padded_rows, LANES), jnp.float32),
-            pltpu.VMEM((parts, tiles, padded_rows, LANES), jnp.float32),
-            pltpu.VMEM((tiles, padded_rows, LANES), jnp.int32),
+            (message[0] + NEAR_ROWS, LANES),
+            message,
+            (NEAR_ROWS, LANES),
+            (fields, tiles + 2, padded_rows, LANES),
+            (parts, tiles, padded_rows, LANES),
+            jax.ShapeDtypeStruct((tiles, padded_rows, LANES), jnp.int32),
+        ],
+        [
             pltpu.SMEM(lat.shape, jnp.int32),
             pltpu.SMEM(lon.shape, jnp.int32),
             pltpu.SMEM(kind.shape, jnp.int32),
             pltpu.SemaphoreType.DMA((4 * members * tiles + tiles + 3,)),
         ],
     )(*held(lat, lon, kind, state, vel, band))
-    pairs_a = [(i, i + 1) for i in range(0, row_tiles - 1, 2)]
-    pairs_b = [(i, i + 1) for i in range(1, row_tiles - 1, 2)]
-    from_a = lax.ppermute(out_a, "tile", pairs_a + [(j, i) for i, j in pairs_a])
-    from_b = lax.ppermute(out_b, "tile", pairs_b + [(j, i) for i, j in pairs_b])
+    devices = lax.axis_size("member")
+    butterfly = row_tiles & (row_tiles - 1) == 0
+    from_a = lax.ppermute(out_a, ("member", "tile"), swaps(devices, row_tiles, 0))
+    from_b = lax.ppermute(out_b, ("member", "tile"), swaps(devices, row_tiles, 1))
     wide = pltpu.VMEM((fields, tiles + 2, padded_rows, LANES), jnp.float32)
-    inner, own_edge, once_edge, vel_edge, bin_edge = call(
-        interior_kernel,
+    inner, own_edge, once_edge, vel_edge, bin_edge, step_of = call(
+        functools.partial(interior_kernel, row_tiles, rows, caps[:-1]),
         "interior_rows",
-        [HBM] * 4,
+        [HBM] * 2 + [VMEM] * 3,
         [
             (fields, tiles, padded_rows, LANES),
             (fields, tiles, 8, LANES),
             (fields, tiles, 8, LANES),
             (2, parts, tiles, 8, LANES),
             (tiles, 8, LANES),
+            (1,),
         ],
         [
             wide,
-            wide,
-            pltpu.VMEM((parts, tiles, padded_rows, LANES), jnp.float32),
-            pltpu.VMEM(band.shape, jnp.int32),
+            pltpu.SMEM(lat.shape, jnp.int32),
             pltpu.SMEM(table.shape, jnp.float32),
-            pltpu.SemaphoreType.DMA((2 * members * tiles + 2,)),
+            pltpu.SemaphoreType.DMA((2,)),
         ],
         flops=20000000,
-    )(*held(table, state, vel, band))
-    if row_tiles & (row_tiles - 1) == 0:
-        (near,) = call(combine_kernel, "combine_near", [VMEM] * 3, [(NEAR_ROWS, LANES)])(near, from_a, bin_edge)
+    )(*held(lat, table), s0, vs, bins)
+    if butterfly:
+        if row_tiles > 1:
+            (near,) = call(combine_kernel, "combine_near", [VMEM] * 3, [(NEAR_ROWS, LANES)])(near, from_a, bin_edge)
         step = 2
         while step < row_tiles // 2:
             near = near + lax.ppermute(near, "tile", partner(row_tiles, step))
             step *= 2
         nears = [near] + ([lax.ppermute(near, "tile", partner(row_tiles, step))] if step < row_tiles else [])
     else:
-        nears = [lax.psum(near, "tile")]
+        near = lax.psum(near, "tile")
+        nears = [near]
     narrow = pltpu.VMEM((fields, tiles + 2, 8, LANES), jnp.float32)
-    halo = pltpu.VMEM((message[0] + 8, LANES), jnp.float32)
+    halo = pltpu.VMEM((message[0] + 2 * PAD, LANES), jnp.float32)
     (field,) = call(
         edge_kernel,
         "edge_rows",
@@ -704,7 +748,8 @@
         [narrow, narrow, halo, halo],
         aliases={7: 0},
     )(table, own_edge, once_edge, vel_edge, bin_edge, from_a, from_b, inner, near)
-    return analyse(CAP, state.shape, field, nears, lat, lon, layer, kind, table, value, error, perturb)
+    operands = (field, nears, lat, lon, layer, kind, table, value, error, perturb)
+    return lax.switch(step_of[0], [functools.partial(analyse, cap, state.shape) for cap in caps], *operands)
 
 
 def solution(mesh):

time: 41 us -> 34.7 us (0.85)
  the two profiles are of different devices: /device:TPU:9 before, /device:TPU:1 now
where the time goes in v3:
time: 34.7 us; the launch traced here: 34.2 us
  Pallas kernels  13.6 us (39%)
  starting transfers between devices  10.5 us (30%)
  waiting for transfers between devices  9.09 us (26%)
  between operations  0.82 us (2%)
    ppermute x3, waiting for transfers between devices, analyse(): lax.ppermute(msg, 'member', partner(devices, 2 * k))  6.3 us
    ppermute x3, starting transfers between devices, analyse(): lax.ppermute(msg, 'member', partner(devices, 2 * k))  2.71 us
    pallas_call x1, Pallas kernels, body(): call(load_kernel, 'load_arguments', [HBM] * 6, [(message[0] + NEAR_ROWS,...  2.71 us
    pallas_call x1, Pallas kernels, analyse(): call(functools.partial(apply_kernel, cap), 'apply_increments', [SMEM] * 2...  2.64 us
    pallas_call x1, Pallas kernels, body(): call(functools.partial(interior_kernel, row_tiles, rows, caps[:-1]), 'int...  2.39 us
    ppermute x1, starting transfers between devices, body(): lax.ppermute(out_a, ('member', 'tile'), swaps(devices, row_tiles, 0))  2.19 us
    ppermute x1, starting transfers between devices, body(): lax.ppermute(near, 'tile', partner(row_tiles, step))  2.15 us
    pallas_call x1, Pallas kernels, analyse(): call(weight_kernel, 'solve_weights', [SMEM] * 2 + [VMEM] * 2, [(members,...  2.11 us
  transfers between devices with their start and end apart: 8, of which 4 were waited for; matrix products, arithmetic and copies ran while one was open for 0% of the time, Pallas kernels for 18%

profile of v3, /device:TPU:1, one launch (start us, length us, event | category | flops | bytes accessed | tf_op | source)
XLA Modules:
  0.0 34.2 jit_solution(15897950790969246733)
XLA Ops:
  0.0 2.7 %load_arguments.1 = (f32[432,128]{1,0:T(8,128)S(1)}, f32[384,128]{1,0:T(8,128)S(1)}, f32[48,128]{1,0:T(8,128)S(1)}, f32[20,10,32,128]{3,2,1,0:T(8,128)S(1)}, f32...) custom-call(s32[16]{0:T(128)} %lat_hbm.3, s32[16]{0:T(128)} %lon_hbm.1, s32[16]{0:T(128)} %kind_hbm.1, ...), custom_call_target="tpu_custom_call" | custom-call | flops 1000 | bytes 1000 | tf_op jit(solution)/shard_map/load_arguments/pallas_call | solution.py:686
  2.7 0.0 copy-start
  2.7 2.2 %collective-permute-start.25 = (f32[432,128]{1,0:T(8,128)S(1)}, f32[432,128]{1,0:T(8,128)S(1)}, u32[]{:S(2)}, u32[]{:S(2)}) collective-permute-start(f32[432,128]{1,0:T(8,128)S(1)} %get-tuple-element.223), channel_id=1, source_target_pairs={{0,1},{1,0},{2,3},{3,2},{4,5},{5,4},{6,7},{7,6},{8,9},{9,8},{10,11... | collective-permute-start | bytes 663560 | tf_op jit(solution)/shard_map/ppermute | solution.py:707
  4.9 1.0 %collective-permute-start.27 = (f32[384,128]{1,0:T(8,128)S(1)}, f32[384,128]{1,0:T(8,128)S(1)}, u32[]{:S(2)}, u32[]{:S(2)}) collective-permute-start(f32[384,128]{1,0:T(8,128)S(1)} %get-tuple-element.228), channel_id=1, source_target_pairs={{0,4},{1,2},{2,1},{3,7},{4,0},{5,6},{6,5},{7,3},{8,12},{9,10},{10,... | collective-permute-start | bytes 589832 | tf_op jit(solution)/shard_map/ppermute | solution.py:708
  5.9 2.4 %interior_rows.1 = (f32[20,8,32,128]{3,2,1,0:T(8,128)S(1)}, f32[20,8,8,128]{3,2,1,0:T(8,128)S(1)}, f32[20,8,8,128]{3,2,1,0:T(8,128)S(1)}, f32[2,8,8,8,128]{4,3,2...) custom-call(s32[16]{0:T(128)} %lat_hbm.3, f32[4,4]{1,0:T(4,128)} %table.1, ...), custom_call_target="tpu_custom_call" | custom-call | flops 20000000 | bytes 1000 | tf_op jit(solution)/shard_map/interior_rows/pallas_call | solution.py:710
  8.3 1.8 %collective-permute-done.25.from_a = f32[432,128]{1,0:T(8,128)S(1)} collective-permute-done((f32[432,128]{1,0:T(8,128)S(1)}, f32[432,128]{1,0:T(8,128)S(1)}, u32[]{:S(2)}, u32[]{:S(2)}) %collective-permute-start.25) | collective-permute-done | bytes 221216 | tf_op jit(solution)/shard_map/ppermute | solution.py:707
  10.1 2.2 %collective-permute-start.26 = (f32[48,128]{1,0:T(8,128)S(1)}, f32[48,128]{1,0:T(8,128)S(1)}, u32[]{:S(2)}, u32[]{:S(2)}) collective-permute-start(f32[48,128]{1,0:T(8,128)S(1)} %combine_near.1.near), channel_id=1, source_target_pairs={{0,2},{1,3},{2,0},{3,1},{4,6},{5,7},{6,4},{7,5},{8,10},{9,11},{10,... | collective-permute-start | bytes 73736 | tf_op jit(solution)/shard_map/ppermute | solution.py:737
  12.9 0.0 collective-permute-done.27.from_b
  12.9 0.0 copy-done
  12.9 0.0 copy-start.1
  12.9 0.0 copy-start.2
  12.9 0.0 copy-start.3
  13.0 0.0 copy-start.4
  13.0 0.0 copy-start.5
  13.0 0.0 copy-start.6
  13.0 0.0 copy-start.7
  13.0 1.6 %edge_rows.1 = f32[20,8,32,128]{3,2,1,0:T(8,128)S(1)} custom-call(f32[4,4]{1,0:T(4,128)S(1)} %copy-done, f32[20,8,8,128]{3,2,1,0:T(8,128)S(1)} %get-tuple-element.225.own_edge, f32[20,8,8,128]{3,2,1,0:T(8,128)S(1)} %get-tuple-element.226.once_edge, f32[2,8,8,8,128]{4,3,2,1,0:T(8,128)S(1)} %get-tuple-element.227.vel_edge, ...), custom_call_target="tpu_custom_call", output_to_operand_aliasing={{}: (7, {})} | custom-call | flops 1000 | bytes 1000 | tf_op jit(solution)/shard_map/edge_rows/pallas_call | solution.py:743
  14.6 0.0 collective-permute-done.26
  14.6 0.0 copy-done.1
  14.6 0.0 copy-done.2
  14.6 0.0 copy-done.3
  14.6 0.0 copy-done.4
  14.6 0.0 copy-done.5
  14.7 0.0 copy-done.6
  14.7 0.0 copy-done.7
  14.7 19.5 %conditional.1 = (f32[2,10,16,1024]{3,2,1,0:T(8,128)}) conditional(s32[]{:T(128)} %bitcast, (s32[16]{0:T(128)S(1)}, s32[16]{0:T(128)S(1)}, f32[4,4]{1,0:T(4,128)S(1)}, f32[48,128]{1,0:T(8,128)S(1)}, f32[48,128]{1,0:T(8,128)S(1)}, /*index=5*/s32[16]{0:T(128)S(1)}, s32[16]{0:T(128)S(1)}, ...), branch_computations={%region_0.0_spmd, %region_1.0_spmd, %region_2.0_spmd, %region_3.0_... | conditional | flops 6000 | bytes 5986368 | solution.py:752
  14.7 0.8 %observe.5.obs = f32[8,128]{1,0:T(8,128)S(1)} custom-call(s32[16]{0:T(128)S(1)} %get-tuple-element.124.layer, s32[16]{0:T(128)S(1)} %get-tuple-element.125.kind, f32[4,4]{1,0:T(4,128)S(1)} %get-tuple-element.126.table, f32[48,128]{1,0:T(8,128)S(1)} %get-tuple-element.127.rest_0_, f32[48,128]{1,0:T(8,128)S(1)} %get-tuple-element.128.rest_1_), custom_call_target="tpu_custom_call" | custom-call | flops 1000 | bytes 1000 | tf_op jit(solution)/shard_map/cond/branch_0_fun/observe/pallas_call | solution.py:633
  15.5 1.1 %cut_patches.5 = (f32[240,128]{1,0:T(8,128)S(1)}, f32[248,128]{1,0:T(8,128)S(1)}, f32[24,128]{1,0:T(8,128)S(1)}) custom-call(s32[16]{0:T(128)S(1)} %get-tuple-element.98.lat, s32[16]{0:T(128)S(1)} %get-tuple-element.120.lon, f32[20,8,32,128]{3,2,1,0:T(8,128)S(1)} %get-tuple-element.122.padded.field, f32[8,128]{1,0:T(8,128)S(1)} %observe.5.obs), custom_call_target="tpu_custom_call" | custom-call | flops 1000 | bytes 1000 | tf_op jit(solution)/shard_map/cond/branch_0_fun/cut_patches/pallas_call | solution.py:639
  16.7 1.9 %collective-permute-start = (f32[248,128]{1,0:T(8,128)S(1)}, f32[248,128]{1,0:T(8,128)S(1)}, u32[]{:S(2)}, u32[]{:S(2)}) collective-permute-start(f32[248,128]{1,0:T(8,128)S(1)} %get-tuple-element.131), channel_id=1, source_target_pairs={{0,4},{4,0},{8,12},{12,8},{16,20},{20,16},{24,28},{28,24},{1,5},{5... | collective-permute-start | bytes 380936 | tf_op jit(solution)/shard_map/cond/branch_0_fun/ppermute | solution.py:646
  18.6 1.0 %collective-permute-done.got = f32[248,128]{1,0:T(8,128)S(1)} collective-permute-done((f32[248,128]{1,0:T(8,128)S(1)}, f32[248,128]{1,0:T(8,128)S(1)}, u32[]{:S(2)}, u32[]{:S(2)}) %collective-permute-start) | collective-permute-done | bytes 127008 | tf_op jit(solution)/shard_map/cond/branch_0_fun/ppermute | solution.py:646
  19.5 0.1 pair_moments.5.rest_0_
  19.7 2.2 %collective-permute-start.3 = (f32[248,128]{1,0:T(8,128)S(1)}, f32[248,128]{1,0:T(8,128)S(1)}, u32[]{:S(2)}, u32[]{:S(2)}) collective-permute-start(f32[248,128]{1,0:T(8,128)S(1)} %pair_moments.5.rest_0_), channel_id=1, source_target_pairs={{0,24},{4,28},{8,16},{12,20},{16,8},{20,12},{24,0},{28,4},{1,25},{... | collective-permute-start | bytes 380936 | tf_op jit(solution)/shard_map/cond/branch_0_fun/ppermute | solution.py:653
  21.9 0.2 collective-permute-start.2
  22.1 0.3 collective-permute-start.1
  22.4 2.9 %collective-permute-done.3.rest_3_ = f32[248,128]{1,0:T(8,128)S(1)} collective-permute-done((f32[248,128]{1,0:T(8,128)S(1)}, f32[248,128]{1,0:T(8,128)S(1)}, u32[]{:S(2)}, u32[]{:S(2)}) %collective-permute-start.3) | collective-permute-done | bytes 127008 | tf_op jit(solution)/shard_map/cond/branch_0_fun/ppermute | solution.py:653
  25.3 3.4 %collective-permute-done.2.rest_2_ = f32[248,128]{1,0:T(8,128)S(1)} collective-permute-done((f32[248,128]{1,0:T(8,128)S(1)}, f32[248,128]{1,0:T(8,128)S(1)}, u32[]{:S(2)}, u32[]{:S(2)}) %collective-permute-start.2) | collective-permute-done | bytes 127008 | tf_op jit(solution)/shard_map/cond/branch_0_fun/ppermute | solution.py:653
  28.7 0.0 collective-permute-done.1.rest_1_
  28.7 0.1 merge_moments.5
  28.8 0.6 %collective-permute-start.4 = (f32[128,128]{1,0:T(8,128)S(1)}, f32[128,128]{1,0:T(8,128)S(1)}, u32[]{:S(2)}, u32[]{:S(2)}) collective-permute-start(f32[128,128]{1,0:T(8,128)S(1)} %get-tuple-element.132.mine), channel_id=1, source_target_pairs={{0,4},{4,0},{8,12},{12,8},{16,20},{20,16},{24,28},{28,24},{1,5},{5... | collective-permute-start | bytes 196616 | tf_op jit(solution)/shard_map/cond/branch_0_fun/ppermute | solution.py:660
  29.4 2.1 %solve_weights.5.weights = f32[2,16,128]{2,1,0:T(8,128)S(1)} custom-call(f32[16]{0:T(128)S(1)} %get-tuple-element.133.value, f32[16]{0:T(128)S(1)} %get-tuple-element.134.error, f32[2,16]{1,0:T(2,128)S(1)} %get-tuple-element.135.perturb, f32[16,128]{1,0:T(8,128)S(1)} %get-tuple-element.136.everyone_ref), custom_call_target="tpu_custom_call" | custom-call | flops 1000 | bytes 1000 | tf_op jit(solution)/shard_map/cond/branch_0_fun/solve_weights/pallas_call | solution.py:661
  31.6 0.0 collective-permute-done.4.theirs
  31.6 2.6 %apply_increments.5 = (f32[2,10,16,1024]{3,2,1,0:T(8,128)}, f32[20,8,32,128]{3,2,1,0:T(8,128)S(1)}) custom-call(s32[16]{0:T(128)S(1)} %get-tuple-element.98.lat, s32[16]{0:T(128)S(1)} %get-tuple-element.120.lon, f32[20,8,32,128]{3,2,1,0:T(8,128)S(1)} %get-tuple-element.122.padded.field, ...), custom_call_target="tpu_custom_call", output_to_operand_aliasing={{1}: (2, {})} | custom-call | flops 1000 | bytes 1000 | tf_op jit(solution)/shard_map/cond/branch_0_fun/apply_increments/pallas_call | solution.py:667
  (1 shorter events, 0.0 us)
Async XLA Ops:
  2.7 10.2 %copy-start = (f32[4,4]{1,0:T(4,128)S(1)}, f32[4,4]{1,0:T(4,128)}, u32[]{:S(2)}) copy-start(f32[4,4]{1,0:T(4,128)} %table.1) | copy-start | bytes 196
  2.7 7.3 %collective-permute-start.25 = (f32[432,128]{1,0:T(8,128)S(1)}, f32[432,128]{1,0:T(8,128)S(1)}, u32[]{:S(2)}, u32[]{:S(2)}) collective-permute-start(f32[432,128]{1,0:T(8,128)S(1)} %get-tuple-element.223), channel_id=1, source_target_pairs={{0,1},{1,0},{2,3},{3,2},{4,5},{5,4},{6,7},{7,6},{8,9},{9,8},{10,11... | collective-permute-start | bytes 663560 | tf_op jit(solution)/shard_map/ppermute | solution.py:707
  4.9 8.0 %collective-permute-start.27 = (f32[384,128]{1,0:T(8,128)S(1)}, f32[384,128]{1,0:T(8,128)S(1)}, u32[]{:S(2)}, u32[]{:S(2)}) collective-permute-start(f32[384,128]{1,0:T(8,128)S(1)} %get-tuple-element.228), channel_id=1, source_target_pairs={{0,4},{1,2},{2,1},{3,7},{4,0},{5,6},{6,5},{7,3},{8,12},{9,10},{10,... | collective-permute-start | bytes 589832 | tf_op jit(solution)/shard_map/ppermute | solution.py:708
  10.1 4.5 %collective-permute-start.26 = (f32[48,128]{1,0:T(8,128)S(1)}, f32[48,128]{1,0:T(8,128)S(1)}, u32[]{:S(2)}, u32[]{:S(2)}) collective-permute-start(f32[48,128]{1,0:T(8,128)S(1)} %combine_near.1.near), channel_id=1, source_target_pairs={{0,2},{1,3},{2,0},{3,1},{4,6},{5,7},{6,4},{7,5},{8,10},{9,11},{10,... | collective-permute-start | bytes 73736 | tf_op jit(solution)/shard_map/ppermute | solution.py:737
  12.9 1.7 %copy-start.1 = (s32[16]{0:T(128)S(1)}, s32[16]{0:T(128)}, u32[]{:S(2)}) copy-start(s32[16]{0:T(128)} %lat_hbm.3) | copy-start | bytes 196
  12.9 1.7 %copy-start.2 = (s32[16]{0:T(128)S(1)}, s32[16]{0:T(128)}, u32[]{:S(2)}) copy-start(s32[16]{0:T(128)} %lon_hbm.1) | copy-start | bytes 196
  12.9 1.7 %copy-start.3 = (f32[2,16]{1,0:T(2,128)S(1)}, f32[2,16]{1,0:T(2,128)}, u32[]{:S(2)}) copy-start(f32[2,16]{1,0:T(2,128)} %param.26) | copy-start | bytes 388
  13.0 1.7 %copy-start.4 = (s32[16]{0:T(128)S(1)}, s32[16]{0:T(128)}, u32[]{:S(2)}) copy-start(s32[16]{0:T(128)} %kind_hbm.1) | copy-start | bytes 196
  13.0 1.7 %copy-start.5 = (s32[16]{0:T(128)S(1)}, s32[16]{0:T(128)}, u32[]{:S(2)}) copy-start(s32[16]{0:T(128)} %param.22) | copy-start | bytes 196
  13.0 1.7 %copy-start.6 = (f32[16]{0:T(128)S(1)}, f32[16]{0:T(128)}, u32[]{:S(2)}) copy-start(f32[16]{0:T(128)} %param.24) | copy-start | bytes 196
  13.0 1.7 %copy-start.7 = (f32[16]{0:T(128)S(1)}, f32[16]{0:T(128)}, u32[]{:S(2)}) copy-start(f32[16]{0:T(128)} %param.25) | copy-start | bytes 196
  16.7 2.9 %collective-permute-start = (f32[248,128]{1,0:T(8,128)S(1)}, f32[248,128]{1,0:T(8,128)S(1)}, u32[]{:S(2)}, u32[]{:S(2)}) collective-permute-start(f32[248,128]{1,0:T(8,128)S(1)} %get-tuple-element.131), channel_id=1, source_target_pairs={{0,4},{4,0},{8,12},{12,8},{16,20},{20,16},{24,28},{28,24},{1,5},{5... | collective-permute-start | bytes 380936 | tf_op jit(solution)/shard_map/cond/branch_0_fun/ppermute | solution.py:646
  19.7 5.6 %collective-permute-start.3 = (f32[248,128]{1,0:T(8,128)S(1)}, f32[248,128]{1,0:T(8,128)S(1)}, u32[]{:S(2)}, u32[]{:S(2)}) collective-permute-start(f32[248,128]{1,0:T(8,128)S(1)} %pair_moments.5.rest_0_), channel_id=1, source_target_pairs={{0,24},{4,28},{8,16},{12,20},{16,8},{20,12},{24,0},{28,4},{1,25},{... | collective-permute-start | bytes 380936 | tf_op jit(solution)/shard_map/cond/branch_0_fun/ppermute | solution.py:653
  21.9 6.8 %collective-permute-start.2 = (f32[248,128]{1,0:T(8,128)S(1)}, f32[248,128]{1,0:T(8,128)S(1)}, u32[]{:S(2)}, u32[]{:S(2)}) collective-permute-start(f32[248,128]{1,0:T(8,128)S(1)} %pair_moments.5.rest_0_), channel_id=1, source_target_pairs={{0,16},{4,20},{8,24},{12,28},{16,0},{20,4},{24,8},{28,12},{1,17},{... | collective-permute-start | bytes 380936 | tf_op jit(solution)/shard_map/cond/branch_0_fun/ppermute | solution.py:653
  22.1 6.6 %collective-permute-start.1 = (f32[248,128]{1,0:T(8,128)S(1)}, f32[248,128]{1,0:T(8,128)S(1)}, u32[]{:S(2)}, u32[]{:S(2)}) collective-permute-start(f32[248,128]{1,0:T(8,128)S(1)} %pair_moments.5.rest_0_), channel_id=1, source_target_pairs={{0,8},{4,12},{8,0},{12,4},{16,24},{20,28},{24,16},{28,20},{1,9},{5... | collective-permute-start | bytes 380936 | tf_op jit(solution)/shard_map/cond/branch_0_fun/ppermute | solution.py:653
  28.8 2.8 %collective-permute-start.4 = (f32[128,128]{1,0:T(8,128)S(1)}, f32[128,128]{1,0:T(8,128)S(1)}, u32[]{:S(2)}, u32[]{:S(2)}) collective-permute-start(f32[128,128]{1,0:T(8,128)S(1)} %get-tuple-element.132.mine), channel_id=1, source_target_pairs={{0,4},{4,0},{8,12},{12,8},{16,20},{20,16},{24,28},{28,24},{1,5},{5... | collective-permute-start | bytes 196616 | tf_op jit(solution)/shard_map/cond/branch_0_fun/ppermute | solution.py:660

commit v4 on v3

--- a/solution.py
+++ b/solution.py
@@ -489,7 +489,7 @@
         pl.when(core == c)(functools.partial(cut, c))
 
 
-def pair_kernel(cap, members, own, got, obs, sel, msg):
+def pair_kernel(cap, members, halves, own, got, obs, sel, *msgs):
     size = cap * WINDOW_HEIGHT
     part = KINDS * size
     seen, theirs = obs[:members, :], got[members * part : members * part + members, :]
@@ -497,18 +497,41 @@
     sources = [(own, m, seen[m : m + 1]) for m in range(members)]
     sources += [(got, m, theirs[m : m + 1]) for m in range(members)]
     weight = [jnp.sum(sel[...] * (o - mean), axis=1, keepdims=True) for _, _, o in sources]
-    for k in range(KINDS):
-        cross = jnp.zeros((size, LANES), jnp.float32)
-        total = jnp.zeros((size, LANES), jnp.float32)
-        for (ref, m, _), o in zip(sources, weight):
-            patch = ref[m * part + k * size : m * part + (k + 1) * size, :]
-            cross = cross + patch * o
-            total = total + patch
-        msg[k * size : (k + 1) * size, :] = cross
-        msg[part + k * size : part + (k + 1) * size, :] = total
-    msg[2 * part :, :] = jnp.zeros((8, LANES), jnp.float32)
-    msg[2 * part : 2 * part + members, :] = seen
-    msg[2 * part + members : 2 * part + 2 * members, :] = theirs
+    for kinds, msg in zip(halves, msgs):
+        sums = len(kinds) * size
+        for n, k in enumerate(kinds):
+            cross = jnp.zeros((size, LANES), jnp.float32)
+            total = jnp.zeros((size, LANES), jnp.float32)
+            for (ref, m, _), o in zip(sources, weight):
+                patch = ref[m * part + k * size : m * part + (k + 1) * size, :]
+                cross = cross + patch * o
+                total = total + patch
+            msg[n * size : (n + 1) * size, :] = cross
+            msg[sums + n * size : sums + (n + 1) * size, :] = total
+        msg[2 * sums :, :] = jnp.zeros((msg.shape[0] - 2 * sums, LANES), jnp.float32)
+        msg[2 * sums : 2 * sums + members, :] = seen
+        msg[2 * sums + members : 2 * sums + 2 * members, :] = theirs
+
+
+def joined(size, count, seen, sel, mine, theirs, n, sums):
+    def mean(ref):
+        return jnp.sum(ref[2 * sums : 2 * sums + seen, :], axis=0, keepdims=True) / seen
+
+    shift = jnp.sum(sel[...] * (0.5 * (mean(mine) - mean(theirs))), axis=1, keepdims=True)
+    at, low = slice(n * size, (n + 1) * size), slice(sums + n * size, sums + (n + 1) * size)
+    return mine[at, :] + theirs[at, :] + shift * (mine[low, :] - theirs[low, :])
+
+
+def join_kernel(size, count, seen, sel, mine, theirs, out):
+    sums = count * size
+    for n in range(count):
+        low = slice(sums + n * size, sums + (n + 1) * size)
+        out[n * size : (n + 1) * size, :] = joined(size, count, seen, sel, mine, theirs, n, sums)
+        out[low, :] = mine[low, :] + theirs[low, :]
+    base = 2 * sums
+    out[base:, :] = jnp.zeros((out.shape[0] - base, LANES), jnp.float32)
+    out[base : base + seen, :] = mine[base : base + seen, :]
+    out[base + seen : base + 2 * seen, :] = theirs[base : base + seen, :]
 
 
 def weight_kernel(value, error, perturb, everyone_ref, weights):
@@ -539,31 +562,25 @@
         )
 
 
-def merge_kernel(cap, members, chips, sel, *rest):
-    msgs, (gain, everyone) = rest[:chips], rest[chips:]
+def merge_kernel(cap, halves, seen, sel, *rest):
+    pairs, (gain, everyone) = rest[:-2], rest[-2:]
     size = cap * WINDOW_HEIGHT
-    part = KINDS * size
-    both = 2 * members
-    number = chips * both
-    means = []
-    for c, msg in enumerate(msgs):
-        seen = msg[2 * part : 2 * part + both, :]
-        everyone[c * both : (c + 1) * both, :] = seen
-        means.append(jnp.sum(seen, axis=0, keepdims=True) / both)
-    mean = functools.reduce(jnp.add, means) / chips
-    shifts = [jnp.sum(sel[...] * (own - mean), axis=1, keepdims=True) for own in means]
+    number = 2 * seen
     row = (row_index(size) % WINDOW_HEIGHT).astype(jnp.float32)
     column = lane_index(size).astype(jnp.float32)
     row = (row + 0.5 - WINDOW_HEIGHT / 2) / (WINDOW_HEIGHT / 2)
     column = (column + 0.5 - WINDOW_WIDTH / 2) / (WINDOW_WIDTH / 2)
     taper = (1.0 - row * row) * (1.0 - column * column) / (number - 1)
-    for k in range(KINDS):
-        cross = jnp.zeros((size, LANES), jnp.float32)
-        for msg, shift in zip(msgs, shifts):
-            cross = cross + msg[k * size : (k + 1) * size, :]
-            cross = cross + shift * msg[part + k * size : part + (k + 1) * size, :]
-        gain[k * size : (k + 1) * size, :] = taper * cross
-    gain[part:, :] = jnp.zeros((8, LANES), jnp.float32)
+    for h, kinds in enumerate(halves):
+        mine, theirs = pairs[2 * h : 2 * h + 2]
+        sums = len(kinds) * size
+        if h == 0:
+            everyone[:seen, :] = mine[2 * sums : 2 * sums + seen, :]
+            everyone[seen:, :] = theirs[2 * sums : 2 * sums + seen, :]
+        for n, k in enumerate(kinds):
+            cross = joined(size, len(kinds), seen, sel, mine, theirs, n, sums)
+            gain[k * size : (k + 1) * size, :] = taper * cross
+    gain[KINDS * size :, :] = jnp.zeros((8, LANES), jnp.float32)
 
 
 def apply_kernel(cap, lat, lon, field, mine, theirs, weights, out, work, slots):
@@ -579,19 +596,22 @@
     def add(layer_of_own):
         def one(s, carry):
             j = slots[s]
-            row, block, after, shift = window(lat, lon, j, first, rows, tiles)
+            row, block, _, shift = window(lat, lon, j, first, rows, tiles)
+            after = (block + 1) % tiles
             here = patch_row & (lane >= shift)
             there = patch_row & (lane < shift)
             w = [weights[m, pl.ds(j, 1), :] for m in range(members)]
             for l, source in ((layer_of_own, mine), (1 - layer_of_own, theirs)):
-                for k in range(KINDS):
-                    gain = pltpu.roll(source[pl.ds(k * size + s * 4, 8), :], shift, 1)
-                    near = jnp.where(here, gain, 0.0)
-                    far = jnp.where(there, gain, 0.0)
-                    for m in range(members):
+                gains = [pltpu.roll(source[pl.ds(k * size + s * 4, 8), :], shift, 1) for k in range(KINDS)]
+                new = []
+                for m in range(members):
+                    for k in range(KINDS):
                         f = m * FIELDS + l * KINDS + k
-                        work[f, block, pl.ds(row, 8), :] += near * w[m]
-                        work[f, after, pl.ds(row, 8), :] += far * w[m]
+                        change = gains[k] * w[m]
+                        for at, part in ((block, here), (after, there)):
+                            new.append((f, at, work[f, at, pl.ds(row, 8), :] + jnp.where(part, change, 0.0)))
+                for f, at, value in new:
+                    work[f, at, pl.ds(row, 8), :] = value
             return carry
 
         lax.fori_loop(0, count, one, 0)
@@ -644,19 +664,39 @@
         [slots],
     )(lat, lon, field, obs)
     got = lax.ppermute(send, "member", other_core)
-    (msg,) = call(
-        functools.partial(pair_kernel, cap, members),
+    halves = (tuple(range((KINDS + 1) // 2)), tuple(range((KINDS + 1) // 2, KINDS)))
+    seen_rows = -(-chips * both // 8) * 8
+    msgs = call(
+        functools.partial(pair_kernel, cap, members, halves),
         "pair_moments",
         [VMEM] * 4,
-        [(2 * part + 8, LANES)],
+        [(2 * len(kinds) * size + seen_rows, LANES) for kinds in halves],
     )(own, got, obs, sel)
-    msgs = [msg] + [lax.ppermute(msg, "member", partner(devices, 2 * k)) for k in range(1, chips)]
+    steps = [1 << n for n in range(1, devices.bit_length() - 1)]
+    seen = both
+    for n in range(len(steps)):
+        others = [
+            lax.ppermute(msg, "member", partner(devices, steps[(n + h) % len(steps)]))
+            for h, msg in enumerate(msgs)
+        ]
+        if n == len(steps) - 1:
+            break
+        msgs = [
+            call(
+                functools.partial(join_kernel, size, len(kinds), seen),
+                "join_moments",
+                [VMEM] * 3,
+                [msg.shape],
+            )(sel, msg, other)[0]
+            for kinds, msg, other in zip(halves, msgs, others)
+        ]
+        seen *= 2
     mine, everyone = call(
-        functools.partial(merge_kernel, cap, members, chips),
+        functools.partial(merge_kernel, cap, halves, seen),
         "merge_moments",
-        [VMEM] * (1 + chips),
+        [VMEM] * 5,
         [(part + 8, LANES), (chips * both, LANES)],
-    )(sel, *msgs)
+    )(sel, msgs[0], others[0], msgs[1], others[1])
     theirs = lax.ppermute(mine, "member", other_core)
     (weights,) = call(
         weight_kernel,

time: 34.7 us -> 35.7 us (1.029)
  starting transfers between devices: 10.5 us -> 14.6 us
  waiting for transfers between devices: 9.09 us -> 6.12 us
    ppermute x3 -> x4, waiting for transfers between devices: 6.3 us -> 3.33 us  [analyse(): lax.ppermute(msg, 'member', partner(devices, steps[(n + h) % len(steps)]))]
    ppermute x3 -> x4, starting transfers between devices: 2.71 us -> 5 us  [analyse(): lax.ppermute(msg, 'member', partner(devices, steps[(n + h) % len(steps)]))]
    ppermute x1, starting transfers between devices: 0.63 us -> 2.39 us  [analyse(): theirs = lax.ppermute(mine, 'member', other_core)]
    pallas_call x1, Pallas kernels: 2.64 us -> 2.28 us  [analyse(): call(functools.partial(apply_kernel, cap), 'apply_increments', [SMEM] * 2...]
  transfers between devices with their start and end apart: 8 -> 9, of which waited for: 4 -> 4; matrix products, arithmetic and copies ran while one was open for 0% -> 0% of each run, Pallas kernels for 18% -> 18%
where the time goes in v4:
time: 35.7 us; the launch traced here: 35 us
  starting transfers between devices  14.6 us (41%)
  Pallas kernels  13.4 us (38%)
  waiting for transfers between devices  6.12 us (17%)
  between operations  0.82 us (2%)
    ppermute x4, starting transfers between devices, analyse(): lax.ppermute(msg, 'member', partner(devices, steps[(n + h) % len(steps)]))  5 us
    ppermute x4, waiting for transfers between devices, analyse(): lax.ppermute(msg, 'member', partner(devices, steps[(n + h) % len(steps)]))  3.33 us
    pallas_call x1, Pallas kernels, body(): call(load_kernel, 'load_arguments', [HBM] * 6, [(message[0] + NEAR_ROWS,...  2.71 us
    pallas_call x1, Pallas kernels, body(): call(functools.partial(interior_kernel, row_tiles, rows, caps[:-1]), 'int...  2.39 us
    ppermute x1, starting transfers between devices, analyse(): theirs = lax.ppermute(mine, 'member', other_core)  2.39 us
    pallas_call x1, Pallas kernels, analyse(): call(functools.partial(apply_kernel, cap), 'apply_increments', [SMEM] * 2...  2.28 us
    ppermute x1, starting transfers between devices, body(): lax.ppermute(out_a, ('member', 'tile'), swaps(devices, row_tiles, 0))  2.19 us
    ppermute x1, starting transfers between devices, body(): lax.ppermute(near, 'tile', partner(row_tiles, step))  2.15 us
  transfers between devices with their start and end apart: 9, of which 4 were waited for; matrix products, arithmetic and copies ran while one was open for 0% of the time, Pallas kernels for 18%

profile of v4, /device:TPU:1, one launch (start us, length us, event | category | flops | bytes accessed | tf_op | source)
XLA Modules:
  0.0 35.0 jit_solution(14041039672359091052)
XLA Ops:
  0.0 2.7 %load_arguments.1 = (f32[432,128]{1,0:T(8,128)S(1)}, f32[384,128]{1,0:T(8,128)S(1)}, f32[48,128]{1,0:T(8,128)S(1)}, f32[20,10,32,128]{3,2,1,0:T(8,128)S(1)}, f32...) custom-call(s32[16]{0:T(128)} %lat_hbm.3, s32[16]{0:T(128)} %lon_hbm.1, s32[16]{0:T(128)} %kind_hbm.1, ...), custom_call_target="tpu_custom_call" | custom-call | flops 1000 | bytes 1000 | tf_op jit(solution)/shard_map/load_arguments/pallas_call | solution.py:726
  2.7 0.0 copy-start
  2.7 2.2 %collective-permute-start.30 = (f32[432,128]{1,0:T(8,128)S(1)}, f32[432,128]{1,0:T(8,128)S(1)}, u32[]{:S(2)}, u32[]{:S(2)}) collective-permute-start(f32[432,128]{1,0:T(8,128)S(1)} %get-tuple-element.233), channel_id=1, source_target_pairs={{0,1},{1,0},{2,3},{3,2},{4,5},{5,4},{6,7},{7,6},{8,9},{9,8},{10,11... | collective-permute-start | bytes 663560 | tf_op jit(solution)/shard_map/ppermute | solution.py:747
  4.9 1.0 %collective-permute-start.32 = (f32[384,128]{1,0:T(8,128)S(1)}, f32[384,128]{1,0:T(8,128)S(1)}, u32[]{:S(2)}, u32[]{:S(2)}) collective-permute-start(f32[384,128]{1,0:T(8,128)S(1)} %get-tuple-element.238), channel_id=1, source_target_pairs={{0,4},{1,2},{2,1},{3,7},{4,0},{5,6},{6,5},{7,3},{8,12},{9,10},{10,... | collective-permute-start | bytes 589832 | tf_op jit(solution)/shard_map/ppermute | solution.py:748
  5.9 2.4 %interior_rows.1 = (f32[20,8,32,128]{3,2,1,0:T(8,128)S(1)}, f32[20,8,8,128]{3,2,1,0:T(8,128)S(1)}, f32[20,8,8,128]{3,2,1,0:T(8,128)S(1)}, f32[2,8,8,8,128]{4,3,2...) custom-call(s32[16]{0:T(128)} %lat_hbm.3, f32[4,4]{1,0:T(4,128)} %table.1, ...), custom_call_target="tpu_custom_call" | custom-call | flops 20000000 | bytes 1000 | tf_op jit(solution)/shard_map/interior_rows/pallas_call | solution.py:750
  8.3 1.8 %collective-permute-done.30.from_a = f32[432,128]{1,0:T(8,128)S(1)} collective-permute-done((f32[432,128]{1,0:T(8,128)S(1)}, f32[432,128]{1,0:T(8,128)S(1)}, u32[]{:S(2)}, u32[]{:S(2)}) %collective-permute-start.30) | collective-permute-done | bytes 221216 | tf_op jit(solution)/shard_map/ppermute | solution.py:747
  10.1 2.2 %collective-permute-start.31 = (f32[48,128]{1,0:T(8,128)S(1)}, f32[48,128]{1,0:T(8,128)S(1)}, u32[]{:S(2)}, u32[]{:S(2)}) collective-permute-start(f32[48,128]{1,0:T(8,128)S(1)} %combine_near.1.near), channel_id=1, source_target_pairs={{0,2},{1,3},{2,0},{3,1},{4,6},{5,7},{6,4},{7,5},{8,10},{9,11},{10,... | collective-permute-start | bytes 73736 | tf_op jit(solution)/shard_map/ppermute | solution.py:777
  12.9 0.0 collective-permute-done.32.from_b
  12.9 0.0 copy-done
  12.9 0.0 copy-start.1
  12.9 0.0 copy-start.2
  12.9 0.0 copy-start.3
  13.0 0.0 copy-start.4
  13.0 0.0 copy-start.5
  13.0 0.0 copy-start.6
  13.0 0.0 copy-start.7
  13.0 1.6 %edge_rows.1 = f32[20,8,32,128]{3,2,1,0:T(8,128)S(1)} custom-call(f32[4,4]{1,0:T(4,128)S(1)} %copy-done, f32[20,8,8,128]{3,2,1,0:T(8,128)S(1)} %get-tuple-element.235.own_edge, f32[20,8,8,128]{3,2,1,0:T(8,128)S(1)} %get-tuple-element.236.once_edge, f32[2,8,8,8,128]{4,3,2,1,0:T(8,128)S(1)} %get-tuple-element.237.vel_edge, ...), custom_call_target="tpu_custom_call", output_to_operand_aliasing={{}: (7, {})} | custom-call | flops 1000 | bytes 1000 | tf_op jit(solution)/shard_map/edge_rows/pallas_call | solution.py:783
  14.6 0.0 collective-permute-done.31
  14.6 0.0 copy-done.1
  14.6 0.0 copy-done.2
  14.6 0.0 copy-done.3
  14.6 0.0 copy-done.4
  14.6 0.0 copy-done.5
  14.7 0.0 copy-done.6
  14.7 0.0 copy-done.7
  14.7 20.3 %conditional.1 = (f32[2,10,16,1024]{3,2,1,0:T(8,128)}) conditional(s32[]{:T(128)} %bitcast, (s32[16]{0:T(128)S(1)}, s32[16]{0:T(128)S(1)}, f32[4,4]{1,0:T(4,128)S(1)}, f32[48,128]{1,0:T(8,128)S(1)}, f32[48,128]{1,0:T(8,128)S(1)}, /*index=5*/s32[16]{0:T(128)S(1)}, s32[16]{0:T(128)S(1)}, ...), branch_computations={%region_0.0_spmd, %region_1.0_spmd, %region_2.0_spmd, %region_3.0_... | conditional | flops 8000 | bytes 4759608 | solution.py:792
  14.7 0.8 %observe.5.obs = f32[8,128]{1,0:T(8,128)S(1)} custom-call(s32[16]{0:T(128)S(1)} %get-tuple-element.124.layer, s32[16]{0:T(128)S(1)} %get-tuple-element.125.kind, f32[4,4]{1,0:T(4,128)S(1)} %get-tuple-element.126.table, f32[48,128]{1,0:T(8,128)S(1)} %get-tuple-element.127.rest_0_, f32[48,128]{1,0:T(8,128)S(1)} %get-tuple-element.128.rest_1_), custom_call_target="tpu_custom_call" | custom-call | flops 1000 | bytes 1000 | tf_op jit(solution)/shard_map/cond/branch_0_fun/observe/pallas_call | solution.py:653
  15.5 1.0 %cut_patches.5 = (f32[240,128]{1,0:T(8,128)S(1)}, f32[248,128]{1,0:T(8,128)S(1)}, f32[24,128]{1,0:T(8,128)S(1)}) custom-call(s32[16]{0:T(128)S(1)} %get-tuple-element.98.lat, s32[16]{0:T(128)S(1)} %get-tuple-element.120.lon, f32[20,8,32,128]{3,2,1,0:T(8,128)S(1)} %get-tuple-element.122.padded.field, f32[8,128]{1,0:T(8,128)S(1)} %observe.5.obs), custom_call_target="tpu_custom_call" | custom-call | flops 1000 | bytes 1000 | tf_op jit(solution)/shard_map/cond/branch_0_fun/cut_patches/pallas_call | solution.py:659
  16.6 1.9 %collective-permute-start = (f32[248,128]{1,0:T(8,128)S(1)}, f32[248,128]{1,0:T(8,128)S(1)}, u32[]{:S(2)}, u32[]{:S(2)}) collective-permute-start(f32[248,128]{1,0:T(8,128)S(1)} %get-tuple-element.131), channel_id=1, source_target_pairs={{0,4},{4,0},{8,12},{12,8},{16,20},{20,16},{24,28},{28,24},{1,5},{5... | collective-permute-start | bytes 380936 | tf_op jit(solution)/shard_map/cond/branch_0_fun/ppermute | solution.py:666
  18.5 1.0 %collective-permute-done.got = f32[248,128]{1,0:T(8,128)S(1)} collective-permute-done((f32[248,128]{1,0:T(8,128)S(1)}, f32[248,128]{1,0:T(8,128)S(1)}, u32[]{:S(2)}, u32[]{:S(2)}) %collective-permute-start) | collective-permute-done | bytes 127008 | tf_op jit(solution)/shard_map/cond/branch_0_fun/ppermute | solution.py:666
  19.4 0.1 pair_moments.5
  19.6 1.3 %collective-permute-start.1 = (f32[160,128]{1,0:T(8,128)S(1)}, f32[160,128]{1,0:T(8,128)S(1)}, u32[]{:S(2)}, u32[]{:S(2)}) collective-permute-start(f32[160,128]{1,0:T(8,128)S(1)} %get-tuple-element.132.mine), channel_id=1, source_target_pairs={{0,8},{4,12},{8,0},{12,4},{16,24},{20,28},{24,16},{28,20},{1,9},{5... | collective-permute-start | bytes 245768 | tf_op jit(solution)/shard_map/cond/branch_0_fun/ppermute | solution.py:679
  20.8 1.2 %collective-permute-start.3 = (f32[112,128]{1,0:T(8,128)S(1)}, f32[112,128]{1,0:T(8,128)S(1)}, u32[]{:S(2)}, u32[]{:S(2)}) collective-permute-start(f32[112,128]{1,0:T(8,128)S(1)} %get-tuple-element.133.mine), channel_id=1, source_target_pairs={{0,16},{4,20},{8,24},{12,28},{16,0},{20,4},{24,8},{28,12},{1,17},{... | collective-permute-start | bytes 172040 | tf_op jit(solution)/shard_map/cond/branch_0_fun/ppermute | solution.py:679
  22.1 1.2 %collective-permute-done.1.theirs = f32[160,128]{1,0:T(8,128)S(1)} collective-permute-done((f32[160,128]{1,0:T(8,128)S(1)}, f32[160,128]{1,0:T(8,128)S(1)}, u32[]{:S(2)}, u32[]{:S(2)}) %collective-permute-start.1) | collective-permute-done | bytes 81952 | tf_op jit(solution)/shard_map/cond/branch_0_fun/ppermute | solution.py:679
  23.3 0.1 join_moments.10.rest_0_
  23.4 1.3 %collective-permute-start.2 = (f32[160,128]{1,0:T(8,128)S(1)}, f32[160,128]{1,0:T(8,128)S(1)}, u32[]{:S(2)}, u32[]{:S(2)}) collective-permute-start(f32[160,128]{1,0:T(8,128)S(1)} %join_moments.10.rest_0_), channel_id=1, source_target_pairs={{0,16},{4,20},{8,24},{12,28},{16,0},{20,4},{24,8},{28,12},{1,17},{... | collective-permute-start | bytes 245768 | tf_op jit(solution)/shard_map/cond/branch_0_fun/ppermute | solution.py:679
  24.7 0.0 collective-permute-done.3.theirs
  24.7 0.1 join_moments.11.rest_2_
  24.8 1.2 %collective-permute-start.4 = (f32[112,128]{1,0:T(8,128)S(1)}, f32[112,128]{1,0:T(8,128)S(1)}, u32[]{:S(2)}, u32[]{:S(2)}) collective-permute-start(f32[112,128]{1,0:T(8,128)S(1)} %join_moments.11.rest_2_), channel_id=1, source_target_pairs={{0,8},{4,12},{8,0},{12,4},{16,24},{20,28},{24,16},{28,20},{1,9},{5... | collective-permute-start | bytes 172040 | tf_op jit(solution)/shard_map/cond/branch_0_fun/ppermute | solution.py:679
  26.0 2.1 %collective-permute-done.4.rest_3_ = f32[112,128]{1,0:T(8,128)S(1)} collective-permute-done((f32[112,128]{1,0:T(8,128)S(1)}, f32[112,128]{1,0:T(8,128)S(1)}, u32[]{:S(2)}, u32[]{:S(2)}) %collective-permute-start.4) | collective-permute-done | bytes 57376 | tf_op jit(solution)/shard_map/cond/branch_0_fun/ppermute | solution.py:679
  28.1 0.0 collective-permute-done.2.rest_1_
  28.1 0.1 merge_moments.5
  28.2 2.4 %collective-permute-start.5 = (f32[128,128]{1,0:T(8,128)S(1)}, f32[128,128]{1,0:T(8,128)S(1)}, u32[]{:S(2)}, u32[]{:S(2)}) collective-permute-start(f32[128,128]{1,0:T(8,128)S(1)} %get-tuple-element.134.mine), channel_id=1, source_target_pairs={{0,4},{4,0},{8,12},{12,8},{16,20},{20,16},{24,28},{28,24},{1,5},{5... | collective-permute-start | bytes 196616 | tf_op jit(solution)/shard_map/cond/branch_0_fun/ppermute | solution.py:700
  30.6 2.1 %solve_weights.5.weights = f32[2,16,128]{2,1,0:T(8,128)S(1)} custom-call(f32[16]{0:T(128)S(1)} %get-tuple-element.135.value, f32[16]{0:T(128)S(1)} %get-tuple-element.136.error, f32[2,16]{1,0:T(2,128)S(1)} %get-tuple-element.137.perturb, f32[16,128]{1,0:T(8,128)S(1)} %get-tuple-element.138.everyone_ref), custom_call_target="tpu_custom_call" | custom-call | flops 1000 | bytes 1000 | tf_op jit(solution)/shard_map/cond/branch_0_fun/solve_weights/pallas_call | solution.py:701
  32.7 0.0 collective-permute-done.5.theirs
  32.7 2.3 %apply_increments.5 = (f32[2,10,16,1024]{3,2,1,0:T(8,128)}, f32[20,8,32,128]{3,2,1,0:T(8,128)S(1)}) custom-call(s32[16]{0:T(128)S(1)} %get-tuple-element.98.lat, s32[16]{0:T(128)S(1)} %get-tuple-element.120.lon, f32[20,8,32,128]{3,2,1,0:T(8,128)S(1)} %get-tuple-element.122.padded.field, ...), custom_call_target="tpu_custom_call", output_to_operand_aliasing={{1}: (2, {})} | custom-call | flops 1000 | bytes 1000 | tf_op jit(solution)/shard_map/cond/branch_0_fun/apply_increments/pallas_call | solution.py:707
  (1 shorter events, 0.0 us)
Async XLA Ops:
  2.7 10.2 %copy-start = (f32[4,4]{1,0:T(4,128)S(1)}, f32[4,4]{1,0:T(4,128)}, u32[]{:S(2)}) copy-start(f32[4,4]{1,0:T(4,128)} %table.1) | copy-start | bytes 196
  2.7 7.3 %collective-permute-start.30 = (f32[432,128]{1,0:T(8,128)S(1)}, f32[432,128]{1,0:T(8,128)S(1)}, u32[]{:S(2)}, u32[]{:S(2)}) collective-permute-start(f32[432,128]{1,0:T(8,128)S(1)} %get-tuple-element.233), channel_id=1, source_target_pairs={{0,1},{1,0},{2,3},{3,2},{4,5},{5,4},{6,7},{7,6},{8,9},{9,8},{10,11... | collective-permute-start | bytes 663560 | tf_op jit(solution)/shard_map/ppermute | solution.py:747
  4.9 8.0 %collective-permute-start.32 = (f32[384,128]{1,0:T(8,128)S(1)}, f32[384,128]{1,0:T(8,128)S(1)}, u32[]{:S(2)}, u32[]{:S(2)}) collective-permute-start(f32[384,128]{1,0:T(8,128)S(1)} %get-tuple-element.238), channel_id=1, source_target_pairs={{0,4},{1,2},{2,1},{3,7},{4,0},{5,6},{6,5},{7,3},{8,12},{9,10},{10,... | collective-permute-start | bytes 589832 | tf_op jit(solution)/shard_map/ppermute | solution.py:748
  10.1 4.5 %collective-permute-start.31 = (f32[48,128]{1,0:T(8,128)S(1)}, f32[48,128]{1,0:T(8,128)S(1)}, u32[]{:S(2)}, u32[]{:S(2)}) collective-permute-start(f32[48,128]{1,0:T(8,128)S(1)} %combine_near.1.near), channel_id=1, source_target_pairs={{0,2},{1,3},{2,0},{3,1},{4,6},{5,7},{6,4},{7,5},{8,10},{9,11},{10,... | collective-permute-start | bytes 73736 | tf_op jit(solution)/shard_map/ppermute | solution.py:777
  12.9 1.7 %copy-start.1 = (s32[16]{0:T(128)S(1)}, s32[16]{0:T(128)}, u32[]{:S(2)}) copy-start(s32[16]{0:T(128)} %lat_hbm.3) | copy-start | bytes 196
  12.9 1.7 %copy-start.2 = (s32[16]{0:T(128)S(1)}, s32[16]{0:T(128)}, u32[]{:S(2)}) copy-start(s32[16]{0:T(128)} %lon_hbm.1) | copy-start | bytes 196
  12.9 1.7 %copy-start.3 = (f32[2,16]{1,0:T(2,128)S(1)}, f32[2,16]{1,0:T(2,128)}, u32[]{:S(2)}) copy-start(f32[2,16]{1,0:T(2,128)} %param.26) | copy-start | bytes 388
  13.0 1.7 %copy-start.4 = (s32[16]{0:T(128)S(1)}, s32[16]{0:T(128)}, u32[]{:S(2)}) copy-start(s32[16]{0:T(128)} %kind_hbm.1) | copy-start | bytes 196
  13.0 1.7 %copy-start.5 = (s32[16]{0:T(128)S(1)}, s32[16]{0:T(128)}, u32[]{:S(2)}) copy-start(s32[16]{0:T(128)} %param.22) | copy-start | bytes 196
  13.0 1.7 %copy-start.6 = (f32[16]{0:T(128)S(1)}, f32[16]{0:T(128)}, u32[]{:S(2)}) copy-start(f32[16]{0:T(128)} %param.24) | copy-start | bytes 196
  13.0 1.7 %copy-start.7 = (f32[16]{0:T(128)S(1)}, f32[16]{0:T(128)}, u32[]{:S(2)}) copy-start(f32[16]{0:T(128)} %param.25) | copy-start | bytes 196
  16.6 2.9 %collective-permute-start = (f32[248,128]{1,0:T(8,128)S(1)}, f32[248,128]{1,0:T(8,128)S(1)}, u32[]{:S(2)}, u32[]{:S(2)}) collective-permute-start(f32[248,128]{1,0:T(8,128)S(1)} %get-tuple-element.131), channel_id=1, source_target_pairs={{0,4},{4,0},{8,12},{12,8},{16,20},{20,16},{24,28},{28,24},{1,5},{5... | collective-permute-start | bytes 380936 | tf_op jit(solution)/shard_map/cond/branch_0_fun/ppermute | solution.py:666
  19.6 3.7 %collective-permute-start.1 = (f32[160,128]{1,0:T(8,128)S(1)}, f32[160,128]{1,0:T(8,128)S(1)}, u32[]{:S(2)}, u32[]{:S(2)}) collective-permute-start(f32[160,128]{1,0:T(8,128)S(1)} %get-tuple-element.132.mine), channel_id=1, source_target_pairs={{0,8},{4,12},{8,0},{12,4},{16,24},{20,28},{24,16},{28,20},{1,9},{5... | collective-permute-start | bytes 245768 | tf_op jit(solution)/shard_map/cond/branch_0_fun/ppermute | solution.py:679
  20.8 3.8 %collective-permute-start.3 = (f32[112,128]{1,0:T(8,128)S(1)}, f32[112,128]{1,0:T(8,128)S(1)}, u32[]{:S(2)}, u32[]{:S(2)}) collective-permute-start(f32[112,128]{1,0:T(8,128)S(1)} %get-tuple-element.133.mine), channel_id=1, source_target_pairs={{0,16},{4,20},{8,24},{12,28},{16,0},{20,4},{24,8},{28,12},{1,17},{... | collective-permute-start | bytes 172040 | tf_op jit(solution)/shard_map/cond/branch_0_fun/ppermute | solution.py:679
  23.4 4.7 %collective-permute-start.2 = (f32[160,128]{1,0:T(8,128)S(1)}, f32[160,128]{1,0:T(8,128)S(1)}, u32[]{:S(2)}, u32[]{:S(2)}) collective-permute-start(f32[160,128]{1,0:T(8,128)S(1)} %join_moments.10.rest_0_), channel_id=1, source_target_pairs={{0,16},{4,20},{8,24},{12,28},{16,0},{20,4},{24,8},{28,12},{1,17},{... | collective-permute-start | bytes 245768 | tf_op jit(solution)/shard_map/cond/branch_0_fun/ppermute | solution.py:679
  24.8 3.3 %collective-permute-start.4 = (f32[112,128]{1,0:T(8,128)S(1)}, f32[112,128]{1,0:T(8,128)S(1)}, u32[]{:S(2)}, u32[]{:S(2)}) collective-permute-start(f32[112,128]{1,0:T(8,128)S(1)} %join_moments.11.rest_2_), channel_id=1, source_target_pairs={{0,8},{4,12},{8,0},{12,4},{16,24},{20,28},{24,16},{28,20},{1,9},{5... | collective-permute-start | bytes 172040 | tf_op jit(solution)/shard_map/cond/branch_0_fun/ppermute | solution.py:679
  28.2 4.5 %collective-permute-start.5 = (f32[128,128]{1,0:T(8,128)S(1)}, f32[128,128]{1,0:T(8,128)S(1)}, u32[]{:S(2)}, u32[]{:S(2)}) collective-permute-start(f32[128,128]{1,0:T(8,128)S(1)} %get-tuple-element.134.mine), channel_id=1, source_target_pairs={{0,4},{4,0},{8,12},{12,8},{16,20},{20,16},{24,28},{28,24},{1,5},{5... | collective-permute-start | bytes 196616 | tf_op jit(solution)/shard_map/cond/branch_0_fun/ppermute | solution.py:700
